TPU v7x, 32 devices: a whole 2x2x4 slice. The times are simulated.
32 devices in a mesh: src: 8 (over z, core), tgt: 4 (over y, x).
Axes of the slice: x: 2, y: 2, z: 4, core: 2. Of those that a mesh axis runs over, the one named last changes fastest.
Arguments:
- src_pts: float32 [64, 8192], P('tgt', 'src'), may hold values from -30 to 30
- tgt_pts: float32 [64, 8192], P('src', 'tgt'), may hold values from -6 to 6
- src_mass: float32 [8192], P('src'), may hold values from 0.1 to 1
- tgt_mass: float32 [8192], P('tgt'), may hold values from 0.1 to 1
- init_pot: float32 [8192], P('tgt'), may hold values from -3 to 3
Outputs:
- src_pot: float32 [8192], P('src')
- tgt_pot: float32 [8192], P('tgt')
- mapped: float32 [64, 8192], P('tgt', 'src')
All inputs are finite; a program needn't handle non-finite values.
Results may differ from a plain program's by a relative error of at most 0.0003.
Values sent between devices are 32-bit elements; how exact they have to be, the bound alone decides.
No kernel may reach another device: no remote copies, remote signals or barrier semaphores. Data moves between devices by JAX's collectives and lax.ppermute only.
A program may use at most 64 MiB of HBM per device.

v0:
```python
import jax
import jax.numpy as jnp
from jax import lax
from jax.sharding import PartitionSpec as P

K = 64
ITERS = 3


EPS = 0.1


def shards(src_pts, tgt_pts, src_mass, tgt_mass, init_pot):
    xs = lax.all_gather(src_pts, "tgt", axis=0, tiled=True)
    ys = lax.all_gather(tgt_pts, "src", axis=0, tiled=True)
    xnorm = jnp.sum(xs * xs, axis=0)
    ynorm = jnp.sum(ys * ys, axis=0)

    def tile_cost():
        cross = lax.dot_general(
            xs,
            ys,
            (((0,), (0,)), ((), ())),
            precision=lax.Precision.HIGHEST,
            preferred_element_type=jnp.float32,
        )
        return (xnorm[:, None] + ynorm[None, :] - 2.0 * cross) / K

    tgt_pot = init_pot
    src_pot = jnp.zeros(src_mass.shape, jnp.float32)
    for step in range(ITERS):
        src_score = (tgt_pot[None, :] - tile_cost()) / EPS
        src_top = jnp.max(src_score, axis=1)
        src_total = jnp.sum(jnp.exp(src_score - src_top[:, None]), axis=1)
        src_whole_top = lax.pmax(src_top, "tgt")
        src_whole_sum = lax.psum(src_total * jnp.exp(src_top - src_whole_top), "tgt")
        src_pot = EPS * jnp.log(src_mass) - EPS * (src_whole_top + jnp.log(src_whole_sum))
        score = (src_pot[:, None] - tile_cost()) / EPS
        top = jnp.max(score, axis=0)
        total = jnp.sum(jnp.exp(score - top[None, :]), axis=0)
        whole_top = lax.pmax(top, "src")
        whole_sum = lax.psum(total * jnp.exp(top - whole_top), "src")
        tgt_pot = EPS * jnp.log(tgt_mass) - EPS * (whole_top + jnp.log(whole_sum))
    weight = jnp.exp((src_pot[:, None] + tgt_pot[None, :] - tile_cost()) / EPS)
    numer = lax.dot_general(
        ys,
        weight,
        (((1,), (1,)), ((), ())),
        precision=lax.Precision.HIGHEST,
        preferred_element_type=jnp.float32,
    )
    denom = jnp.sum(weight, axis=1)
    feat_rows = src_pts.shape[0]
    numer_all, denom_all = lax.psum((numer, denom), "tgt")
    start = lax.axis_index("tgt") * feat_rows
    own = lax.dynamic_slice_in_dim(numer_all, start, feat_rows, 0)
    mapped = own / denom_all[None, :]
    return (src_pot, tgt_pot, mapped)


def solution(mesh):
    return jax.shard_map(
        shards,
        mesh=mesh,
        in_specs=(P("tgt", "src"), P("src", "tgt"), P("src"), P("tgt"), P("tgt")),
        out_specs=(P("src"), P("tgt"), P("tgt", "src")),
        check_vma=False,
    )
```

profile of v0, /device:TPU:0, one launch (start us, length us, event | category | flops | bytes accessed | tf_op | source)
XLA Modules:
  0.0 292.1 jit_solution(5100036081648086333)
XLA Ops:
  7.2 16.8 %all_gather.7 = f32[64,2048]{1,0:T(8,128)S(1)} all-gather(f32[8,2048]{1,0:T(8,128)} %param.6), channel_id=1, replica_groups=mesh['src'=8,'tgt'=4] {'src'}, dimensions={0}, use_global_device_ids=true | all-gather | bytes 589824 | tf_op jit(solution)/shard_map/all_gather | solution.py:15
  24.1 9.3 %all_gather.6 = f32[64,1024]{1,0:T(8,128)S(1)} all-gather(f32[16,1024]{1,0:T(8,128)} %param.5), channel_id=1, replica_groups=mesh['src'=8,'tgt'=4] {'tgt'}, dimensions={0}, use_global_device_ids=true | all-gather | bytes 327680 | tf_op jit(solution)/shard_map/all_gather | solution.py:14
  33.4 11.4 %fusion = (f32[1024]{0:T(1024)S(1)}, f32[1024,2048]{1,0:T(8,128)}) fusion(f32[2048]{0:T(1024)} %param.9, f32[64,1024]{1,0:T(8,128)S(1)} %all_gather.6, f32[64,2048]{1,0:T(8,128)S(1)} %all_gather.7, f32[2048]{0:T(1024)S(1)} %multiply_reduce_fusion, f32[1024]{0:T(1024)S(1)} %multiply_reduce_fusion.1), kind=kOutput, calls=%fused_computation.14 | convolution fusion | flops 1625291776 | bytes 9199616 | tf_op jit(solution)/shard_map/dot_general | solution.py:20
  44.8 9.0 %pmax.42 = f32[1024]{0:T(1024)S(1)} all-reduce(f32[1024]{0:T(1024)S(1)} %get-tuple-element.3), channel_id=1, replica_groups=mesh['src'=8,'tgt'=4] {'tgt'}, use_global_device_ids=true, to_apply=%region_3.0 | all-reduce | flops 1024 | bytes 8192 | tf_op jit(solution)/shard_map/pmax | solution.py:35
  58.3 8.6 %psum.56 = f32[1024]{0:T(1024)S(1)} all-reduce(f32[1024]{0:T(1024)S(1)} %exponential_multiply_fusion.5), channel_id=1, replica_groups=mesh['src'=8,'tgt'=4] {'tgt'}, use_global_device_ids=true, to_apply=%region_5.0 | all-reduce | flops 1024 | bytes 8192 | tf_op jit(solution)/shard_map/psum | solution.py:36
  71.3 4.5 %exponential_reduce_fusion.4 = f32[2048]{0:T(1024)S(1)} fusion(f32[1024,2048]{1,0:T(8,128)} %get-tuple-element.4, f32[2048]{0:T(1024)S(1)} %fusion.1, f32[1024]{0:T(1024)S(1)} %multiply_subtract_fusion.5), kind=kLoop, calls=%fused_computation.9 | loop fusion | flops 8386560 | bytes 8409088 | tf_op jit(solution)/shard_map/reduce_sum | solution.py:40
  75.8 13.9 %pmax.43 = f32[2048]{0:T(1024)S(1)} all-reduce(f32[2048]{0:T(1024)S(1)} %fusion.1), channel_id=1, replica_groups=mesh['src'=8,'tgt'=4] {'src'}, use_global_device_ids=true, to_apply=%region_7.0 | all-reduce | flops 2048 | bytes 16384 | tf_op jit(solution)/shard_map/pmax | solution.py:41
  89.7 13.9 %psum.57 = f32[2048]{0:T(1024)S(1)} all-reduce(f32[2048]{0:T(1024)S(1)} %exponential_multiply_fusion.2), channel_id=1, replica_groups=mesh['src'=8,'tgt'=4] {'src'}, use_global_device_ids=true, to_apply=%region_9.0 | all-reduce | flops 2048 | bytes 16384 | tf_op jit(solution)/shard_map/psum | solution.py:42
  108.0 4.5 %exponential_reduce_fusion.3 = f32[1024]{0:T(1024)S(1)} fusion(f32[1024,2048]{1,0:T(8,128)} %get-tuple-element.4, f32[1024]{0:T(1024)S(1)} %fusion.2, f32[2048]{0:T(1024)S(1)} %multiply_subtract_fusion.2), kind=kLoop, calls=%fused_computation.7 | loop fusion | flops 8387584 | bytes 8404992 | tf_op jit(solution)/shard_map/reduce_sum | solution.py:34
  112.5 8.9 %pmax.44 = f32[1024]{0:T(1024)S(1)} all-reduce(f32[1024]{0:T(1024)S(1)} %fusion.2), channel_id=1, replica_groups=mesh['src'=8,'tgt'=4] {'tgt'}, use_global_device_ids=true, to_apply=%region_11.0 | all-reduce | flops 1024 | bytes 8192 | tf_op jit(solution)/shard_map/pmax | solution.py:35
  121.4 8.2 %psum.58 = f32[1024]{0:T(1024)S(1)} all-reduce(f32[1024]{0:T(1024)S(1)} %exponential_multiply_fusion.4), channel_id=1, replica_groups=mesh['src'=8,'tgt'=4] {'tgt'}, use_global_device_ids=true, to_apply=%region_13.0 | all-reduce | flops 1024 | bytes 8192 | tf_op jit(solution)/shard_map/psum | solution.py:36
  134.0 4.5 %exponential_reduce_fusion.2 = f32[2048]{0:T(1024)S(1)} fusion(f32[1024,2048]{1,0:T(8,128)} %get-tuple-element.4, f32[2048]{0:T(1024)S(1)} %fusion.3, f32[1024]{0:T(1024)S(1)} %multiply_subtract_fusion.4), kind=kLoop, calls=%fused_computation.5 | loop fusion | flops 8386560 | bytes 8409088 | tf_op jit(solution)/shard_map/reduce_sum | solution.py:40
  138.5 13.9 %pmax.45 = f32[2048]{0:T(1024)S(1)} all-reduce(f32[2048]{0:T(1024)S(1)} %fusion.3), channel_id=1, replica_groups=mesh['src'=8,'tgt'=4] {'src'}, use_global_device_ids=true, to_apply=%region_15.0 | all-reduce | flops 2048 | bytes 16384 | tf_op jit(solution)/shard_map/pmax | solution.py:41
  152.4 13.9 %psum.59 = f32[2048]{0:T(1024)S(1)} all-reduce(f32[2048]{0:T(1024)S(1)} %exponential_multiply_fusion.1), channel_id=1, replica_groups=mesh['src'=8,'tgt'=4] {'src'}, use_global_device_ids=true, to_apply=%region_17.0 | all-reduce | flops 2048 | bytes 16384 | tf_op jit(solution)/shard_map/psum | solution.py:42
  170.7 4.5 %exponential_reduce_fusion.1 = f32[1024]{0:T(1024)S(1)} fusion(f32[1024,2048]{1,0:T(8,128)} %get-tuple-element.4, f32[1024]{0:T(1024)S(1)} %fusion.4, f32[2048]{0:T(1024)S(1)} %multiply_subtract_fusion.1), kind=kLoop, calls=%fused_computation.3 | loop fusion | flops 8387584 | bytes 8404992 | tf_op jit(solution)/shard_map/reduce_sum | solution.py:34
  175.2 8.9 %pmax.46 = f32[1024]{0:T(1024)S(1)} all-reduce(f32[1024]{0:T(1024)S(1)} %fusion.4), channel_id=1, replica_groups=mesh['src'=8,'tgt'=4] {'tgt'}, use_global_device_ids=true, to_apply=%region_19.0 | all-reduce | flops 1024 | bytes 8192 | tf_op jit(solution)/shard_map/pmax | solution.py:35
  184.1 8.6 %psum.60 = f32[1024]{0:T(1024)S(1)} all-reduce(f32[1024]{0:T(1024)S(1)} %exponential_multiply_fusion.3), channel_id=1, replica_groups=mesh['src'=8,'tgt'=4] {'tgt'}, use_global_device_ids=true, to_apply=%region_21.0 | all-reduce | flops 1024 | bytes 8192 | tf_op jit(solution)/shard_map/psum | solution.py:36
  197.0 4.5 %exponential_reduce_fusion = f32[2048]{0:T(1024)S(1)} fusion(f32[1024,2048]{1,0:T(8,128)} %get-tuple-element.4, f32[2048]{0:T(1024)S(1)} %fusion.5, f32[1024]{0:T(1024)S(1)} %multiply_subtract_fusion.3), kind=kLoop, calls=%fused_computation.1 | loop fusion | flops 8386560 | bytes 8409088 | tf_op jit(solution)/shard_map/reduce_sum | solution.py:40
  201.6 13.9 %pmax.47 = f32[2048]{0:T(1024)S(1)} all-reduce(f32[2048]{0:T(1024)S(1)} %fusion.5), channel_id=1, replica_groups=mesh['src'=8,'tgt'=4] {'src'}, use_global_device_ids=true, to_apply=%region_23.0 | all-reduce | flops 2048 | bytes 16384 | tf_op jit(solution)/shard_map/pmax | solution.py:41
  215.5 14.1 %psum.61 = f32[2048]{0:T(1024)S(1)} all-reduce(f32[2048]{0:T(1024)S(1)} %exponential_multiply_fusion), channel_id=1, replica_groups=mesh['src'=8,'tgt'=4] {'src'}, use_global_device_ids=true, to_apply=%region_25.0 | all-reduce | flops 2048 | bytes 16384 | tf_op jit(solution)/shard_map/psum | solution.py:42
  229.7 13.6 %fusion.11 = f32[64,1024]{1,0:T(8,128)} fusion(f32[64,2048]{1,0:T(8,128)S(1)} %all_gather.7, f32[1024,2048]{1,0:T(8,128)} %get-tuple-element.4, f32[2048]{0:T(1024)S(1)} %multiply_subtract_fusion, f32[1024]{0:T(1024)S(1)} %multiply_subtract_fusion.3), kind=kOutput, calls=%fused_computation.25 | convolution fusion | flops 1616904192 | bytes 9187328 | tf_op jit(solution)/shard_map/dot_general | solution.py:45
  243.3 4.6 %fusion.6 = f32[1024]{0:T(1024)S(1)} fusion(f32[1024,2048]{1,0:T(8,128)} %get-tuple-element.4, f32[2048]{0:T(1024)S(1)} %multiply_subtract_fusion, f32[1024]{0:T(1024)S(1)} %multiply_subtract_fusion.3), kind=kLoop, calls=%fused_computation.20 | loop fusion | flops 8387584 | bytes 8404992 | tf_op jit(solution)/shard_map/reduce_sum | solution.py:52
  247.9 8.8 %psum.63 = f32[1024]{0:T(1024)S(1)} all-reduce(f32[1024]{0:T(1024)S(1)} %fusion.6), channel_id=1, replica_groups=mesh['src'=8,'tgt'=4] {'tgt'}, use_global_device_ids=true, to_apply=%region_28.0 | all-reduce | flops 1024 | bytes 8192 | tf_op jit(solution)/shard_map/psum | solution.py:54
  256.8 27.0 %all-reduce.2.cloned.1.call-done = f32[64,1024]{1,0:T(8,128)} async-done(((f32[64,1024]{1,0:T(8,128)}), f32[64,1024]{1,0:T(8,128)}) %all-reduce.2.cloned.1.call-update) | async-done | bytes 262160 | tf_op jit(solution)/shard_map/psum | solution.py:54
  (33 shorter events, 27.7 us)
Async XLA Ops:
  7.2 276.6 %all-reduce.2.cloned.1.call-start = ((), (), s32[]{:S(2)}) async-start(), calls=%async_computation | async-start | bytes 524288 | tf_op jit(solution)/shard_map/psum | solution.py:54
  33.4 20.4 %copy-start.4 = (f32[2048]{0:T(1024)S(1)}, f32[2048]{0:T(1024)}, u32[]{:S(2)}) copy-start(f32[2048]{0:T(1024)} %param.9) | copy-start | bytes 24580
  44.8 22.2 %copy-start.2 = (f32[1024]{0:T(1024)S(1)}, f32[1024]{0:T(1024)}, u32[]{:S(2)}) copy-start(f32[1024]{0:T(1024)} %param.7) | copy-start | bytes 12292
  67.0 36.7 %copy-start = (f32[2048]{0:T(1024)S(1)}, f32[2048]{0:T(1024)}, u32[]{:S(2)}) copy-start(f32[2048]{0:T(1024)} %param.8) | copy-start | bytes 24580
  192.8 50.5 %copy-start.1 = (f32[1024]{0:T(1024)}, f32[1024]{0:T(1024)S(1)}, u32[]{:S(2)}) copy-start(f32[1024]{0:T(1024)S(1)} %multiply_subtract_fusion.3) | copy-start | bytes 12292
  229.7 18.2 %copy-start.3 = (f32[2048]{0:T(1024)}, f32[2048]{0:T(1024)S(1)}, u32[]{:S(2)}) copy-start(f32[2048]{0:T(1024)S(1)} %multiply_subtract_fusion) | copy-start | bytes 24580
Sparse Core Ops, SparseCore 0:
  243.4 40.3 all-reduce.1
where the time goes:
time: 293 us; the launch traced here: 292 us
  blocking collectives  171 us (58%)
  other arithmetic  54.8 us (19%)
  waiting for transfers between devices  27 us (9%)
  matrix products  25 us (9%)
  between operations  14.2 us (5%)
    psum x3, blocking collectives, shards(): whole_sum = lax.psum(total * jnp.exp(top - whole_top), 'src')  42 us
    pmax x3, blocking collectives, shards(): whole_top = lax.pmax(top, 'src')  41.7 us
    psum x1, waiting for transfers between devices, shards(): numer_all, denom_all = lax.psum((numer, denom), 'tgt')  27 us
    pmax x3, blocking collectives, shards(): src_whole_top = lax.pmax(src_top, 'tgt')  26.9 us
    psum x3, blocking collectives, shards(): lax.psum(src_total * jnp.exp(src_top - src_whole_top), 'tgt')  25.5 us
    all_gather x1, blocking collectives, shards(): ys = lax.all_gather(tgt_pts, 'src', axis=0, tiled=True)  16.8 us
    dot_general x1, matrix products, shards(): lax.dot_general(ys, weight, (((1,), (1,)), ((), ())), precision=lax.Preci...  13.6 us
    reduce_sum x3, other arithmetic, shards(): total = jnp.sum(jnp.exp(score - top[None, :]), axis=0)  13.5 us
  transfers between devices with their start and end apart: 1, of which 1 were waited for; matrix products, arithmetic and copies ran while one was open for 2% of the time, Pallas kernels for 0%

commit v1 on v0

v1 whole, which is shorter than its diff:
```python
import functools
import math

import jax
import jax.numpy as jnp
from jax import lax
from jax.experimental import pallas as pl
from jax.experimental.pallas import tpu as pltpu
from jax.sharding import PartitionSpec as P

ITERS = 3
EPS = 0.1
UNIT = EPS * math.log(2.0)

F32 = jnp.float32
BF16 = jnp.bfloat16
VMEM = pl.BlockSpec(memory_space=pltpu.VMEM)
LANES = 128


def pieces(v):
    a = v.astype(BF16)
    r = v - a.astype(F32)
    b = r.astype(BF16)
    c = (r - b.astype(F32)).astype(BF16)
    return a, b, c


def tree(op, items):
    items = list(items)
    while len(items) > 1:
        half = (len(items) + 1) // 2
        rest = items[half:]
        items = [op(items[k], rest[k]) if k < len(rest) else items[k] for k in range(half)]
    return items[0]


def whole_log_sum(parts):
    top = tree(jnp.maximum, parts)
    return top + jnp.log2(tree(jnp.add, [jnp.exp2(p - top) for p in parts]))


def rows_log_sum(s_ref, pot, top_ref, sum_ref):
    n, width = s_ref.shape
    cols = width // LANES
    pot8 = jnp.broadcast_to(pot, (8, width))

    def strip(k, _):
        rows = pl.ds(pl.multiple_of(k * 8, 8), 8)
        z = [s_ref[rows, pl.ds(c * LANES, LANES)] + pot8[:, c * LANES : (c + 1) * LANES] for c in range(cols)]
        top = tree(jnp.maximum, z)
        top_ref[rows, :] = top
        sum_ref[rows, :] = tree(jnp.add, [jnp.exp2(v - top) for v in z])
        return 0

    lax.fori_loop(0, n // 8, strip, 0, unroll=4)
    tops = top_ref[...].T
    top = jnp.max(tops, axis=0, keepdims=True)
    total = jnp.sum(sum_ref[...].T * jnp.exp2(tops - top), axis=0, keepdims=True)
    return top + jnp.log2(total)


def across(pot, out_ref):
    n = pot.shape[1]
    out_ref[...] = jnp.broadcast_to(pot, (LANES, n)).T


def cols_log_sum(s_ref, pot_ref):
    n, width = s_ref.shape
    cols = width // LANES

    def load(k):
        rows = pl.ds(pl.multiple_of(k * 8, 8), 8)
        f = pot_ref[rows, :]
        return [s_ref[rows, pl.ds(c * LANES, LANES)] + f for c in range(cols)]

    def find(k, top):
        return tuple(jnp.maximum(t, v) for t, v in zip(top, load(k)))

    top = lax.fori_loop(1, n // 8, find, tuple(load(0)), unroll=4)

    def add(k, total):
        return tuple(a + jnp.exp2(v - t) for a, v, t in zip(total, load(k), top))

    zero = tuple(jnp.zeros((8, LANES), F32) for _ in range(cols))
    total = lax.fori_loop(0, n // 8, add, zero, unroll=4)
    out = []
    for t, a in zip(top, total):
        m = jnp.max(t, axis=0, keepdims=True)
        out.append(m + jnp.log2(jnp.sum(a * jnp.exp2(t - m), axis=0, keepdims=True)))
    return jnp.concatenate(out, axis=1)


def first_kernel(x_ref, y_ref, pot_ref, s_ref, l_ref, xn_ref, yn_ref, xw, yw, top_ref, sum_ref):
    k = x_ref.shape[0]
    x = x_ref[...]
    y = y_ref[...]
    xn = jnp.sum(x * x, axis=0, keepdims=True) / k
    yn = jnp.sum(y * y, axis=0, keepdims=True) / k
    xn_ref[...] = xn
    yn_ref[...] = yn
    x1, x2, x3 = pieces(x)
    y1, y2, y3 = pieces(y * (2.0 / (k * UNIT)))
    for p, (xp, yp) in enumerate(((x1, y1), (x1, y2), (x2, y1), (x2, y2), (x1, y3), (x3, y1))):
        xw[pl.ds(p * k, k), :] = xp
        yw[pl.ds(p * k, k), :] = yp
    step = 256

    def block(b, _):
        rows = pl.ds(pl.multiple_of(b * step, step), step)
        s_ref[rows, :] = lax.dot_general(
            xw[:, rows], yw[...], (((0,), (0,)), ((), ())), preferred_element_type=F32
        )
        return 0

    lax.fori_loop(0, s_ref.shape[0] // step, block, 0)
    pot = (pot_ref[...] - yn) * (1.0 / UNIT)
    l_ref[...] = rows_log_sum(s_ref, pot, top_ref, sum_ref)


def src_kernel(count, s_ref, mass_ref, *refs):
    parts, (f_ref, l_ref, wide) = refs[:count], refs[count:]
    f = jnp.log2(mass_ref[...]) - whole_log_sum([p[...] for p in parts])
    f_ref[...] = f
    across(f, wide)
    l_ref[...] = cols_log_sum(s_ref, wide)


def tgt_kernel(count, s_ref, mass_ref, *refs):
    parts, (l_ref, top_ref, sum_ref) = refs[:count], refs[count:]
    g = jnp.log2(mass_ref[...]) - whole_log_sum([p[...] for p in parts])
    l_ref[...] = rows_log_sum(s_ref, g, top_ref, sum_ref)


def last_kernel(count, peers, me_ref, s_ref, mass_ref, f_ref, xn_ref, yn_ref, y_ref, *refs):
    parts, refs = refs[:count], refs[count:]
    sp_ref, tp_ref, outs, (wide, yw, acc, flat) = refs[0], refs[1], refs[2 : 2 + peers], refs[2 + peers :]
    k = y_ref.shape[0]
    n, width = s_ref.shape
    g = jnp.log2(mass_ref[...]) - whole_log_sum([p[...] for p in parts])
    f = f_ref[...]
    sp_ref[...] = f * UNIT + xn_ref[...]
    tp_ref[...] = g * UNIT + yn_ref[...]
    across(f, wide)
    y1, y2, _ = pieces(y_ref[...])
    yw[pl.ds(0, k), :] = y1
    yw[pl.ds(k, k), :] = y2
    yw[pl.ds(2 * k, 16), :] = jnp.ones((16, width), BF16)
    step = 128

    def block(b, _):
        rows = pl.ds(pl.multiple_of(b * step, step), step)
        fb = wide[rows, :]
        w = jnp.exp2(s_ref[rows, :] + g + jnp.concatenate([fb] * (width // LANES), axis=1))
        w1 = w.astype(BF16)
        w2 = (w - w1.astype(F32)).astype(BF16)
        dims = (((1,), (1,)), ((), ()))
        one = lax.dot_general(w1, yw[...], dims, preferred_element_type=F32)
        two = lax.dot_general(w2, yw[...], dims, preferred_element_type=F32)
        acc[rows, :] = one + two
        return 0

    lax.fori_loop(0, n // step, block, 0)
    whole = acc[:, : 2 * k].T
    num = whole[:k, :] + whole[k:, :]
    own = k // peers
    for t in range(peers):
        flat[t] = num[t * own : (t + 1) * own, :]
    den = jnp.broadcast_to(acc[:, 2 * k : 2 * k + 1], (n, LANES)).T[0:1, :]
    me = me_ref[0]
    for d, out in enumerate(outs):
        out[pl.ds(0, own), :] = flat[lax.rem(me + d, peers)]
        out[pl.ds(own, 1), :] = den


def join_kernel(own, *refs):
    parts, out_ref = refs[:-1], refs[-1]
    num = tree(jnp.add, [p[pl.ds(0, own), :] for p in parts])
    den = tree(jnp.add, [p[pl.ds(own, 1), :] for p in parts])
    out_ref[...] = num / den


def call(kernel, outs, scratch, *args, scalars=0):
    smem = pl.BlockSpec(memory_space=pltpu.SMEM)
    return pl.pallas_call(
        kernel,
        out_shape=[jax.ShapeDtypeStruct(s, F32) for s in outs],
        in_specs=[smem] * scalars + [VMEM] * (len(args) - scalars),
        out_specs=[VMEM] * len(outs),
        scratch_shapes=scratch,
        compiler_params=pltpu.CompilerParams(vmem_limit_bytes=32 * 2**20),
    )(*args)


def everyone(v, axis, size):
    return [v] + [lax.ppermute(v, axis, [(i, (i + d) % size) for i in range(size)]) for d in range(1, size)]


def shards(peers_src, peers_tgt, src_pts, tgt_pts, src_mass, tgt_mass, init_pot):
    own = src_pts.shape[0]
    n, width = src_pts.shape[1], tgt_pts.shape[1]
    xs = lax.all_gather(src_pts, "tgt", axis=0, tiled=True)
    ys = lax.all_gather(tgt_pts, "src", axis=0, tiled=True)
    k = xs.shape[0]
    src_mass = src_mass.reshape(1, n)
    tgt_mass = tgt_mass.reshape(1, width)
    row, col = (1, n), (1, width)
    lane = pltpu.VMEM((n, LANES), F32)
    s, l, xn, yn = call(
        first_kernel,
        [(n, width), row, row, col],
        [pltpu.VMEM((6 * k, n), BF16), pltpu.VMEM((6 * k, width), BF16), lane, lane],
        xs,
        ys,
        init_pot.reshape(1, width),
    )
    for step in range(ITERS):
        parts = everyone(l, "tgt", peers_tgt)
        f, l = call(functools.partial(src_kernel, len(parts)), [row, col], [lane], s, src_mass, *parts)
        parts = everyone(l, "src", peers_src)
        if step < ITERS - 1:
            (l,) = call(functools.partial(tgt_kernel, len(parts)), [row], [lane, lane], s, tgt_mass, *parts)
    me = lax.axis_index("tgt").astype(jnp.int32).reshape(1)
    src_pot, tgt_pot, *blocks = call(
        functools.partial(last_kernel, len(parts), peers_tgt),
        [row, col] + [(own + 1, n)] * peers_tgt,
        [lane, pltpu.VMEM((2 * k + 16, width), BF16), pltpu.VMEM((n, 2 * k + 16), F32), pltpu.VMEM((peers_tgt, own, n), F32)],
        me,
        s,
        tgt_mass,
        f,
        xn,
        yn,
        ys,
        *parts,
        scalars=1,
    )
    came = [blocks[0]] + [
        lax.ppermute(blocks[d], "tgt", [(i, (i + d) % peers_tgt) for i in range(peers_tgt)])
        for d in range(1, peers_tgt)
    ]
    (mapped,) = call(functools.partial(join_kernel, own), [(own, n)], [], *came)
    return src_pot.reshape(n), tgt_pot.reshape(width), mapped


def solution(mesh):
    return jax.shard_map(
        functools.partial(shards, mesh.shape["src"], mesh.shape["tgt"]),
        mesh=mesh,
        in_specs=(P("tgt", "src"), P("src", "tgt"), P("src"), P("tgt"), P("tgt")),
        out_specs=(P("src"), P("tgt"), P("tgt", "src")),
        check_vma=False,
    )
```

time: 293 us -> 115 us (0.39)
  blocking collectives: 171 us -> 26.3 us
  other arithmetic: 54.8 us -> 0 us
  starting transfers between devices: 0.04 us -> 30.4 us
  Pallas kernels: 0 us -> 25.4 us
  matrix products: 25 us -> 0 us
  between operations: 14.2 us -> 0.72 us
  local copies, waits for them, and re-layouts: 0.03 us -> 4.78 us
    psum x7 -> x0, blocking collectives: 76.3 us -> none  [the longest x3 42 us: shards(): whole_sum = lax.psum(total * jnp.exp(top - whole_top), 'src')]
    pmax x6 -> x0, blocking collectives: 68.7 us -> none  [the longest x3 41.7 us: shards(): whole_top = lax.pmax(top, 'src')]
    reduce_sum x9 -> x0, other arithmetic: 31.7 us -> none  [the longest x3 13.5 us: shards(): total = jnp.sum(jnp.exp(score - top[None, :]), axis=0)]
    ppermute x0 -> x33, starting transfers between devices: none -> 30.4 us  [the longest x30 26.2 us: everyone(): lax.ppermute(v, axis, [(i, (i + d) % size) for i in range(size)])]
    psum x1 -> x0, waiting for transfers between devices: 27 us -> none  [shards(): numer_all, denom_all = lax.psum((numer, denom), 'tgt')]
    ppermute x0 -> x33, waiting for transfers between devices: none -> 26.8 us  [the longest x30 24.6 us: everyone(): lax.ppermute(v, axis, [(i, (i + d) % size) for i in range(size)])]
    pallas_call x0 -> x8, Pallas kernels: none -> 25.4 us  [call(): pl.pallas_call(kernel, out_shape=[jax.ShapeDtypeStruct(s, F32) for s in o...]
    dot_general x2 -> x0, matrix products: 25 us -> none  [the longest x1 13.6 us: shards(): lax.dot_general(ys, weight, (((1,), (1,)), ((), ())), precision=lax.Preci...]
  transfers between devices with their start and end apart: 1 -> 33, of which waited for: 1 -> 22; matrix products, arithmetic and copies ran while one was open for 2% -> 0% of each run, Pallas kernels for 0% -> 0%
where the time goes in v1:
time: 115 us; the launch traced here: 114 us
  starting transfers between devices  30.4 us (26%)
  waiting for transfers between devices  26.8 us (23%)
  blocking collectives  26.3 us (23%)
  Pallas kernels  25.4 us (22%)
  local copies, waits for them, and re-layouts  4.78 us (4%)
    ppermute x30, starting transfers between devices, everyone(): lax.ppermute(v, axis, [(i, (i + d) % size) for i in range(size)])  26.2 us
    pallas_call x8, Pallas kernels, call(): pl.pallas_call(kernel, out_shape=[jax.ShapeDtypeStruct(s, F32) for s in o...  25.4 us
    ppermute x30, waiting for transfers between devices, everyone(): lax.ppermute(v, axis, [(i, (i + d) % size) for i in range(size)])  24.6 us
    all_gather x1, blocking collectives, shards(): ys = lax.all_gather(tgt_pts, 'src', axis=0, tiled=True)  15.6 us
    all_gather x1, blocking collectives, shards(): xs = lax.all_gather(src_pts, 'tgt', axis=0, tiled=True)  10.7 us
    unnamed x12, local copies, waits for them, and re-layouts  4.78 us
    ppermute x3, starting transfers between devices, shards(): lax.ppermute(blocks[d], 'tgt', [(i, (i + d) % peers_tgt) for i in range(p...  4.14 us
  transfers between devices with their start and end apart: 33, of which 22 were waited for; matrix products, arithmetic and copies ran while one was open for 0% of the time, Pallas kernels for 0%

profile of v1, /device:TPU:0, one launch (start us, length us, event | category | flops | bytes accessed | tf_op | source)
XLA Modules:
  0.0 114.4 jit_solution(14778457858973263614)
XLA Ops:
  0.6 10.7 %all_gather.6.x_ref = f32[64,1024]{1,0:T(8,128)S(1)} all-gather(f32[16,1024]{1,0:T(8,128)} %param.5), channel_id=1, replica_groups=mesh['src'=8,'tgt'=4] {'tgt'}, dimensions={0}, use_global_device_ids=true | all-gather | bytes 327680 | tf_op jit(solution)/shard_map/all_gather | solution.py:202
  11.4 15.6 %all_gather.7.y_ref = f32[64,2048]{1,0:T(8,128)S(1)} all-gather(f32[8,2048]{1,0:T(8,128)} %param.6), channel_id=1, replica_groups=mesh['src'=8,'tgt'=4] {'src'}, dimensions={0}, use_global_device_ids=true | all-gather | bytes 589824 | tf_op jit(solution)/shard_map/all_gather | solution.py:203
  27.7 5.8 %shard_map.76 = (f32[1024,2048]{1,0:T(8,128)S(1)}, f32[1,1024]{1,0:T(1,128)S(1)}, f32[1,1024]{1,0:T(1,128)S(1)}, f32[1,2048]{1,0:T(1,128)S(1)}) custom-call(f32[64,1024]{1,0:T(8,128)S(1)} %all_gather.6.x_ref, f32[64,2048]{1,0:T(8,128)S(1)} %all_gather.7.y_ref, f32[1,2048]{1,0:T(1,128)S(1)} %bitcast.12), custom_call_target="tpu_custom_call" | custom-call | tf_op jit(solution)/shard_map/pallas_call | solution.py:185
  33.5 1.5 %collective-permute-start.2 = (f32[1,1024]{1,0:T(1,128)S(1)}, f32[1,1024]{1,0:T(1,128)S(1)}, u32[]{:S(2)}, u32[]{:S(2)}) collective-permute-start(f32[1,1024]{1,0:T(1,128)S(1)} %get-tuple-element.18.refs_0_), channel_id=1, source_target_pairs={{0,3},{1,0},{2,1},{3,2},{4,7},{5,4},{6,5},{7,6},{8,11},{9,8},{10,9... | collective-permute-start | bytes 12296 | tf_op jit(solution)/shard_map/ppermute | solution.py:196
  38.6 2.1 %collective-permute-done.refs_1_ = f32[1,1024]{1,0:T(1,128)S(1)} collective-permute-done((f32[1,1024]{1,0:T(1,128)S(1)}, f32[1,1024]{1,0:T(1,128)S(1)}, u32[]{:S(2)}, u32[]{:S(2)}) %collective-permute-start) | collective-permute-done | bytes 4128 | tf_op jit(solution)/shard_map/ppermute | solution.py:196
  41.4 3.1 %shard_map.77 = (f32[1,1024]{1,0:T(1,128)}, f32[1,2048]{1,0:T(1,128)S(1)}) custom-call(f32[1024,2048]{1,0:T(8,128)S(1)} %get-tuple-element.17.s_ref, f32[1,1024]{1,0:T(1,128)S(1)} %bitcast.9, f32[1,1024]{1,0:T(1,128)S(1)} %get-tuple-element.18.refs_0_, f32[1,1024]{1,0:T(1,128)S(1)} %collective-permute-done.refs_1_, ...), custom_call_target="tpu_custom_call" | custom-call | tf_op jit(solution)/shard_map/pallas_call | solution.py:185
  45.9 1.8 %collective-permute-start.8 = (f32[1,2048]{1,0:T(1,128)S(1)}, f32[1,2048]{1,0:T(1,128)S(1)}, u32[]{:S(2)}, u32[]{:S(2)}) collective-permute-start(f32[1,2048]{1,0:T(1,128)S(1)} %get-tuple-element.19.refs_0_), channel_id=1, source_target_pairs={{0,24},{4,28},{8,0},{12,4},{16,8},{20,12},{24,16},{28,20},{1,25},{... | collective-permute-start | bytes 24584 | tf_op jit(solution)/shard_map/ppermute | solution.py:196
  47.6 2.8 %collective-permute-start.6 = (f32[1,2048]{1,0:T(1,128)S(1)}, f32[1,2048]{1,0:T(1,128)S(1)}, u32[]{:S(2)}, u32[]{:S(2)}) collective-permute-start(f32[1,2048]{1,0:T(1,128)S(1)} %get-tuple-element.19.refs_0_), channel_id=1, source_target_pairs={{0,16},{4,20},{8,24},{12,28},{16,0},{20,4},{24,8},{28,12},{1,17},{... | collective-permute-start | bytes 24584 | tf_op jit(solution)/shard_map/ppermute | solution.py:196
  52.2 2.2 %collective-permute-done.5.refs_3_ = f32[1,2048]{1,0:T(1,128)S(1)} collective-permute-done((f32[1,2048]{1,0:T(1,128)S(1)}, f32[1,2048]{1,0:T(1,128)S(1)}, u32[]{:S(2)}, u32[]{:S(2)}) %collective-permute-start.5) | collective-permute-done | bytes 8224 | tf_op jit(solution)/shard_map/ppermute | solution.py:196
  55.8 2.5 %shard_map.78.refs_0_ = f32[1,1024]{1,0:T(1,128)S(1)} custom-call(f32[1024,2048]{1,0:T(8,128)S(1)} %get-tuple-element.17.s_ref, f32[1,2048]{1,0:T(1,128)S(1)} %bitcast.6, f32[1,2048]{1,0:T(1,128)S(1)} %get-tuple-element.19.refs_0_, f32[1,2048]{1,0:T(1,128)S(1)} %collective-permute-done.3.refs_1_, f32[1,2048]{1,0:T(1,128)S(1)} %collective-permute-done.4.refs_2_, ...), custom_call_target="tpu_custom_call" | custom-call | tf_op jit(solution)/shard_map/pallas_call | solution.py:185
  59.6 1.7 %collective-permute-start.10 = (f32[1,1024]{1,0:T(1,128)S(1)}, f32[1,1024]{1,0:T(1,128)S(1)}, u32[]{:S(2)}, u32[]{:S(2)}) collective-permute-start(f32[1,1024]{1,0:T(1,128)S(1)} %shard_map.78.refs_0_), channel_id=1, source_target_pairs={{0,1},{1,2},{2,3},{3,0},{4,5},{5,6},{6,7},{7,4},{8,9},{9,10},{10,1... | collective-permute-start | bytes 12296 | tf_op jit(solution)/shard_map/ppermute | solution.py:196
  62.1 1.9 %collective-permute-done.10.refs_1_ = f32[1,1024]{1,0:T(1,128)S(1)} collective-permute-done((f32[1,1024]{1,0:T(1,128)S(1)}, f32[1,1024]{1,0:T(1,128)S(1)}, u32[]{:S(2)}, u32[]{:S(2)}) %collective-permute-start.10) | collective-permute-done | bytes 4128 | tf_op jit(solution)/shard_map/ppermute | solution.py:196
  64.1 3.1 %shard_map.79 = (f32[1,1024]{1,0:T(1,128)}, f32[1,2048]{1,0:T(1,128)S(1)}) custom-call(f32[1024,2048]{1,0:T(8,128)S(1)} %get-tuple-element.17.s_ref, f32[1,1024]{1,0:T(1,128)S(1)} %bitcast.10, f32[1,1024]{1,0:T(1,128)S(1)} %shard_map.78.refs_0_, f32[1,1024]{1,0:T(1,128)S(1)} %collective-permute-done.10.refs_1_, ...), custom_call_target="tpu_custom_call" | custom-call | tf_op jit(solution)/shard_map/pallas_call | solution.py:185
  68.6 2.8 %collective-permute-start.16 = (f32[1,2048]{1,0:T(1,128)S(1)}, f32[1,2048]{1,0:T(1,128)S(1)}, u32[]{:S(2)}, u32[]{:S(2)}) collective-permute-start(f32[1,2048]{1,0:T(1,128)S(1)} %get-tuple-element.20.refs_0_), channel_id=1, source_target_pairs={{0,16},{4,20},{8,24},{12,28},{16,0},{20,4},{24,8},{28,12},{1,17},{... | collective-permute-start | bytes 24584 | tf_op jit(solution)/shard_map/ppermute | solution.py:196
  73.3 2.1 %collective-permute-done.15.refs_3_ = f32[1,2048]{1,0:T(1,128)S(1)} collective-permute-done((f32[1,2048]{1,0:T(1,128)S(1)}, f32[1,2048]{1,0:T(1,128)S(1)}, u32[]{:S(2)}, u32[]{:S(2)}) %collective-permute-start.15) | collective-permute-done | bytes 8224 | tf_op jit(solution)/shard_map/ppermute | solution.py:196
  77.2 2.5 %shard_map.80.refs_0_ = f32[1,1024]{1,0:T(1,128)S(1)} custom-call(f32[1024,2048]{1,0:T(8,128)S(1)} %get-tuple-element.17.s_ref, f32[1,2048]{1,0:T(1,128)S(1)} %bitcast.7, f32[1,2048]{1,0:T(1,128)S(1)} %get-tuple-element.20.refs_0_, f32[1,2048]{1,0:T(1,128)S(1)} %collective-permute-done.13.refs_1_, f32[1,2048]{1,0:T(1,128)S(1)} %collective-permute-done.14.refs_2_, ...), custom_call_target="tpu_custom_call" | custom-call | tf_op jit(solution)/shard_map/pallas_call | solution.py:185
  84.6 1.7 %collective-permute-done.20.refs_1_ = f32[1,1024]{1,0:T(1,128)S(1)} collective-permute-done((f32[1,1024]{1,0:T(1,128)S(1)}, f32[1,1024]{1,0:T(1,128)S(1)}, u32[]{:S(2)}, u32[]{:S(2)}) %collective-permute-start.20) | collective-permute-done | bytes 4128 | tf_op jit(solution)/shard_map/ppermute | solution.py:196
  86.3 2.6 %shard_map.81 = (f32[1,1024]{1,0:T(1,128)S(1)}, f32[1,2048]{1,0:T(1,128)S(1)}) custom-call(f32[1024,2048]{1,0:T(8,128)S(1)} %get-tuple-element.17.s_ref, f32[1,1024]{1,0:T(1,128)S(1)} %bitcast.11, f32[1,1024]{1,0:T(1,128)S(1)} %shard_map.80.refs_0_, f32[1,1024]{1,0:T(1,128)S(1)} %collective-permute-done.20.refs_1_, ...), custom_call_target="tpu_custom_call" | custom-call | tf_op jit(solution)/shard_map/pallas_call | solution.py:185
  90.4 2.7 %collective-permute-start.26 = (f32[1,2048]{1,0:T(1,128)S(1)}, f32[1,2048]{1,0:T(1,128)S(1)}, u32[]{:S(2)}, u32[]{:S(2)}) collective-permute-start(f32[1,2048]{1,0:T(1,128)S(1)} %get-tuple-element.24.refs_0_), channel_id=1, source_target_pairs={{0,16},{4,20},{8,24},{12,28},{16,0},{20,4},{24,8},{28,12},{1,17},{... | collective-permute-start | bytes 24584 | tf_op jit(solution)/shard_map/ppermute | solution.py:196
  95.0 2.1 %collective-permute-done.25.refs_3_ = f32[1,2048]{1,0:T(1,128)S(1)} collective-permute-done((f32[1,2048]{1,0:T(1,128)S(1)}, f32[1,2048]{1,0:T(1,128)S(1)}, u32[]{:S(2)}, u32[]{:S(2)}) %collective-permute-start.25) | collective-permute-done | bytes 8224 | tf_op jit(solution)/shard_map/ppermute | solution.py:196
  99.0 3.4 %copy-done.1 = f32[1024,2048]{1,0:T(8,128)S(1)} copy-done((f32[1024,2048]{1,0:T(8,128)S(1)}, f32[1024,2048]{1,0:T(8,128)}, u32[]{:S(2)}) %copy-start.1) | copy-done | bytes 8388632
  102.3 5.1 %shard_map.82 = (f32[1,1024]{1,0:T(1,128)}, f32[1,2048]{1,0:T(1,128)}, f32[17,1024]{1,0:T(8,128)S(1)}, f32[17,1024]{1,0:T(8,128)S(1)}, f32[17,1024]{1,0:T(8,128)S(1)}, /*index=5*/f32[17,1024]{1,0:T(8,128)S(1)}) custom-call(s32[1]{0:T(128)} %bitcast.me_ref, f32[1024,2048]{1,0:T(8,128)S(1)} %copy-done.1, f32[1,2048]{1,0:T(1,128)S(1)} %bitcast.8, ...), custom_call_target="tpu_custom_call" | custom-call | tf_op jit(solution)/shard_map/pallas_call | solution.py:185
  108.6 2.9 %collective-permute-start.32 = (f32[17,1024]{1,0:T(8,128)S(1)}, f32[17,1024]{1,0:T(8,128)S(1)}, u32[]{:S(2)}, u32[]{:S(2)}) collective-permute-start(f32[17,1024]{1,0:T(8,128)S(1)} %get-tuple-element.30), channel_id=1, source_target_pairs={{0,3},{1,0},{2,1},{3,2},{4,7},{5,4},{6,5},{7,6},{8,11},{9,8},{10,9... | collective-permute-start | bytes 208904 | tf_op jit(solution)/shard_map/ppermute | solution.py:239
  111.6 1.5 %collective-permute-done.30.refs_1_ = f32[17,1024]{1,0:T(8,128)S(1)} collective-permute-done((f32[17,1024]{1,0:T(8,128)S(1)}, f32[17,1024]{1,0:T(8,128)S(1)}, u32[]{:S(2)}, u32[]{:S(2)}) %collective-permute-start.30) | collective-permute-done | bytes 69664 | tf_op jit(solution)/shard_map/ppermute | solution.py:239
  (64 shorter events, 29.5 us)
Async XLA Ops:
  36.2 4.5 %collective-permute-start = (f32[1,1024]{1,0:T(1,128)S(1)}, f32[1,1024]{1,0:T(1,128)S(1)}, u32[]{:S(2)}, u32[]{:S(2)}) collective-permute-start(f32[1,1024]{1,0:T(1,128)S(1)} %get-tuple-element.18.refs_0_), channel_id=1, source_target_pairs={{0,1},{1,2},{2,3},{3,0},{4,5},{5,6},{6,7},{7,4},{8,9},{9,10},{10,1... | collective-permute-start | bytes 12296 | tf_op jit(solution)/shard_map/ppermute | solution.py:196
  44.5 5.8 %collective-permute-start.9 = (f32[1,2048]{1,0:T(1,128)S(1)}, f32[1,2048]{1,0:T(1,128)S(1)}, u32[]{:S(2)}, u32[]{:S(2)}) collective-permute-start(f32[1,2048]{1,0:T(1,128)S(1)} %get-tuple-element.19.refs_0_), channel_id=1, source_target_pairs={{0,28},{4,0},{8,4},{12,8},{16,12},{20,16},{24,20},{28,24},{1,29},{... | collective-permute-start | bytes 24584 | tf_op jit(solution)/shard_map/ppermute | solution.py:196
  45.9 4.8 %collective-permute-start.8 = (f32[1,2048]{1,0:T(1,128)S(1)}, f32[1,2048]{1,0:T(1,128)S(1)}, u32[]{:S(2)}, u32[]{:S(2)}) collective-permute-start(f32[1,2048]{1,0:T(1,128)S(1)} %get-tuple-element.19.refs_0_), channel_id=1, source_target_pairs={{0,24},{4,28},{8,0},{12,4},{16,8},{20,12},{24,16},{28,20},{1,25},{... | collective-permute-start | bytes 24584 | tf_op jit(solution)/shard_map/ppermute | solution.py:196
  47.6 4.5 %collective-permute-start.6 = (f32[1,2048]{1,0:T(1,128)S(1)}, f32[1,2048]{1,0:T(1,128)S(1)}, u32[]{:S(2)}, u32[]{:S(2)}) collective-permute-start(f32[1,2048]{1,0:T(1,128)S(1)} %get-tuple-element.19.refs_0_), channel_id=1, source_target_pairs={{0,16},{4,20},{8,24},{12,28},{16,0},{20,4},{24,8},{28,12},{1,17},{... | collective-permute-start | bytes 24584 | tf_op jit(solution)/shard_map/ppermute | solution.py:196
  50.4 4.0 %collective-permute-start.5 = (f32[1,2048]{1,0:T(1,128)S(1)}, f32[1,2048]{1,0:T(1,128)S(1)}, u32[]{:S(2)}, u32[]{:S(2)}) collective-permute-start(f32[1,2048]{1,0:T(1,128)S(1)} %get-tuple-element.19.refs_0_), channel_id=1, source_target_pairs={{0,12},{4,16},{8,20},{12,24},{16,28},{20,0},{24,4},{28,8},{1,13},{... | collective-permute-start | bytes 24584 | tf_op jit(solution)/shard_map/ppermute | solution.py:196
  50.4 5.5 %collective-permute-start.4 = (f32[1,2048]{1,0:T(1,128)S(1)}, f32[1,2048]{1,0:T(1,128)S(1)}, u32[]{:S(2)}, u32[]{:S(2)}) collective-permute-start(f32[1,2048]{1,0:T(1,128)S(1)} %get-tuple-element.19.refs_0_), channel_id=1, source_target_pairs={{0,8},{4,12},{8,16},{12,20},{16,24},{20,28},{24,0},{28,4},{1,9},{5... | collective-permute-start | bytes 24584 | tf_op jit(solution)/shard_map/ppermute | solution.py:196
  50.7 5.1 %collective-permute-start.3 = (f32[1,2048]{1,0:T(1,128)S(1)}, f32[1,2048]{1,0:T(1,128)S(1)}, u32[]{:S(2)}, u32[]{:S(2)}) collective-permute-start(f32[1,2048]{1,0:T(1,128)S(1)} %get-tuple-element.19.refs_0_), channel_id=1, source_target_pairs={{0,4},{4,8},{8,12},{12,16},{16,20},{20,24},{24,28},{28,0},{1,5},{5... | collective-permute-start | bytes 24584 | tf_op jit(solution)/shard_map/ppermute | solution.py:196
  59.6 4.5 %collective-permute-start.10 = (f32[1,1024]{1,0:T(1,128)S(1)}, f32[1,1024]{1,0:T(1,128)S(1)}, u32[]{:S(2)}, u32[]{:S(2)}) collective-permute-start(f32[1,1024]{1,0:T(1,128)S(1)} %shard_map.78.refs_0_), channel_id=1, source_target_pairs={{0,1},{1,2},{2,3},{3,0},{4,5},{5,6},{6,7},{7,4},{8,9},{9,10},{10,1... | collective-permute-start | bytes 12296 | tf_op jit(solution)/shard_map/ppermute | solution.py:196
  67.2 4.2 %collective-permute-start.19 = (f32[1,2048]{1,0:T(1,128)S(1)}, f32[1,2048]{1,0:T(1,128)S(1)}, u32[]{:S(2)}, u32[]{:S(2)}) collective-permute-start(f32[1,2048]{1,0:T(1,128)S(1)} %get-tuple-element.20.refs_0_), channel_id=1, source_target_pairs={{0,28},{4,0},{8,4},{12,8},{16,12},{20,16},{24,20},{28,24},{1,29},{... | collective-permute-start | bytes 24584 | tf_op jit(solution)/shard_map/ppermute | solution.py:196
  67.2 5.1 %collective-permute-start.18 = (f32[1,2048]{1,0:T(1,128)S(1)}, f32[1,2048]{1,0:T(1,128)S(1)}, u32[]{:S(2)}, u32[]{:S(2)}) collective-permute-start(f32[1,2048]{1,0:T(1,128)S(1)} %get-tuple-element.20.refs_0_), channel_id=1, source_target_pairs={{0,24},{4,28},{8,0},{12,4},{16,8},{20,12},{24,16},{28,20},{1,25},{... | collective-permute-start | bytes 24584 | tf_op jit(solution)/shard_map/ppermute | solution.py:196
  68.6 4.6 %collective-permute-start.16 = (f32[1,2048]{1,0:T(1,128)S(1)}, f32[1,2048]{1,0:T(1,128)S(1)}, u32[]{:S(2)}, u32[]{:S(2)}) collective-permute-start(f32[1,2048]{1,0:T(1,128)S(1)} %get-tuple-element.20.refs_0_), channel_id=1, source_target_pairs={{0,16},{4,20},{8,24},{12,28},{16,0},{20,4},{24,8},{28,12},{1,17},{... | collective-permute-start | bytes 24584 | tf_op jit(solution)/shard_map/ppermute | solution.py:196
  71.4 4.0 %collective-permute-start.15 = (f32[1,2048]{1,0:T(1,128)S(1)}, f32[1,2048]{1,0:T(1,128)S(1)}, u32[]{:S(2)}, u32[]{:S(2)}) collective-permute-start(f32[1,2048]{1,0:T(1,128)S(1)} %get-tuple-element.20.refs_0_), channel_id=1, source_target_pairs={{0,12},{4,16},{8,20},{12,24},{16,28},{20,0},{24,4},{28,8},{1,13},{... | collective-permute-start | bytes 24584 | tf_op jit(solution)/shard_map/ppermute | solution.py:196
  71.4 5.5 %collective-permute-start.14 = (f32[1,2048]{1,0:T(1,128)S(1)}, f32[1,2048]{1,0:T(1,128)S(1)}, u32[]{:S(2)}, u32[]{:S(2)}) collective-permute-start(f32[1,2048]{1,0:T(1,128)S(1)} %get-tuple-element.20.refs_0_), channel_id=1, source_target_pairs={{0,8},{4,12},{8,16},{12,20},{16,24},{20,28},{24,0},{28,4},{1,9},{5... | collective-permute-start | bytes 24584 | tf_op jit(solution)/shard_map/ppermute | solution.py:196
  72.3 4.9 %collective-permute-start.13 = (f32[1,2048]{1,0:T(1,128)S(1)}, f32[1,2048]{1,0:T(1,128)S(1)}, u32[]{:S(2)}, u32[]{:S(2)}) collective-permute-start(f32[1,2048]{1,0:T(1,128)S(1)} %get-tuple-element.20.refs_0_), channel_id=1, source_target_pairs={{0,4},{4,8},{8,12},{12,16},{16,20},{20,24},{24,28},{28,0},{1,5},{5... | collective-permute-start | bytes 24584 | tf_op jit(solution)/shard_map/ppermute | solution.py:196
  81.8 4.5 %collective-permute-start.20 = (f32[1,1024]{1,0:T(1,128)S(1)}, f32[1,1024]{1,0:T(1,128)S(1)}, u32[]{:S(2)}, u32[]{:S(2)}) collective-permute-start(f32[1,1024]{1,0:T(1,128)S(1)} %shard_map.80.refs_0_), channel_id=1, source_target_pairs={{0,1},{1,2},{2,3},{3,0},{4,5},{5,6},{6,7},{7,4},{8,9},{9,10},{10,1... | collective-permute-start | bytes 12296 | tf_op jit(solution)/shard_map/ppermute | solution.py:196
  88.9 4.2 %collective-permute-start.29 = (f32[1,2048]{1,0:T(1,128)S(1)}, f32[1,2048]{1,0:T(1,128)S(1)}, u32[]{:S(2)}, u32[]{:S(2)}) collective-permute-start(f32[1,2048]{1,0:T(1,128)S(1)} %get-tuple-element.24.refs_0_), channel_id=1, source_target_pairs={{0,28},{4,0},{8,4},{12,8},{16,12},{20,16},{24,20},{28,24},{1,29},{... | collective-permute-start | bytes 24584 | tf_op jit(solution)/shard_map/ppermute | solution.py:196
  89.0 5.1 %collective-permute-start.28 = (f32[1,2048]{1,0:T(1,128)S(1)}, f32[1,2048]{1,0:T(1,128)S(1)}, u32[]{:S(2)}, u32[]{:S(2)}) collective-permute-start(f32[1,2048]{1,0:T(1,128)S(1)} %get-tuple-element.24.refs_0_), channel_id=1, source_target_pairs={{0,24},{4,28},{8,0},{12,4},{16,8},{20,12},{24,16},{28,20},{1,25},{... | collective-permute-start | bytes 24584 | tf_op jit(solution)/shard_map/ppermute | solution.py:196
  90.4 4.6 %collective-permute-start.26 = (f32[1,2048]{1,0:T(1,128)S(1)}, f32[1,2048]{1,0:T(1,128)S(1)}, u32[]{:S(2)}, u32[]{:S(2)}) collective-permute-start(f32[1,2048]{1,0:T(1,128)S(1)} %get-tuple-element.24.refs_0_), channel_id=1, source_target_pairs={{0,16},{4,20},{8,24},{12,28},{16,0},{20,4},{24,8},{28,12},{1,17},{... | collective-permute-start | bytes 24584 | tf_op jit(solution)/shard_map/ppermute | solution.py:196
  93.1 4.0 %collective-permute-start.25 = (f32[1,2048]{1,0:T(1,128)S(1)}, f32[1,2048]{1,0:T(1,128)S(1)}, u32[]{:S(2)}, u32[]{:S(2)}) collective-permute-start(f32[1,2048]{1,0:T(1,128)S(1)} %get-tuple-element.24.refs_0_), channel_id=1, source_target_pairs={{0,12},{4,16},{8,20},{12,24},{16,28},{20,0},{24,4},{28,8},{1,13},{... | collective-permute-start | bytes 24584 | tf_op jit(solution)/shard_map/ppermute | solution.py:196
  93.1 5.5 %collective-permute-start.24 = (f32[1,2048]{1,0:T(1,128)S(1)}, f32[1,2048]{1,0:T(1,128)S(1)}, u32[]{:S(2)}, u32[]{:S(2)}) collective-permute-start(f32[1,2048]{1,0:T(1,128)S(1)} %get-tuple-element.24.refs_0_), channel_id=1, source_target_pairs={{0,8},{4,12},{8,16},{12,20},{16,24},{20,28},{24,0},{28,4},{1,9},{5... | collective-permute-start | bytes 24584 | tf_op jit(solution)/shard_map/ppermute | solution.py:196
  94.1 4.9 %collective-permute-start.23 = (f32[1,2048]{1,0:T(1,128)S(1)}, f32[1,2048]{1,0:T(1,128)S(1)}, u32[]{:S(2)}, u32[]{:S(2)}) collective-permute-start(f32[1,2048]{1,0:T(1,128)S(1)} %get-tuple-element.24.refs_0_), channel_id=1, source_target_pairs={{0,4},{4,8},{8,12},{12,16},{16,20},{20,24},{24,28},{28,0},{1,5},{5... | collective-permute-start | bytes 24584 | tf_op jit(solution)/shard_map/ppermute | solution.py:196
  107.4 5.6 %collective-permute-start.30 = (f32[17,1024]{1,0:T(8,128)S(1)}, f32[17,1024]{1,0:T(8,128)S(1)}, u32[]{:S(2)}, u32[]{:S(2)}) collective-permute-start(f32[17,1024]{1,0:T(8,128)S(1)} %get-tuple-element.28), channel_id=1, source_target_pairs={{0,1},{1,2},{2,3},{3,0},{4,5},{5,6},{6,7},{7,4},{8,9},{9,10},{10,1... | collective-permute-start | bytes 208904 | tf_op jit(solution)/shard_map/ppermute | solution.py:239
  107.4 5.7 %collective-permute-start.31 = (f32[17,1024]{1,0:T(8,128)S(1)}, f32[17,1024]{1,0:T(8,128)S(1)}, u32[]{:S(2)}, u32[]{:S(2)}) collective-permute-start(f32[17,1024]{1,0:T(8,128)S(1)} %get-tuple-element.29), channel_id=1, source_target_pairs={{0,2},{1,3},{2,0},{3,1},{4,6},{5,7},{6,4},{7,5},{8,10},{9,11},{10,... | collective-permute-start | bytes 208904 | tf_op jit(solution)/shard_map/ppermute | solution.py:239
  108.6 5.2 %collective-permute-start.32 = (f32[17,1024]{1,0:T(8,128)S(1)}, f32[17,1024]{1,0:T(8,128)S(1)}, u32[]{:S(2)}, u32[]{:S(2)}) collective-permute-start(f32[17,1024]{1,0:T(8,128)S(1)} %get-tuple-element.30), channel_id=1, source_target_pairs={{0,3},{1,0},{2,1},{3,2},{4,7},{5,4},{6,5},{7,6},{8,11},{9,8},{10,9... | collective-permute-start | bytes 208904 | tf_op jit(solution)/shard_map/ppermute | solution.py:239
  (15 other events, 168.5 us)

commit v2 on v1

--- a/solution.py
+++ b/solution.py
@@ -35,7 +35,8 @@
     return items[0]
 
 
-def whole_log_sum(parts):
+def whole_log_sum(parts_ref):
+    parts = [parts_ref[t] for t in range(parts_ref.shape[0])]
     top = tree(jnp.maximum, parts)
     return top + jnp.log2(tree(jnp.add, [jnp.exp2(p - top) for p in parts]))
 
@@ -91,9 +92,20 @@
     return jnp.concatenate(out, axis=1)
 
 
-def first_kernel(x_ref, y_ref, pot_ref, s_ref, l_ref, xn_ref, yn_ref, xw, yw, top_ref, sum_ref):
-    k = x_ref.shape[0]
-    x = x_ref[...]
+def repeat(v, out_ref):
+    for t in range(out_ref.shape[0]):
+        out_ref[t] = v
+
+
+def first_kernel(count, me_ref, pot_ref, y_ref, *refs):
+    parts, (s_ref, l_ref, xn_ref, yn_ref, yo_ref, xs, xw, yw, top_ref, sum_ref) = refs[:count], refs[count:]
+    k = y_ref.shape[0]
+    if count == 1:
+        x = parts[0][...]
+    else:
+        for d, part in enumerate(parts):
+            xs[lax.rem(me_ref[0] - d + count, count)] = part[...]
+        x = jnp.concatenate([xs[t] for t in range(count)], axis=0)
     y = y_ref[...]
     xn = jnp.sum(x * x, axis=0, keepdims=True) / k
     yn = jnp.sum(y * y, axis=0, keepdims=True) / k
@@ -104,6 +116,9 @@
     for p, (xp, yp) in enumerate(((x1, y1), (x1, y2), (x2, y1), (x2, y2), (x1, y3), (x3, y1))):
         xw[pl.ds(p * k, k), :] = xp
         yw[pl.ds(p * k, k), :] = yp
+    yo_ref[pl.ds(0, k), :] = y1
+    yo_ref[pl.ds(k, k), :] = y2
+    yo_ref[pl.ds(2 * k, 16), :] = jnp.ones((16, y.shape[1]), BF16)
     step = 256
 
     def block(b, _):
@@ -115,37 +130,30 @@
 
     lax.fori_loop(0, s_ref.shape[0] // step, block, 0)
     pot = (pot_ref[...] - yn) * (1.0 / UNIT)
-    l_ref[...] = rows_log_sum(s_ref, pot, top_ref, sum_ref)
-
-
-def src_kernel(count, s_ref, mass_ref, *refs):
-    parts, (f_ref, l_ref, wide) = refs[:count], refs[count:]
-    f = jnp.log2(mass_ref[...]) - whole_log_sum([p[...] for p in parts])
+    repeat(rows_log_sum(s_ref, pot, top_ref, sum_ref), l_ref)
+
+
+def src_kernel(s_ref, mass_ref, parts_ref, f_ref, l_ref, wide):
+    f = jnp.log2(mass_ref[...]) - whole_log_sum(parts_ref)
     f_ref[...] = f
     across(f, wide)
-    l_ref[...] = cols_log_sum(s_ref, wide)
-
-
-def tgt_kernel(count, s_ref, mass_ref, *refs):
-    parts, (l_ref, top_ref, sum_ref) = refs[:count], refs[count:]
-    g = jnp.log2(mass_ref[...]) - whole_log_sum([p[...] for p in parts])
-    l_ref[...] = rows_log_sum(s_ref, g, top_ref, sum_ref)
-
-
-def last_kernel(count, peers, me_ref, s_ref, mass_ref, f_ref, xn_ref, yn_ref, y_ref, *refs):
-    parts, refs = refs[:count], refs[count:]
-    sp_ref, tp_ref, outs, (wide, yw, acc, flat) = refs[0], refs[1], refs[2 : 2 + peers], refs[2 + peers :]
-    k = y_ref.shape[0]
+    repeat(cols_log_sum(s_ref, wide), l_ref)
+
+
+def tgt_kernel(s_ref, mass_ref, parts_ref, l_ref, top_ref, sum_ref):
+    g = jnp.log2(mass_ref[...]) - whole_log_sum(parts_ref)
+    repeat(rows_log_sum(s_ref, g, top_ref, sum_ref), l_ref)
+
+
+def last_kernel(s_ref, mass_ref, f_ref, xn_ref, yn_ref, yw, parts_ref, sp_ref, tp_ref, out_ref, wide, acc):
     n, width = s_ref.shape
-    g = jnp.log2(mass_ref[...]) - whole_log_sum([p[...] for p in parts])
+    peers, own = out_ref.shape[0], out_ref.shape[1] - 1
+    k = peers * own
+    g = jnp.log2(mass_ref[...]) - whole_log_sum(parts_ref)
     f = f_ref[...]
     sp_ref[...] = f * UNIT + xn_ref[...]
     tp_ref[...] = g * UNIT + yn_ref[...]
     across(f, wide)
-    y1, y2, _ = pieces(y_ref[...])
-    yw[pl.ds(0, k), :] = y1
-    yw[pl.ds(k, k), :] = y2
-    yw[pl.ds(2 * k, 16), :] = jnp.ones((16, width), BF16)
     step = 128
 
     def block(b, _):
@@ -162,21 +170,17 @@
 
     lax.fori_loop(0, n // step, block, 0)
     whole = acc[:, : 2 * k].T
-    num = whole[:k, :] + whole[k:, :]
-    own = k // peers
+    num = (whole[:k, :] + whole[k:, :]) * (k * UNIT / 2.0)
+    den = jnp.broadcast_to(acc[:, 2 * k : 2 * k + 1], (n, LANES)).T[0:1, :]
     for t in range(peers):
-        flat[t] = num[t * own : (t + 1) * own, :]
-    den = jnp.broadcast_to(acc[:, 2 * k : 2 * k + 1], (n, LANES)).T[0:1, :]
-    me = me_ref[0]
-    for d, out in enumerate(outs):
-        out[pl.ds(0, own), :] = flat[lax.rem(me + d, peers)]
-        out[pl.ds(own, 1), :] = den
-
-
-def join_kernel(own, *refs):
-    parts, out_ref = refs[:-1], refs[-1]
-    num = tree(jnp.add, [p[pl.ds(0, own), :] for p in parts])
-    den = tree(jnp.add, [p[pl.ds(own, 1), :] for p in parts])
+        out_ref[t, pl.ds(0, own), :] = num[t * own : (t + 1) * own, :]
+        out_ref[t, pl.ds(own, 1), :] = den
+
+
+def join_kernel(parts_ref, out_ref):
+    peers, own = parts_ref.shape[0], parts_ref.shape[1] - 1
+    num = tree(jnp.add, [parts_ref[t, pl.ds(0, own), :] for t in range(peers)])
+    den = tree(jnp.add, [parts_ref[t, pl.ds(own, 1), :] for t in range(peers)])
     out_ref[...] = num / den
 
 
@@ -184,7 +188,7 @@
     smem = pl.BlockSpec(memory_space=pltpu.SMEM)
     return pl.pallas_call(
         kernel,
-        out_shape=[jax.ShapeDtypeStruct(s, F32) for s in outs],
+        out_shape=[o if isinstance(o, jax.ShapeDtypeStruct) else jax.ShapeDtypeStruct(o, F32) for o in outs],
         in_specs=[smem] * scalars + [VMEM] * (len(args) - scalars),
         out_specs=[VMEM] * len(outs),
         scratch_shapes=scratch,
@@ -192,54 +196,55 @@
     )(*args)
 
 
-def everyone(v, axis, size):
-    return [v] + [lax.ppermute(v, axis, [(i, (i + d) % size) for i in range(size)]) for d in range(1, size)]
+def swap(v, axis):
+    return lax.all_to_all(v, axis, 0, 0, tiled=True)
 
 
 def shards(peers_src, peers_tgt, src_pts, tgt_pts, src_mass, tgt_mass, init_pot):
     own = src_pts.shape[0]
     n, width = src_pts.shape[1], tgt_pts.shape[1]
-    xs = lax.all_gather(src_pts, "tgt", axis=0, tiled=True)
+    if own % 8 == 0:
+        xs = [src_pts] + [
+            lax.ppermute(src_pts, "tgt", [(i, (i + d) % peers_tgt) for i in range(peers_tgt)])
+            for d in range(1, peers_tgt)
+        ]
+    else:
+        xs = [lax.all_gather(src_pts, "tgt", axis=0, tiled=True)]
     ys = lax.all_gather(tgt_pts, "src", axis=0, tiled=True)
-    k = xs.shape[0]
+    k = ys.shape[0]
     src_mass = src_mass.reshape(1, n)
     tgt_mass = tgt_mass.reshape(1, width)
     row, col = (1, n), (1, width)
+    rows, cols = (peers_tgt, 1, n), (peers_src, 1, width)
     lane = pltpu.VMEM((n, LANES), F32)
-    s, l, xn, yn = call(
-        first_kernel,
-        [(n, width), row, row, col],
-        [pltpu.VMEM((6 * k, n), BF16), pltpu.VMEM((6 * k, width), BF16), lane, lane],
-        xs,
+    s, l, xn, yn, yo = call(
+        functools.partial(first_kernel, len(xs)),
+        [(n, width), rows, row, col, jax.ShapeDtypeStruct((2 * k + 16, width), BF16)],
+        [pltpu.VMEM((peers_tgt, own, n), F32), pltpu.VMEM((6 * k, n), BF16), pltpu.VMEM((6 * k, width), BF16), lane, lane],
+        lax.axis_index("tgt").astype(jnp.int32).reshape(1),
+        init_pot.reshape(1, width),
         ys,
-        init_pot.reshape(1, width),
+        *xs,
+        scalars=1,
     )
     for step in range(ITERS):
-        parts = everyone(l, "tgt", peers_tgt)
-        f, l = call(functools.partial(src_kernel, len(parts)), [row, col], [lane], s, src_mass, *parts)
-        parts = everyone(l, "src", peers_src)
+        f, l = call(src_kernel, [row, cols], [lane], s, src_mass, swap(l, "tgt"))
+        l = swap(l, "src")
         if step < ITERS - 1:
-            (l,) = call(functools.partial(tgt_kernel, len(parts)), [row], [lane, lane], s, tgt_mass, *parts)
-    me = lax.axis_index("tgt").astype(jnp.int32).reshape(1)
-    src_pot, tgt_pot, *blocks = call(
-        functools.partial(last_kernel, len(parts), peers_tgt),
-        [row, col] + [(own + 1, n)] * peers_tgt,
-        [lane, pltpu.VMEM((2 * k + 16, width), BF16), pltpu.VMEM((n, 2 * k + 16), F32), pltpu.VMEM((peers_tgt, own, n), F32)],
-        me,
+            (l,) = call(tgt_kernel, [rows], [lane, lane], s, tgt_mass, l)
+    src_pot, tgt_pot, blocks = call(
+        last_kernel,
+        [row, col, (peers_tgt, own + 1, n)],
+        [lane, pltpu.VMEM((n, 2 * k + 16), F32)],
         s,
         tgt_mass,
         f,
         xn,
         yn,
-        ys,
-        *parts,
-        scalars=1,
+        yo,
+        l,
     )
-    came = [blocks[0]] + [
-        lax.ppermute(blocks[d], "tgt", [(i, (i + d) % peers_tgt) for i in range(peers_tgt)])
-        for d in range(1, peers_tgt)
-    ]
-    (mapped,) = call(functools.partial(join_kernel, own), [(own, n)], [], *came)
+    (mapped,) = call(join_kernel, [(own, n)], [], swap(blocks, "tgt"))
     return src_pot.reshape(n), tgt_pot.reshape(width), mapped
 
 

time: 115 us -> 108 us (0.939)
  blocking collectives: 26.3 us -> 73.1 us
  waiting for transfers between devices: 26.8 us -> 0.01 us
  starting transfers between devices: 30.4 us -> 5.96 us
  local copies, waits for them, and re-layouts: 4.78 us -> 2.23 us
    all_to_all x0 -> x7, blocking collectives: none -> 57.8 us  [swap(): return lax.all_to_all(v, axis, 0, 0, tiled=True)]
    ppermute x33 -> x3, waiting for transfers between devices: 26.8 us -> 0.01 us  [shards(): lax.ppermute(src_pts, 'tgt', [(i, (i + d) % peers_tgt) for i in range(pee...]
    ppermute x33 -> x3, starting transfers between devices: 30.4 us -> 5.96 us  [shards(): lax.ppermute(src_pts, 'tgt', [(i, (i + d) % peers_tgt) for i in range(pee...]
    all_gather x1 -> x0, blocking collectives: 10.7 us -> none  [shards(): xs = lax.all_gather(src_pts, 'tgt', axis=0, tiled=True)]
    unnamed x12 -> x10, local copies, waits for them, and re-layouts: 4.78 us -> 2.23 us
  transfers between devices with their start and end apart: 33 -> 3, of which waited for: 22 -> 0; matrix products, arithmetic and copies ran while one was open for 0% -> 0% of each run, Pallas kernels for 0% -> 0%
where the time goes in v2:
time: 108 us; the launch traced here: 107 us
  blocking collectives  73.1 us (68%)
  Pallas kernels  25.3 us (23%)
  starting transfers between devices  5.96 us (6%)
  local copies, waits for them, and re-layouts  2.23 us (2%)
    all_to_all x7, blocking collectives, swap(): return lax.all_to_all(v, axis, 0, 0, tiled=True)  57.8 us
    pallas_call x8, Pallas kernels, call(): pl.pallas_call(kernel, out_shape=[o if isinstance(o, jax.ShapeDtypeStruct...  25.3 us
    all_gather x1, blocking collectives, shards(): ys = lax.all_gather(tgt_pts, 'src', axis=0, tiled=True)  15.3 us
    ppermute x3, starting transfers between devices, shards(): lax.ppermute(src_pts, 'tgt', [(i, (i + d) % peers_tgt) for i in range(pee...  5.96 us
    unnamed x10, local copies, waits for them, and re-layouts  2.23 us
  transfers between devices with their start and end apart: 3, of which 0 were waited for; matrix products, arithmetic and copies ran while one was open for 0% of the time, Pallas kernels for 0%

profile of v2, /device:TPU:0, one launch (start us, length us, event | category | flops | bytes accessed | tf_op | source)
XLA Modules:
  0.0 107.2 jit_solution(13787991391312220779)
XLA Ops:
  0.6 3.0 %collective-permute-start.1 = (f32[16,1024]{1,0:T(8,128)}, f32[16,1024]{1,0:T(8,128)S(1)}, u32[]{:S(2)}, u32[]{:S(2)}) collective-permute-start(f32[16,1024]{1,0:T(8,128)} %refs_0_.1), channel_id=1, source_target_pairs={{0,2},{1,3},{2,0},{3,1},{4,6},{5,7},{6,4},{7,5},{8,10},{9,11},{10,... | collective-permute-start | bytes 196616 | tf_op jit(solution)/shard_map/ppermute | solution.py:208
  3.7 1.5 %collective-permute-start = (f32[16,1024]{1,0:T(8,128)}, f32[16,1024]{1,0:T(8,128)S(1)}, u32[]{:S(2)}, u32[]{:S(2)}) collective-permute-start(f32[16,1024]{1,0:T(8,128)} %refs_0_.1), channel_id=1, source_target_pairs={{0,1},{1,2},{2,3},{3,0},{4,5},{5,6},{6,7},{7,4},{8,9},{9,10},{10,1... | collective-permute-start | bytes 196616 | tf_op jit(solution)/shard_map/ppermute | solution.py:208
  5.2 1.4 %collective-permute-start.2 = (f32[16,1024]{1,0:T(8,128)}, f32[16,1024]{1,0:T(8,128)S(1)}, u32[]{:S(2)}, u32[]{:S(2)}) collective-permute-start(f32[16,1024]{1,0:T(8,128)} %refs_0_.1), channel_id=1, source_target_pairs={{0,3},{1,0},{2,1},{3,2},{4,7},{5,4},{6,5},{7,6},{8,11},{9,8},{10,9... | collective-permute-start | bytes 196616 | tf_op jit(solution)/shard_map/ppermute | solution.py:208
  6.6 15.3 %all_gather.3.y_ref = f32[64,2048]{1,0:T(8,128)S(1)} all-gather(f32[8,2048]{1,0:T(8,128)} %param.6), channel_id=1, replica_groups=mesh['src'=8,'tgt'=4] {'src'}, dimensions={0}, use_global_device_ids=true | all-gather | bytes 589824 | tf_op jit(solution)/shard_map/all_gather | solution.py:213
  21.9 0.0 collective-permute-done.refs_1_
  21.9 0.0 copy-start.1
  21.9 0.8 copy-done.1
  22.7 0.7 copy-done.4
  23.4 6.0 %shard_map.76 = (f32[1024,2048]{1,0:T(8,128)S(1)}, f32[4,1,1024]{2,1,0:T(1,128)S(1)}, f32[1,1024]{1,0:T(1,128)S(1)}, f32[1,2048]{1,0:T(1,128)S(1)}, bf16[144,2048]{1,0:T(8,128)(2,1)S(1)}) custom-call(s32[1]{0:T(128)} %bitcast.me_ref, f32[1,2048]{1,0:T(1,128)S(1)} %bitcast.12, f32[64,2048]{1,0:T(8,128)S(1)} %all_gather.3.y_ref, f32[16,1024]{1,0:T(8,128)S(1)} %copy-done.1, ...), custom_call_target="tpu_custom_call" | custom-call | tf_op jit(solution)/shard_map/pallas_call | solution.py:189
  29.4 7.1 %all_to_all.35.parts_ref = f32[4,1,1024]{2,1,0:T(1,128)S(1)} all-to-all(f32[4,1,1024]{2,1,0:T(1,128)S(1)} %get-tuple-element.16), channel_id=1, replica_groups=mesh['src'=8,'tgt'=4] {'tgt'}, dimensions={0} | all-to-all | bytes 32768 | tf_op jit(solution)/shard_map/all_to_all | solution.py:200
  36.5 0.7 copy-done.2
  37.1 3.1 %shard_map.77 = (f32[1,1024]{1,0:T(1,128)}, f32[8,1,2048]{2,1,0:T(1,128)S(1)}) custom-call(f32[1024,2048]{1,0:T(8,128)S(1)} %get-tuple-element.15.s_ref, f32[1,1024]{1,0:T(1,128)S(1)} %bitcast.9, f32[4,1,1024]{2,1,0:T(1,128)S(1)} %all_to_all.35.parts_ref), custom_call_target="tpu_custom_call" | custom-call | tf_op jit(solution)/shard_map/pallas_call | solution.py:189
  40.3 10.4 %all_to_all.36.parts_ref = f32[8,1,2048]{2,1,0:T(1,128)S(1)} all-to-all(f32[8,1,2048]{2,1,0:T(1,128)S(1)} %get-tuple-element.17), channel_id=1, replica_groups=mesh['src'=8,'tgt'=4] {'src'}, dimensions={0} | all-to-all | bytes 131072 | tf_op jit(solution)/shard_map/all_to_all | solution.py:200
  50.7 2.5 %shard_map.78 = f32[4,1,1024]{2,1,0:T(1,128)S(1)} custom-call(f32[1024,2048]{1,0:T(8,128)S(1)} %get-tuple-element.15.s_ref, f32[1,2048]{1,0:T(1,128)S(1)} %bitcast.6, f32[8,1,2048]{2,1,0:T(1,128)S(1)} %all_to_all.36.parts_ref), custom_call_target="tpu_custom_call" | custom-call | tf_op jit(solution)/shard_map/pallas_call | solution.py:189
  53.2 7.1 %all_to_all.37.parts_ref = f32[4,1,1024]{2,1,0:T(1,128)S(1)} all-to-all(f32[4,1,1024]{2,1,0:T(1,128)S(1)} %shard_map.78), channel_id=1, replica_groups=mesh['src'=8,'tgt'=4] {'tgt'}, dimensions={0} | all-to-all | bytes 32768 | tf_op jit(solution)/shard_map/all_to_all | solution.py:200
  60.3 3.1 %shard_map.79 = (f32[1,1024]{1,0:T(1,128)}, f32[8,1,2048]{2,1,0:T(1,128)S(1)}) custom-call(f32[1024,2048]{1,0:T(8,128)S(1)} %get-tuple-element.15.s_ref, f32[1,1024]{1,0:T(1,128)S(1)} %bitcast.10, f32[4,1,1024]{2,1,0:T(1,128)S(1)} %all_to_all.37.parts_ref), custom_call_target="tpu_custom_call" | custom-call | tf_op jit(solution)/shard_map/pallas_call | solution.py:189
  63.4 8.3 %all_to_all.38.parts_ref = f32[8,1,2048]{2,1,0:T(1,128)S(1)} all-to-all(f32[8,1,2048]{2,1,0:T(1,128)S(1)} %get-tuple-element.18), channel_id=1, replica_groups=mesh['src'=8,'tgt'=4] {'src'}, dimensions={0} | all-to-all | bytes 131072 | tf_op jit(solution)/shard_map/all_to_all | solution.py:200
  71.7 2.5 %shard_map.80 = f32[4,1,1024]{2,1,0:T(1,128)S(1)} custom-call(f32[1024,2048]{1,0:T(8,128)S(1)} %get-tuple-element.15.s_ref, f32[1,2048]{1,0:T(1,128)S(1)} %bitcast.7, f32[8,1,2048]{2,1,0:T(1,128)S(1)} %all_to_all.38.parts_ref), custom_call_target="tpu_custom_call" | custom-call | tf_op jit(solution)/shard_map/pallas_call | solution.py:189
  74.2 7.1 %all_to_all.39.parts_ref = f32[4,1,1024]{2,1,0:T(1,128)S(1)} all-to-all(f32[4,1,1024]{2,1,0:T(1,128)S(1)} %shard_map.80), channel_id=1, replica_groups=mesh['src'=8,'tgt'=4] {'tgt'}, dimensions={0} | all-to-all | bytes 32768 | tf_op jit(solution)/shard_map/all_to_all | solution.py:200
  81.3 2.6 %shard_map.81 = (f32[1,1024]{1,0:T(1,128)S(1)}, f32[8,1,2048]{2,1,0:T(1,128)S(1)}) custom-call(f32[1024,2048]{1,0:T(8,128)S(1)} %get-tuple-element.15.s_ref, f32[1,1024]{1,0:T(1,128)S(1)} %bitcast.11, f32[4,1,1024]{2,1,0:T(1,128)S(1)} %all_to_all.39.parts_ref), custom_call_target="tpu_custom_call" | custom-call | tf_op jit(solution)/shard_map/pallas_call | solution.py:189
  83.9 8.3 %all_to_all.40.parts_ref = f32[8,1,2048]{2,1,0:T(1,128)S(1)} all-to-all(f32[8,1,2048]{2,1,0:T(1,128)S(1)} %get-tuple-element.23), channel_id=1, replica_groups=mesh['src'=8,'tgt'=4] {'src'}, dimensions={0} | all-to-all | bytes 131072 | tf_op jit(solution)/shard_map/all_to_all | solution.py:200
  92.2 4.8 %shard_map.82 = (f32[1,1024]{1,0:T(1,128)}, f32[1,2048]{1,0:T(1,128)}, f32[4,17,1024]{2,1,0:T(8,128)S(1)}) custom-call(f32[1024,2048]{1,0:T(8,128)S(1)} %get-tuple-element.15.s_ref, f32[1,2048]{1,0:T(1,128)S(1)} %bitcast.8, f32[1,1024]{1,0:T(1,128)S(1)} %get-tuple-element.19.f_ref, f32[1,1024]{1,0:T(1,128)S(1)} %get-tuple-element.20.xn_ref, ...), custom_call_target="tpu_custom_call" | custom-call | tf_op jit(solution)/shard_map/pallas_call | solution.py:189
  96.9 9.6 %all_to_all.41.parts_ref = f32[4,17,1024]{2,1,0:T(8,128)S(1)} all-to-all(f32[4,17,1024]{2,1,0:T(8,128)S(1)} %get-tuple-element.26), channel_id=1, replica_groups=mesh['src'=8,'tgt'=4] {'tgt'}, dimensions={0} | all-to-all | bytes 557056 | tf_op jit(solution)/shard_map/all_to_all | solution.py:200
  106.6 0.7 shard_map.83
  (8 shorter events, 0.0 us)
Async XLA Ops:
  0.6 50.0 %copy-start = (f32[2048]{0:T(1024)S(1)}, f32[2048]{0:T(1024)}, u32[]{:S(2)}) copy-start(f32[2048]{0:T(1024)} %param.8) | copy-start | bytes 24580
  0.6 21.2 %collective-permute-start.1 = (f32[16,1024]{1,0:T(8,128)}, f32[16,1024]{1,0:T(8,128)S(1)}, u32[]{:S(2)}, u32[]{:S(2)}) collective-permute-start(f32[16,1024]{1,0:T(8,128)} %refs_0_.1), channel_id=1, source_target_pairs={{0,2},{1,3},{2,0},{3,1},{4,6},{5,7},{6,4},{7,5},{8,10},{9,11},{10,... | collective-permute-start | bytes 196616 | tf_op jit(solution)/shard_map/ppermute | solution.py:208
  3.7 18.2 %collective-permute-start = (f32[16,1024]{1,0:T(8,128)}, f32[16,1024]{1,0:T(8,128)S(1)}, u32[]{:S(2)}, u32[]{:S(2)}) collective-permute-start(f32[16,1024]{1,0:T(8,128)} %refs_0_.1), channel_id=1, source_target_pairs={{0,1},{1,2},{2,3},{3,0},{4,5},{5,6},{6,7},{7,4},{8,9},{9,10},{10,1... | collective-permute-start | bytes 196616 | tf_op jit(solution)/shard_map/ppermute | solution.py:208
  5.2 16.7 %collective-permute-start.2 = (f32[16,1024]{1,0:T(8,128)}, f32[16,1024]{1,0:T(8,128)S(1)}, u32[]{:S(2)}, u32[]{:S(2)}) collective-permute-start(f32[16,1024]{1,0:T(8,128)} %refs_0_.1), channel_id=1, source_target_pairs={{0,3},{1,0},{2,1},{3,2},{4,7},{5,4},{6,5},{7,6},{8,11},{9,8},{10,9... | collective-permute-start | bytes 196616 | tf_op jit(solution)/shard_map/ppermute | solution.py:208
  21.9 0.8 copy-start.1
  22.7 0.7 copy-start.4
  36.5 0.7 copy-start.2
  60.3 21.0 %copy-start.3 = (f32[1024]{0:T(1024)S(1)}, f32[1024]{0:T(1024)}, u32[]{:S(2)}) copy-start(f32[1024]{0:T(1024)} %param.7) | copy-start | bytes 12292

commit v3 on v2

--- a/solution.py
+++ b/solution.py
@@ -92,21 +92,23 @@
     return jnp.concatenate(out, axis=1)
 
 
-def repeat(v, out_ref):
-    for t in range(out_ref.shape[0]):
-        out_ref[t] = v
-
-
-def first_kernel(count, me_ref, pot_ref, y_ref, *refs):
-    parts, (s_ref, l_ref, xn_ref, yn_ref, yo_ref, xs, xw, yw, top_ref, sum_ref) = refs[:count], refs[count:]
-    k = y_ref.shape[0]
-    if count == 1:
-        x = parts[0][...]
-    else:
-        for d, part in enumerate(parts):
-            xs[lax.rem(me_ref[0] - d + count, count)] = part[...]
-        x = jnp.concatenate([xs[t] for t in range(count)], axis=0)
-    y = y_ref[...]
+def first_kernel(peers_tgt, xplan, yplan, me_ref, pot_ref, *refs):
+    xcount = len(xplan)
+    xparts, refs = refs[:xcount], refs[xcount:]
+    yparts, (s_ref, l_ref, xn_ref, yn_ref, yo_ref, xs, ys, xw, yw, top_ref, sum_ref) = refs[:-11], refs[-11:]
+    k = xs.shape[0]
+    me_src, me_tgt = me_ref[0] // peers_tgt, lax.rem(me_ref[0], peers_tgt)
+    for parts, plan, me, all_ref in ((xparts, xplan, me_tgt, xs), (yparts, yplan, me_src, ys)):
+        for part, owners in zip(parts, plan):
+            if owners is None:
+                all_ref[...] = part[...]
+                continue
+            own = part.shape[0] // len(owners)
+            for b, d in enumerate(owners):
+                rows = pl.ds(pl.multiple_of((me ^ d) * own, 8), own)
+                all_ref[rows, :] = part[pl.ds(b * own, own), :]
+    x = xs[...]
+    y = ys[...]
     xn = jnp.sum(x * x, axis=0, keepdims=True) / k
     yn = jnp.sum(y * y, axis=0, keepdims=True) / k
     xn_ref[...] = xn
@@ -130,24 +132,25 @@
 
     lax.fori_loop(0, s_ref.shape[0] // step, block, 0)
     pot = (pot_ref[...] - yn) * (1.0 / UNIT)
-    repeat(rows_log_sum(s_ref, pot, top_ref, sum_ref), l_ref)
+    l_ref[...] = rows_log_sum(s_ref, pot, top_ref, sum_ref)
 
 
 def src_kernel(s_ref, mass_ref, parts_ref, f_ref, l_ref, wide):
     f = jnp.log2(mass_ref[...]) - whole_log_sum(parts_ref)
     f_ref[...] = f
     across(f, wide)
-    repeat(cols_log_sum(s_ref, wide), l_ref)
+    l_ref[...] = cols_log_sum(s_ref, wide)
 
 
 def tgt_kernel(s_ref, mass_ref, parts_ref, l_ref, top_ref, sum_ref):
     g = jnp.log2(mass_ref[...]) - whole_log_sum(parts_ref)
-    repeat(rows_log_sum(s_ref, g, top_ref, sum_ref), l_ref)
-
-
-def last_kernel(s_ref, mass_ref, f_ref, xn_ref, yn_ref, yw, parts_ref, sp_ref, tp_ref, out_ref, wide, acc):
+    l_ref[...] = rows_log_sum(s_ref, g, top_ref, sum_ref)
+
+
+def last_kernel(me_ref, s_ref, mass_ref, f_ref, xn_ref, yn_ref, yw, parts_ref, sp_ref, tp_ref, *refs):
+    outs, (wide, acc, flat) = refs[:-3], refs[-3:]
     n, width = s_ref.shape
-    peers, own = out_ref.shape[0], out_ref.shape[1] - 1
+    peers, own = len(outs), outs[0].shape[0] - 1
     k = peers * own
     g = jnp.log2(mass_ref[...]) - whole_log_sum(parts_ref)
     f = f_ref[...]
@@ -173,14 +176,17 @@
     num = (whole[:k, :] + whole[k:, :]) * (k * UNIT / 2.0)
     den = jnp.broadcast_to(acc[:, 2 * k : 2 * k + 1], (n, LANES)).T[0:1, :]
     for t in range(peers):
-        out_ref[t, pl.ds(0, own), :] = num[t * own : (t + 1) * own, :]
-        out_ref[t, pl.ds(own, 1), :] = den
-
-
-def join_kernel(parts_ref, out_ref):
-    peers, own = parts_ref.shape[0], parts_ref.shape[1] - 1
-    num = tree(jnp.add, [parts_ref[t, pl.ds(0, own), :] for t in range(peers)])
-    den = tree(jnp.add, [parts_ref[t, pl.ds(own, 1), :] for t in range(peers)])
+        flat[t] = num[t * own : (t + 1) * own, :]
+    for d, out in enumerate(outs):
+        out[pl.ds(0, own), :] = flat[lax.rem(me_ref[0], peers) ^ d]
+        out[pl.ds(own, 1), :] = den
+
+
+def join_kernel(*refs):
+    parts, out_ref = refs[:-1], refs[-1]
+    own = out_ref.shape[0]
+    num = tree(jnp.add, [p[pl.ds(0, own), :] for p in parts])
+    den = tree(jnp.add, [p[pl.ds(own, 1), :] for p in parts])
     out_ref[...] = num / den
 
 
@@ -196,46 +202,64 @@
     )(*args)
 
 
-def swap(v, axis):
-    return lax.all_to_all(v, axis, 0, 0, tiled=True)
+def everyone(v, axis):
+    return lax.all_gather(v, axis, axis=0, tiled=False)
+
+
+def flip(v, axis, size, bit):
+    return lax.ppermute(v, axis, [(i, i ^ bit) for i in range(size)])
+
+
+def gather(v, axis, size, pair):
+    if v.shape[0] % 8 or size & (size - 1):
+        return [lax.all_gather(v, axis, axis=0, tiled=True)], [None]
+    step = 2 if pair else 1
+    blocks = [v] + [flip(v, axis, size, d) for d in range(step, size, step)]
+    order = list(range(0, size, step))
+    if not pair:
+        return blocks, [[d] for d in order]
+    mine = jnp.concatenate(blocks, axis=0)
+    return [mine, flip(mine, axis, size, 1)], [order, [d + 1 for d in order]]
 
 
 def shards(peers_src, peers_tgt, src_pts, tgt_pts, src_mass, tgt_mass, init_pot):
     own = src_pts.shape[0]
     n, width = src_pts.shape[1], tgt_pts.shape[1]
-    if own % 8 == 0:
-        xs = [src_pts] + [
-            lax.ppermute(src_pts, "tgt", [(i, (i + d) % peers_tgt) for i in range(peers_tgt)])
-            for d in range(1, peers_tgt)
-        ]
-    else:
-        xs = [lax.all_gather(src_pts, "tgt", axis=0, tiled=True)]
-    ys = lax.all_gather(tgt_pts, "src", axis=0, tiled=True)
-    k = ys.shape[0]
+    ys, yplan = gather(tgt_pts, "src", peers_src, True)
+    xs, xplan = gather(src_pts, "tgt", peers_tgt, False)
+    k = own * peers_tgt
+    me = lax.axis_index(("src", "tgt")).astype(jnp.int32).reshape(1)
     src_mass = src_mass.reshape(1, n)
     tgt_mass = tgt_mass.reshape(1, width)
     row, col = (1, n), (1, width)
-    rows, cols = (peers_tgt, 1, n), (peers_src, 1, width)
     lane = pltpu.VMEM((n, LANES), F32)
     s, l, xn, yn, yo = call(
-        functools.partial(first_kernel, len(xs)),
-        [(n, width), rows, row, col, jax.ShapeDtypeStruct((2 * k + 16, width), BF16)],
-        [pltpu.VMEM((peers_tgt, own, n), F32), pltpu.VMEM((6 * k, n), BF16), pltpu.VMEM((6 * k, width), BF16), lane, lane],
-        lax.axis_index("tgt").astype(jnp.int32).reshape(1),
+        functools.partial(first_kernel, peers_tgt, xplan, yplan),
+        [(n, width), row, row, col, jax.ShapeDtypeStruct((2 * k + 16, width), BF16)],
+        [
+            pltpu.VMEM((k, n), F32),
+            pltpu.VMEM((k, width), F32),
+            pltpu.VMEM((6 * k, n), BF16),
+            pltpu.VMEM((6 * k, width), BF16),
+            lane,
+            lane,
+        ],
+        me,
         init_pot.reshape(1, width),
-        ys,
         *xs,
+        *ys,
         scalars=1,
     )
     for step in range(ITERS):
-        f, l = call(src_kernel, [row, cols], [lane], s, src_mass, swap(l, "tgt"))
-        l = swap(l, "src")
+        f, l = call(src_kernel, [row, col], [lane], s, src_mass, everyone(l, "tgt"))
+        l = everyone(l, "src")
         if step < ITERS - 1:
-            (l,) = call(tgt_kernel, [rows], [lane, lane], s, tgt_mass, l)
-    src_pot, tgt_pot, blocks = call(
+            (l,) = call(tgt_kernel, [row], [lane, lane], s, tgt_mass, l)
+    src_pot, tgt_pot, *blocks = call(
         last_kernel,
-        [row, col, (peers_tgt, own + 1, n)],
-        [lane, pltpu.VMEM((n, 2 * k + 16), F32)],
+        [row, col] + [(own + 1, n)] * peers_tgt,
+        [lane, pltpu.VMEM((n, 2 * k + 16), F32), pltpu.VMEM((peers_tgt, own, n), F32)],
+        me,
         s,
         tgt_mass,
         f,
@@ -243,8 +267,10 @@
         yn,
         yo,
         l,
+        scalars=1,
     )
-    (mapped,) = call(join_kernel, [(own, n)], [], swap(blocks, "tgt"))
+    came = [blocks[0]] + [flip(blocks[d], "tgt", peers_tgt, d) for d in range(1, peers_tgt)]
+    (mapped,) = call(join_kernel, [(own, n)], [], *came)
     return src_pot.reshape(n), tgt_pot.reshape(width), mapped
 
 

time: 108 us -> 122 us (1.13)
  waiting for transfers between devices: 0.01 us -> 15.1 us
  blocking collectives: 73.1 us -> 64.4 us
  starting transfers between devices: 5.96 us -> 12.7 us
    all_to_all x7 -> x0, blocking collectives: 57.8 us -> none  [swap(): return lax.all_to_all(v, axis, 0, 0, tiled=True)]
    all_gather x1 -> x6, blocking collectives: 15.3 us -> 64.4 us  [everyone(): return lax.all_gather(v, axis, axis=0, tiled=False)]
    ppermute x3 -> x10, waiting for transfers between devices: 0.01 us -> 15.1 us  [flip(): return lax.ppermute(v, axis, [(i, i ^ bit) for i in range(size)])]
    ppermute x3 -> x10, starting transfers between devices: 5.96 us -> 12.7 us  [flip(): return lax.ppermute(v, axis, [(i, i ^ bit) for i in range(size)])]
    unnamed x10 -> x11, local copies, waits for them, and re-layouts: 2.23 us -> 3.15 us
  transfers between devices with their start and end apart: 3 -> 10, of which waited for: 0 -> 7; matrix products, arithmetic and copies ran while one was open for 0% -> 1% of each run, Pallas kernels for 0% -> 0%
where the time goes in v3:
time: 122 us
  blocking collectives  64.4 us (53%)
  Pallas kernels  25.5 us (21%)
  waiting for transfers between devices  15.1 us (12%)
  starting transfers between devices  12.7 us (10%)
  local copies, waits for them, and re-layouts  3.16 us (3%)
    all_gather x6, blocking collectives, everyone(): return lax.all_gather(v, axis, axis=0, tiled=False)  64.4 us
    pallas_call x8, Pallas kernels, call(): pl.pallas_call(kernel, out_shape=[o if isinstance(o, jax.ShapeDtypeStruct...  25.5 us
    ppermute x10, waiting for transfers between devices, flip(): return lax.ppermute(v, axis, [(i, i ^ bit) for i in range(size)])  15.1 us
    ppermute x10, starting transfers between devices, flip(): return lax.ppermute(v, axis, [(i, i ^ bit) for i in range(size)])  12.7 us
    unnamed x11, local copies, waits for them, and re-layouts  3.15 us
  transfers between devices with their start and end apart: 10, of which 7 were waited for; matrix products, arithmetic and copies ran while one was open for 1% of the time, Pallas kernels for 0%

profile of v3, /device:TPU:0, one launch (start us, length us, event | category | flops | bytes accessed | tf_op | source)
XLA Modules:
  0.0 121.5 jit_solution(13243685346914870826)
XLA Ops:
  0.6 4.1 %collective-permute-start.4 = (f32[8,2048]{1,0:T(8,128)}, f32[8,2048]{1,0:T(8,128)S(1)}, u32[]{:S(2)}, u32[]{:S(2)}) collective-permute-start(f32[8,2048]{1,0:T(8,128)} %param.6), channel_id=1, source_target_pairs={{0,16},{4,20},{8,24},{12,28},{16,0},{20,4},{24,8},{28,12},{1,17},{... | collective-permute-start | bytes 196616 | tf_op jit(solution)/shard_map/ppermute | solution.py:210
  4.7 1.6 %collective-permute-start.3 = (f32[8,2048]{1,0:T(8,128)}, f32[8,2048]{1,0:T(8,128)S(1)}, u32[]{:S(2)}, u32[]{:S(2)}) collective-permute-start(f32[8,2048]{1,0:T(8,128)} %param.6), channel_id=1, source_target_pairs={{0,8},{4,12},{8,0},{12,4},{16,24},{20,28},{24,16},{28,20},{1,9},{5... | collective-permute-start | bytes 196616 | tf_op jit(solution)/shard_map/ppermute | solution.py:210
  7.2 2.0 %collective-permute-done.3 = f32[8,2048]{1,0:T(8,128)S(1)} collective-permute-done((f32[8,2048]{1,0:T(8,128)}, f32[8,2048]{1,0:T(8,128)S(1)}, u32[]{:S(2)}, u32[]{:S(2)}) %collective-permute-start.3) | collective-permute-done | bytes 65568 | tf_op jit(solution)/shard_map/ppermute | solution.py:210
  9.2 3.3 %collective-permute-done.5 = f32[8,2048]{1,0:T(8,128)S(1)} collective-permute-done((f32[8,2048]{1,0:T(8,128)}, f32[8,2048]{1,0:T(8,128)S(1)}, u32[]{:S(2)}, u32[]{:S(2)}) %collective-permute-start.5) | collective-permute-done | bytes 65568 | tf_op jit(solution)/shard_map/ppermute | solution.py:210
  12.6 1.6 %collective-permute-start.1 = (f32[16,1024]{1,0:T(8,128)}, f32[16,1024]{1,0:T(8,128)S(1)}, u32[]{:S(2)}, u32[]{:S(2)}) collective-permute-start(f32[16,1024]{1,0:T(8,128)} %refs_0_.1), channel_id=1, source_target_pairs={{0,2},{1,3},{2,0},{3,1},{4,6},{5,7},{6,4},{7,5},{8,10},{9,11},{10,... | collective-permute-start | bytes 196616 | tf_op jit(solution)/shard_map/ppermute | solution.py:210
  14.2 1.5 %collective-permute-start = (f32[16,1024]{1,0:T(8,128)}, f32[16,1024]{1,0:T(8,128)S(1)}, u32[]{:S(2)}, u32[]{:S(2)}) collective-permute-start(f32[16,1024]{1,0:T(8,128)} %refs_0_.1), channel_id=1, source_target_pairs={{0,1},{1,0},{2,3},{3,2},{4,5},{5,4},{6,7},{7,6},{8,9},{9,8},{10,11... | collective-permute-start | bytes 196616 | tf_op jit(solution)/shard_map/ppermute | solution.py:210
  17.3 1.7 %collective-permute-done.refs_1_ = f32[16,1024]{1,0:T(8,128)S(1)} collective-permute-done((f32[16,1024]{1,0:T(8,128)}, f32[16,1024]{1,0:T(8,128)S(1)}, u32[]{:S(2)}, u32[]{:S(2)}) %collective-permute-start) | collective-permute-done | bytes 65568 | tf_op jit(solution)/shard_map/ppermute | solution.py:210
  19.0 2.0 %collective-permute-done.2.refs_3_ = f32[16,1024]{1,0:T(8,128)S(1)} collective-permute-done((f32[16,1024]{1,0:T(8,128)}, f32[16,1024]{1,0:T(8,128)S(1)}, u32[]{:S(2)}, u32[]{:S(2)}) %collective-permute-start.2) | collective-permute-done | bytes 65568 | tf_op jit(solution)/shard_map/ppermute | solution.py:210
  22.6 6.0 %shard_map.76 = (f32[1024,2048]{1,0:T(8,128)S(1)}, f32[1,1024]{1,0:T(1,128)S(1)}, f32[1,1024]{1,0:T(1,128)S(1)}, f32[1,2048]{1,0:T(1,128)S(1)}, bf16[144,2048]{1,0:T(8,128)(2,1)S(1)}) custom-call(s32[1]{0:T(128)} %bitcast.me_ref, f32[1,2048]{1,0:T(1,128)S(1)} %bitcast.20, f32[16,1024]{1,0:T(8,128)S(1)} %copy-done.1, ...), custom_call_target="tpu_custom_call" | custom-call | tf_op jit(solution)/shard_map/pallas_call | solution.py:195
  28.6 7.2 %all-gather.6.parts_ref = f32[4,1,1024]{2,1,0:T(1,128)S(1)} all-gather(f32[1,1,1024]{2,1,0:T(1,128)S(1)} %bitcast.24), channel_id=2, replica_groups=mesh['src'=8,'tgt'=4] {'tgt'}, dimensions={0}, use_global_device_ids=true | all-gather | bytes 20480 | tf_op jit(solution)/shard_map/all_gather | solution.py:206
  36.5 3.0 %shard_map.77 = (f32[1,1024]{1,0:T(1,128)}, f32[1,2048]{1,0:T(1,128)S(1)}) custom-call(f32[1024,2048]{1,0:T(8,128)S(1)} %get-tuple-element.18.s_ref, f32[1,1024]{1,0:T(1,128)S(1)} %bitcast.15, f32[4,1,1024]{2,1,0:T(1,128)S(1)} %all-gather.6.parts_ref), custom_call_target="tpu_custom_call" | custom-call | tf_op jit(solution)/shard_map/pallas_call | solution.py:195
  39.5 14.0 %all-gather.7.parts_ref = f32[8,1,2048]{2,1,0:T(1,128)S(1)} all-gather(f32[1,1,2048]{2,1,0:T(1,128)S(1)} %bitcast.21), channel_id=3, replica_groups=mesh['src'=8,'tgt'=4] {'src'}, dimensions={0}, use_global_device_ids=true | all-gather | bytes 73728 | tf_op jit(solution)/shard_map/all_gather | solution.py:206
  53.5 2.5 %shard_map.78 = f32[1,1024]{1,0:T(1,128)S(1)} custom-call(f32[1024,2048]{1,0:T(8,128)S(1)} %get-tuple-element.18.s_ref, f32[1,2048]{1,0:T(1,128)S(1)} %bitcast.12, f32[8,1,2048]{2,1,0:T(1,128)S(1)} %all-gather.7.parts_ref), custom_call_target="tpu_custom_call" | custom-call | tf_op jit(solution)/shard_map/pallas_call | solution.py:195
  56.0 8.1 %all-gather.8.parts_ref = f32[4,1,1024]{2,1,0:T(1,128)S(1)} all-gather(f32[1,1,1024]{2,1,0:T(1,128)S(1)} %bitcast.18), channel_id=4, replica_groups=mesh['src'=8,'tgt'=4] {'tgt'}, dimensions={0}, use_global_device_ids=true | all-gather | bytes 20480 | tf_op jit(solution)/shard_map/all_gather | solution.py:206
  64.2 3.0 %shard_map.79 = (f32[1,1024]{1,0:T(1,128)}, f32[1,2048]{1,0:T(1,128)S(1)}) custom-call(f32[1024,2048]{1,0:T(8,128)S(1)} %get-tuple-element.18.s_ref, f32[1,1024]{1,0:T(1,128)S(1)} %bitcast.16, f32[4,1,1024]{2,1,0:T(1,128)S(1)} %all-gather.8.parts_ref), custom_call_target="tpu_custom_call" | custom-call | tf_op jit(solution)/shard_map/pallas_call | solution.py:195
  67.2 14.0 %all-gather.9.parts_ref = f32[8,1,2048]{2,1,0:T(1,128)S(1)} all-gather(f32[1,1,2048]{2,1,0:T(1,128)S(1)} %bitcast.22), channel_id=5, replica_groups=mesh['src'=8,'tgt'=4] {'src'}, dimensions={0}, use_global_device_ids=true | all-gather | bytes 73728 | tf_op jit(solution)/shard_map/all_gather | solution.py:206
  81.1 2.5 %shard_map.80 = f32[1,1024]{1,0:T(1,128)S(1)} custom-call(f32[1024,2048]{1,0:T(8,128)S(1)} %get-tuple-element.18.s_ref, f32[1,2048]{1,0:T(1,128)S(1)} %bitcast.13, f32[8,1,2048]{2,1,0:T(1,128)S(1)} %all-gather.9.parts_ref), custom_call_target="tpu_custom_call" | custom-call | tf_op jit(solution)/shard_map/pallas_call | solution.py:195
  83.7 7.2 %all-gather.10.parts_ref = f32[4,1,1024]{2,1,0:T(1,128)S(1)} all-gather(f32[1,1,1024]{2,1,0:T(1,128)S(1)} %bitcast.19), channel_id=6, replica_groups=mesh['src'=8,'tgt'=4] {'tgt'}, dimensions={0}, use_global_device_ids=true | all-gather | bytes 20480 | tf_op jit(solution)/shard_map/all_gather | solution.py:206
  90.9 2.6 %shard_map.81 = (f32[1,1024]{1,0:T(1,128)S(1)}, f32[1,2048]{1,0:T(1,128)S(1)}) custom-call(f32[1024,2048]{1,0:T(8,128)S(1)} %get-tuple-element.18.s_ref, f32[1,1024]{1,0:T(1,128)S(1)} %bitcast.17, f32[4,1,1024]{2,1,0:T(1,128)S(1)} %all-gather.10.parts_ref), custom_call_target="tpu_custom_call" | custom-call | tf_op jit(solution)/shard_map/pallas_call | solution.py:195
  93.4 14.0 %all-gather.11.parts_ref = f32[8,1,2048]{2,1,0:T(1,128)S(1)} all-gather(f32[1,1,2048]{2,1,0:T(1,128)S(1)} %bitcast.23), channel_id=7, replica_groups=mesh['src'=8,'tgt'=4] {'src'}, dimensions={0}, use_global_device_ids=true | all-gather | bytes 73728 | tf_op jit(solution)/shard_map/all_gather | solution.py:206
  107.4 5.1 %shard_map.82 = (f32[1,1024]{1,0:T(1,128)}, f32[1,2048]{1,0:T(1,128)}, f32[17,1024]{1,0:T(8,128)S(1)}, f32[17,1024]{1,0:T(8,128)S(1)}, f32[17,1024]{1,0:T(8,128)S(1)}, /*index=5*/f32[17,1024]{1,0:T(8,128)S(1)}) custom-call(s32[1]{0:T(128)} %bitcast.me_ref, f32[1024,2048]{1,0:T(8,128)S(1)} %get-tuple-element.18.s_ref, f32[1,2048]{1,0:T(1,128)S(1)} %bitcast.14, ...), custom_call_target="tpu_custom_call" | custom-call | tf_op jit(solution)/shard_map/pallas_call | solution.py:195
  112.5 1.5 %collective-permute-start.7 = (f32[17,1024]{1,0:T(8,128)S(1)}, f32[17,1024]{1,0:T(8,128)S(1)}, u32[]{:S(2)}, u32[]{:S(2)}) collective-permute-start(f32[17,1024]{1,0:T(8,128)S(1)} %get-tuple-element.30), channel_id=1, source_target_pairs={{0,1},{1,0},{2,3},{3,2},{4,5},{5,4},{6,7},{7,6},{8,9},{9,8},{10,11... | collective-permute-start | bytes 208904 | tf_op jit(solution)/shard_map/ppermute | solution.py:210
  116.0 1.5 %collective-permute-done.7.refs_1_ = f32[17,1024]{1,0:T(8,128)S(1)} collective-permute-done((f32[17,1024]{1,0:T(8,128)S(1)}, f32[17,1024]{1,0:T(8,128)S(1)}, u32[]{:S(2)}, u32[]{:S(2)}) %collective-permute-start.7) | collective-permute-done | bytes 69664 | tf_op jit(solution)/shard_map/ppermute | solution.py:210
  117.5 3.3 %collective-permute-done.8.refs_2_ = f32[17,1024]{1,0:T(8,128)S(1)} collective-permute-done((f32[17,1024]{1,0:T(8,128)S(1)}, f32[17,1024]{1,0:T(8,128)S(1)}, u32[]{:S(2)}, u32[]{:S(2)}) %collective-permute-start.8) | collective-permute-done | bytes 69664 | tf_op jit(solution)/shard_map/ppermute | solution.py:210
  (22 shorter events, 7.5 us)
Async XLA Ops:
  0.6 52.8 %copy-start = (f32[2048]{0:T(1024)S(1)}, f32[2048]{0:T(1024)}, u32[]{:S(2)}) copy-start(f32[2048]{0:T(1024)} %param.8) | copy-start | bytes 24580
  0.6 8.6 %collective-permute-start.4 = (f32[8,2048]{1,0:T(8,128)}, f32[8,2048]{1,0:T(8,128)S(1)}, u32[]{:S(2)}, u32[]{:S(2)}) collective-permute-start(f32[8,2048]{1,0:T(8,128)} %param.6), channel_id=1, source_target_pairs={{0,16},{4,20},{8,24},{12,28},{16,0},{20,4},{24,8},{28,12},{1,17},{... | collective-permute-start | bytes 196616 | tf_op jit(solution)/shard_map/ppermute | solution.py:210
  4.7 4.5 %collective-permute-start.3 = (f32[8,2048]{1,0:T(8,128)}, f32[8,2048]{1,0:T(8,128)S(1)}, u32[]{:S(2)}, u32[]{:S(2)}) collective-permute-start(f32[8,2048]{1,0:T(8,128)} %param.6), channel_id=1, source_target_pairs={{0,8},{4,12},{8,0},{12,4},{16,24},{20,28},{24,16},{28,20},{1,9},{5... | collective-permute-start | bytes 196616 | tf_op jit(solution)/shard_map/ppermute | solution.py:210
  6.3 6.3 %collective-permute-start.5 = (f32[8,2048]{1,0:T(8,128)}, f32[8,2048]{1,0:T(8,128)S(1)}, u32[]{:S(2)}, u32[]{:S(2)}) collective-permute-start(f32[8,2048]{1,0:T(8,128)} %param.6), channel_id=1, source_target_pairs={{0,24},{4,28},{8,16},{12,20},{16,8},{20,12},{24,0},{28,4},{1,25},{... | collective-permute-start | bytes 196616 | tf_op jit(solution)/shard_map/ppermute | solution.py:210
  12.6 8.5 %collective-permute-start.6 = (f32[32,2048]{1,0:T(8,128)S(1)}, f32[32,2048]{1,0:T(8,128)S(1)}, u32[]{:S(2)}, u32[]{:S(2)}) collective-permute-start(f32[32,2048]{1,0:T(8,128)S(1)} %constant_dynamic-update-slice_fusion.refs_4_), channel_id=1, source_target_pairs={{0,4},{4,0},{8,12},{12,8},{16,20},{20,16},{24,28},{28,24},{1,5},{5... | collective-permute-start | bytes 786440 | tf_op jit(solution)/shard_map/ppermute | solution.py:210
  12.6 4.7 %collective-permute-start.1 = (f32[16,1024]{1,0:T(8,128)}, f32[16,1024]{1,0:T(8,128)S(1)}, u32[]{:S(2)}, u32[]{:S(2)}) collective-permute-start(f32[16,1024]{1,0:T(8,128)} %refs_0_.1), channel_id=1, source_target_pairs={{0,2},{1,3},{2,0},{3,1},{4,6},{5,7},{6,4},{7,5},{8,10},{9,11},{10,... | collective-permute-start | bytes 196616 | tf_op jit(solution)/shard_map/ppermute | solution.py:210
  14.2 4.8 %collective-permute-start = (f32[16,1024]{1,0:T(8,128)}, f32[16,1024]{1,0:T(8,128)S(1)}, u32[]{:S(2)}, u32[]{:S(2)}) collective-permute-start(f32[16,1024]{1,0:T(8,128)} %refs_0_.1), channel_id=1, source_target_pairs={{0,1},{1,0},{2,3},{3,2},{4,5},{5,4},{6,7},{7,6},{8,9},{9,8},{10,11... | collective-permute-start | bytes 196616 | tf_op jit(solution)/shard_map/ppermute | solution.py:210
  15.7 5.4 %collective-permute-start.2 = (f32[16,1024]{1,0:T(8,128)}, f32[16,1024]{1,0:T(8,128)S(1)}, u32[]{:S(2)}, u32[]{:S(2)}) collective-permute-start(f32[16,1024]{1,0:T(8,128)} %refs_0_.1), channel_id=1, source_target_pairs={{0,3},{1,2},{2,1},{3,0},{4,7},{5,6},{6,5},{7,4},{8,11},{9,10},{10,... | collective-permute-start | bytes 196616 | tf_op jit(solution)/shard_map/ppermute | solution.py:210
  21.1 0.8 copy-start.1
  21.9 0.7 copy-start.3
  35.8 0.7 copy-start.2
  112.5 5.0 %collective-permute-start.7 = (f32[17,1024]{1,0:T(8,128)S(1)}, f32[17,1024]{1,0:T(8,128)S(1)}, u32[]{:S(2)}, u32[]{:S(2)}) collective-permute-start(f32[17,1024]{1,0:T(8,128)S(1)} %get-tuple-element.30), channel_id=1, source_target_pairs={{0,1},{1,0},{2,3},{3,2},{4,5},{5,4},{6,7},{7,6},{8,9},{9,8},{10,11... | collective-permute-start | bytes 208904 | tf_op jit(solution)/shard_map/ppermute | solution.py:210
  114.0 6.8 %collective-permute-start.8 = (f32[17,1024]{1,0:T(8,128)S(1)}, f32[17,1024]{1,0:T(8,128)S(1)}, u32[]{:S(2)}, u32[]{:S(2)}) collective-permute-start(f32[17,1024]{1,0:T(8,128)S(1)} %get-tuple-element.31), channel_id=1, source_target_pairs={{0,2},{1,3},{2,0},{3,1},{4,6},{5,7},{6,4},{7,5},{8,10},{9,11},{10,... | collective-permute-start | bytes 208904 | tf_op jit(solution)/shard_map/ppermute | solution.py:210
  114.6 6.3 %collective-permute-start.9 = (f32[17,1024]{1,0:T(8,128)S(1)}, f32[17,1024]{1,0:T(8,128)S(1)}, u32[]{:S(2)}, u32[]{:S(2)}) collective-permute-start(f32[17,1024]{1,0:T(8,128)S(1)} %get-tuple-element.32), channel_id=1, source_target_pairs={{0,3},{1,2},{2,1},{3,0},{4,7},{5,6},{6,5},{7,4},{8,11},{9,10},{10,... | collective-permute-start | bytes 208904 | tf_op jit(solution)/shard_map/ppermute | solution.py:210

commit v4 on v1

v4 whole, which is shorter than its diff:
```python
import functools
import math

import jax
import jax.numpy as jnp
from jax import lax
from jax.experimental import pallas as pl
from jax.experimental.pallas import tpu as pltpu
from jax.sharding import PartitionSpec as P

ITERS = 3
EPS = 0.1
UNIT = EPS * math.log(2.0)
LOW = 2.0**-40
HIGH = 2.0**20

F32 = jnp.float32
BF16 = jnp.bfloat16
VMEM = pl.BlockSpec(memory_space=pltpu.VMEM)
SMEM = pl.BlockSpec(memory_space=pltpu.SMEM)
HBM = pl.BlockSpec(memory_space=pltpu.HBM)
LANES = 128


def pieces(v):
    a = v.astype(BF16)
    r = v - a.astype(F32)
    b = r.astype(BF16)
    c = (r - b.astype(F32)).astype(BF16)
    return a, b, c


def tree(op, items):
    items = list(items)
    while len(items) > 1:
        half = (len(items) + 1) // 2
        rest = items[half:]
        items = [op(items[k], rest[k]) if k < len(rest) else items[k] for k in range(half)]
    return items[0]


def whole_log_sum(part_refs):
    if len(part_refs) == 1:
        parts = [part_refs[0][t] for t in range(part_refs[0].shape[0])]
    else:
        parts = [p[0] for p in part_refs]
    top = tree(jnp.maximum, parts)
    return top + jnp.log2(tree(jnp.add, [jnp.exp2(p - top) for p in parts]))


def to_row(wide):
    split = jnp.concatenate(pieces(wide), axis=1)
    ones = jnp.ones((16, split.shape[1]), BF16)
    return lax.dot_general(ones, split, (((1,), (1,)), ((), ())), preferred_element_type=F32)[0:1, :]


def across(row, out_ref):
    n = row.shape[1]
    a, b, c = [p.astype(F32) for p in pieces(row)]
    at = lax.broadcasted_iota(jnp.int32, (16, n), 0)
    split = jnp.where(at == 0, a, jnp.where(at == 1, b, jnp.where(at == 2, c, 0.0))).astype(BF16)
    ones = jnp.ones((16, LANES), BF16)
    out_ref[...] = lax.dot_general(split, ones, (((0,), (0,)), ((), ())), preferred_element_type=F32)


def eight(k):
    return pl.ds(pl.multiple_of(k * 8, 8), 8)


def chunk(c):
    return pl.ds(c * LANES, LANES)


def lanes_log_sum(s_ref, rows, pot8, top_ref, sum_ref):
    cols = s_ref.shape[1] // LANES
    z = [s_ref[rows, chunk(c)] + pot8[:, c * LANES : (c + 1) * LANES] for c in range(cols)]
    top = tree(jnp.maximum, z)
    top_ref[rows, :] = top
    sum_ref[rows, :] = tree(jnp.add, [jnp.exp2(v - top) for v in z])


def join_lanes(top_ref, sum_ref):
    def strip(k, _):
        rows = eight(k)
        part = top_ref[rows, :]
        top = jnp.broadcast_to(jnp.max(part, axis=1, keepdims=True), part.shape)
        sum_ref[rows, :] = sum_ref[rows, :] * jnp.exp2(part - top)
        top_ref[rows, :] = top * (1.0 / LANES)
        return 0

    lax.fori_loop(0, top_ref.shape[0] // 8, strip, 0, unroll=16)
    return to_row(top_ref[...]) + jnp.log2(to_row(sum_ref[...]))


def rows_log_sum(s_ref, pot, top_ref, sum_ref):
    n, width = s_ref.shape
    pot8 = jnp.broadcast_to(pot, (8, width))

    def strip(k, _):
        lanes_log_sum(s_ref, eight(k), pot8, top_ref, sum_ref)
        return 0

    lax.fori_loop(0, n // 8, strip, 0, unroll=4)
    return join_lanes(top_ref, sum_ref)


def cols_log_sum(s_ref, pot_ref):
    n, width = s_ref.shape
    cols = width // LANES

    def load(k):
        rows = eight(k)
        f = pot_ref[rows, :]
        return [s_ref[rows, chunk(c)] + f for c in range(cols)]

    def find(k, top):
        return tuple(jnp.maximum(t, v) for t, v in zip(top, load(k)))

    top = lax.fori_loop(1, n // 8, find, tuple(load(0)), unroll=4)

    def add(k, total):
        return tuple(a + jnp.exp2(v - t) for a, v, t in zip(total, load(k), top))

    zero = tuple(jnp.zeros((8, LANES), F32) for _ in range(cols))
    total = lax.fori_loop(0, n // 8, add, zero, unroll=4)
    out = []
    for t, a in zip(top, total):
        m = jnp.max(t, axis=0, keepdims=True)
        out.append(m + jnp.log2(jnp.sum(a * jnp.exp2(t - m), axis=0, keepdims=True)))
    return jnp.concatenate(out, axis=1)


def repeat(row, out_ref):
    for t in range(out_ref.shape[0]):
        out_ref[t] = row


def early_kernel(sm_ref, tm_ref, pot_ref, x_ref, ls_ref, lt_ref, to_ref, xo_ref):
    ls_ref[...] = jnp.log2(sm_ref[...])
    lt_ref[...] = jnp.log2(tm_ref[...])
    to_ref[...] = pot_ref[...]
    xo_ref[...] = x_ref[...]


def first_kernel(peers, xplan, yplan, me_ref, pot_ref, *refs):
    xcount, ycount = len(xplan), len(yplan)
    xparts, yparts, refs = refs[:xcount], refs[xcount : xcount + ycount], refs[xcount + ycount :]
    s_ref, l_ref, xn_ref, yn_ref, yo_ref, xs, xw, yw, top_ref, sum_ref = refs
    k = xs.shape[0]
    me_src, me_tgt = me_ref[0] // peers, lax.rem(me_ref[0], peers)
    for part, owners in zip(yparts, yplan):
        if owners is None:
            yo_ref[...] = part[...]
            continue
        own = part.shape[0] // len(owners)
        for b, d in enumerate(owners):
            yo_ref[pl.ds(pl.multiple_of((me_src ^ d) * own, 8), own), :] = part[pl.ds(b * own, own), :]
    for part, d in zip(xparts, xplan):
        if d is None:
            xs[...] = part[...]
            continue
        own = part.shape[0]
        xs[pl.ds(pl.multiple_of(lax.rem(me_tgt - d + peers, peers) * own, 8), own), :] = part[...]
    y = yo_ref[...]
    yn = jnp.sum(y * y, axis=0, keepdims=True) / k
    yn_ref[...] = yn
    y1, y2, y3 = pieces(y * (2.0 / (k * UNIT)))
    x = xs[...]
    xn_ref[...] = jnp.sum(x * x, axis=0, keepdims=True) / k
    x1, x2, x3 = pieces(x)
    for p, (xp, yp) in enumerate(((x1, y1), (x1, y2), (x2, y1), (x2, y2), (x1, y3), (x3, y1))):
        xw[pl.ds(p * k, k), :] = xp
        yw[pl.ds(p * k, k), :] = yp
    n, width = s_ref.shape
    pot8 = jnp.broadcast_to((pot_ref[...] - yn) * (1.0 / UNIT), (8, width))
    step = 256
    for b in range(n // step + 1):
        if b < n // step:
            s_ref[pl.ds(b * step, step), :] = lax.dot_general(
                xw[:, pl.ds(b * step, step)], yw[...], (((0,), (0,)), ((), ())), preferred_element_type=F32
            )
        if b > 0:
            for r in range((b - 1) * step, b * step, 8):
                lanes_log_sum(s_ref, pl.ds(r, 8), pot8, top_ref, sum_ref)
    l_ref[0] = join_lanes(top_ref, sum_ref)


def src_first_kernel(count, s_ref, mass_ref, *refs):
    parts, (f_ref, wide_ref, l_ref) = refs[:count], refs[count:]
    f = mass_ref[...] - whole_log_sum(parts)
    f_ref[...] = f
    across(f, wide_ref)
    repeat(cols_log_sum(s_ref, wide_ref), l_ref)


def tgt_first_kernel(count, s_ref, mass_ref, f_ref, wide_ref, *refs):
    parts, (g_ref, p_ref, l_ref, top_ref, sum_ref) = refs[:count], refs[count:]
    n, width = s_ref.shape
    g = mass_ref[...] - whole_log_sum(parts)
    g_ref[...] = g
    g8 = jnp.broadcast_to(g, (8, width))

    def strip(k, _):
        rows = eight(k)
        f = wide_ref[rows, :]
        out = []
        for c in range(width // LANES):
            p = jnp.exp2((s_ref[rows, chunk(c)] + f) + g8[:, c * LANES : (c + 1) * LANES])
            p_ref[rows, chunk(c)] = p
            out.append(p)
        sum_ref[rows, :] = tree(jnp.add, out)
        return 0

    lax.fori_loop(0, n // 8, strip, 0, unroll=4)
    total = to_row(sum_ref[...])
    l_ref[0] = jnp.log2(total)

    @pl.when(jnp.logical_not(jnp.min(total) >= LOW))
    def _():
        l_ref[0] = f_ref[...] + rows_log_sum(s_ref, g, top_ref, sum_ref)


def src_kernel(count, s_ref, p_ref, mass_ref, f_ref, g_ref, *refs):
    parts, (u_ref, l_ref, wide) = refs[:count], refs[count:]
    n, width = p_ref.shape
    cols = width // LANES
    change = mass_ref[...] - whole_log_sum(parts)
    u_ref[...] = change
    u = jnp.exp2(change)
    across(u, wide)

    def add(k, total):
        rows = eight(k)
        f = wide[rows, :]
        return tuple(a + p_ref[rows, chunk(c)] * f for c, a in enumerate(total))

    zero = tuple(jnp.zeros((8, LANES), F32) for _ in range(cols))
    parts = lax.fori_loop(0, n // 8, add, zero, unroll=4)
    total = jnp.concatenate([jnp.sum(a, axis=0, keepdims=True) for a in parts], axis=1)
    repeat(jnp.log2(total), l_ref)
    fine = jnp.logical_and(jnp.min(total) >= LOW, jnp.max(u) <= HIGH)

    @pl.when(jnp.logical_not(fine))
    def _():
        across(f_ref[...] + change, wide)
        repeat(g_ref[...] + cols_log_sum(s_ref, wide), l_ref)


def tgt_kernel(count, s_ref, p_ref, mass_ref, f_ref, g_ref, *refs):
    parts, (l_ref, top_ref, sum_ref) = refs[:count], refs[count:]
    n, width = p_ref.shape
    change = mass_ref[...] - whole_log_sum(parts)
    v = jnp.exp2(change)
    v8 = jnp.broadcast_to(v, (8, width))

    def strip(k, _):
        rows = eight(k)
        sum_ref[rows, :] = tree(
            jnp.add, [p_ref[rows, chunk(c)] * v8[:, c * LANES : (c + 1) * LANES] for c in range(width // LANES)]
        )
        return 0

    lax.fori_loop(0, n // 8, strip, 0, unroll=4)
    total = to_row(sum_ref[...])
    l_ref[0] = jnp.log2(total)
    fine = jnp.logical_and(jnp.min(total) >= LOW, jnp.max(v) <= HIGH)

    @pl.when(jnp.logical_not(fine))
    def _():
        l_ref[0] = f_ref[...] + rows_log_sum(s_ref, g_ref[...] + change, top_ref, sum_ref)


def last_kernel(count, me_ref, s_ref, p_ref, mass_ref, f_ref, g_ref, u_ref, xn_ref, yn_ref, y_ref, *refs):
    parts, refs = refs[:count], refs[count:]
    sp_any, tp_any, outs = refs[0], refs[1], refs[2:-7]
    sp, tp, yw, acc, flat, wide, sem = refs[-7:]
    k = y_ref.shape[0]
    n, width = s_ref.shape
    peers = len(outs)
    own = k // peers
    change = mass_ref[...] - whole_log_sum(parts)
    g = g_ref[...] + change
    f = f_ref[...] + u_ref[...]
    sp[...] = f * UNIT + xn_ref[...]
    tp[...] = g * UNIT + yn_ref[...]
    copies = [pltpu.make_async_copy(sp, sp_any, sem.at[0]), pltpu.make_async_copy(tp, tp_any, sem.at[1])]
    for copy in copies:
        copy.start()
    u = jnp.exp2(u_ref[...])
    v = jnp.exp2(change)
    step = 256

    def project(weight, scale, rescale):
        y1, y2, _ = pieces(y_ref[...] * scale)
        s1, s2, _ = [p.astype(F32) for p in pieces(scale)]
        yw[pl.ds(0, k), :] = y1
        at = lax.broadcasted_iota(jnp.int32, (LANES - k, width), 0)
        yw[pl.ds(k, LANES - k), :] = jnp.where(at == 0, s1, jnp.where(at == 1, s2, 0.0)).astype(BF16)
        yw[pl.ds(LANES, k), :] = y2
        yw[pl.ds(LANES + k, LANES - k), :] = jnp.zeros((LANES - k, width), BF16)
        for b in range(n // step):
            w = weight(pl.ds(b * step, step))
            w1 = w.astype(BF16)
            w2 = (w - w1.astype(F32)).astype(BF16)
            dims = (((1,), (1,)), ((), ()))
            out = lax.dot_general(w1, yw[...], dims, preferred_element_type=F32) + lax.dot_general(
                w2, yw[...], dims, preferred_element_type=F32
            )
            acc[pl.ds(b * step, step), :] = out[:, :LANES] + out[:, LANES:]
        total = acc[...].T * rescale
        den = total[k : k + 1, :] + total[k + 1 : k + 2, :]
        for t in range(peers):
            flat[t] = total[t * own : (t + 1) * own, :]
        for d, out in enumerate(outs):
            out[pl.ds(0, own), :] = flat[lax.rem(me_ref[0] + d, peers)]
            out[pl.ds(own, 1), :] = den
        return den

    den = project(lambda rows: p_ref[rows, :], v, u)
    fine = jnp.logical_and(jnp.min(den) >= LOW, jnp.logical_and(jnp.max(u) <= HIGH, jnp.max(v) <= HIGH))

    @pl.when(jnp.logical_not(fine))
    def _():
        across(f, wide)

        def weight(rows):
            fb = jnp.concatenate([wide[rows, :]] * (width // LANES), axis=1)
            return jnp.exp2((s_ref[rows, :] + fb) + g)

        project(weight, jnp.ones_like(v), jnp.ones_like(u))

    for copy in copies:
        copy.wait()


def join_kernel(*refs):
    parts, out_ref = refs[:-1], refs[-1]
    own = out_ref.shape[0]
    num = tree(jnp.add, [p[pl.ds(0, own), :] for p in parts])
    den = tree(jnp.add, [p[pl.ds(own, 1), :] for p in parts])
    out_ref[...] = num / den


def call(kernel, outs, scratch, ins, out_specs=None):
    return pl.pallas_call(
        kernel,
        out_shape=[jax.ShapeDtypeStruct(o, F32) for o in outs],
        in_specs=[spec for spec, _ in ins],
        out_specs=out_specs or [VMEM] * len(outs),
        scratch_shapes=scratch,
        compiler_params=pltpu.CompilerParams(vmem_limit_bytes=20 * 2**20),
    )(*[a for _, a in ins])


def put(*arrays):
    return [(VMEM, a) for a in arrays]


def turn(v, axis, size, d):
    return lax.ppermute(v, axis, [(i, (i + d) % size) for i in range(size)])


def flip(v, axis, size, bit):
    return lax.ppermute(v, axis, [(i, i ^ bit) for i in range(size)])


def few(size):
    return size <= 4


def everyone(v, axis, size):
    if few(size):
        return [v] + [turn(v, axis, size, d) for d in range(1, size)]
    return [lax.all_to_all(v, axis, 0, 0, tiled=True)]


def copies_of(size):
    return 1 if few(size) else size


def gather_src(v, size):
    if v.shape[0] % 8 or not few(size):
        return [lax.all_gather(v, "tgt", axis=0, tiled=True)], [None]
    return [v] + [turn(v, "tgt", size, d) for d in range(1, size)], list(range(size))


def gather_tgt(v, size, other):
    if v.shape[0] % 8 or size & (size - 1):
        return [lax.all_gather(v, "src", axis=0, tiled=True)], [None], other
    order = list(range(0, size, 2))
    mine = jnp.concatenate([v] + [flip(v, "src", size, d) for d in order[1:]], axis=0)
    mine, *early = lax.optimization_barrier([mine] + other[:-1])
    other = early + other[-1:]
    return [mine, flip(mine, "src", size, 1)], [order, [d + 1 for d in order]], other


def shards(peers_src, peers_tgt, src_pts, tgt_pts, src_mass, tgt_mass, init_pot):
    own = src_pts.shape[0]
    n, width = src_pts.shape[1], tgt_pts.shape[1]
    k = own * peers_tgt
    xs, xplan = gather_src(src_pts, peers_tgt)
    row, col = (1, n), (1, width)
    early = call(
        early_kernel,
        [row, col, col, src_pts.shape],
        [],
        put(src_mass.reshape(row), tgt_mass.reshape(col), init_pot.reshape(col), src_pts),
    )
    sm, tm, pot, x = early
    if xplan[0] is not None:
        xs[0] = x
    ys, yplan, (sm, tm, pot, *xs) = gather_tgt(tgt_pts, peers_src, [sm, tm, pot] + xs)
    me = lax.axis_index(("src", "tgt")).astype(jnp.int32).reshape(1)
    rows, cols = (copies_of(peers_tgt), 1, n), (copies_of(peers_src), 1, width)
    lane = pltpu.VMEM((n, LANES), F32)
    s, l, xn, yn, yo = call(
        functools.partial(first_kernel, peers_tgt, xplan, yplan),
        [(n, width), rows, row, col, (k, width)],
        [
            pltpu.VMEM((k, n), F32),
            pltpu.VMEM((6 * k, n), BF16),
            pltpu.VMEM((6 * k, width), BF16),
            lane,
            lane,
        ],
        [(SMEM, me)] + put(pot, *xs, *ys),
    )
    parts = everyone(l, "tgt", peers_tgt)
    f, wide, l = call(
        functools.partial(src_first_kernel, len(parts)), [row, (n, LANES), cols], [], put(s, sm, *parts)
    )
    parts = everyone(l, "src", peers_src)
    g, p, l = call(
        functools.partial(tgt_first_kernel, len(parts)),
        [col, (n, width), rows],
        [lane, lane],
        put(s, tm, f, wide, *parts),
    )
    for step in range(1, ITERS):
        parts = everyone(l, "tgt", peers_tgt)
        u, l = call(functools.partial(src_kernel, len(parts)), [row, cols], [lane], put(s, p, sm, f, g, *parts))
        parts = everyone(l, "src", peers_src)
        if step < ITERS - 1:
            (l,) = call(functools.partial(tgt_kernel, len(parts)), [rows], [lane, lane], put(s, p, tm, f, g, *parts))
    src_pot, tgt_pot, *blocks = call(
        functools.partial(last_kernel, len(parts)),
        [row, col] + [(own + 1, n)] * peers_tgt,
        [
            pltpu.VMEM(row, F32),
            pltpu.VMEM(col, F32),
            pltpu.VMEM((2 * LANES, width), BF16),
            lane,
            pltpu.VMEM((peers_tgt, own, n), F32),
            lane,
            pltpu.SemaphoreType.DMA((2,)),
        ],
        [(SMEM, me)] + put(s, p, tm, f, g, u, xn, yn, yo, *parts),
        [HBM, HBM] + [VMEM] * peers_tgt,
    )
    came = [blocks[0]] + [turn(blocks[d], "tgt", peers_tgt, d) for d in range(1, peers_tgt)]
    (mapped,) = call(join_kernel, [(own, n)], [], put(*came))
    return src_pot.reshape(n), tgt_pot.reshape(width), mapped


def solution(mesh):
    return jax.shard_map(
        functools.partial(shards, mesh.shape["src"], mesh.shape["tgt"]),
        mesh=mesh,
        in_specs=(P("tgt", "src"), P("src", "tgt"), P("src"), P("tgt"), P("tgt")),
        out_specs=(P("src"), P("tgt"), P("tgt", "src")),
        check_vma=False,
    )
```

time: 115 us -> 97.6 us (0.85); the launches traced: 114 us -> 98.6 us
  waiting for transfers between devices: 26.8 us -> 16.8 us
  starting transfers between devices: 30.4 us -> 25.1 us
  local copies, waits for them, and re-layouts: 4.78 us -> 2.08 us
  Pallas kernels: 25.4 us -> 26.8 us
    all_gather x2 -> x0, blocking collectives: 26.3 us -> none  [the longest x1 15.6 us: shards(): ys = lax.all_gather(tgt_pts, 'src', axis=0, tiled=True)]
    all_to_all x0 -> x3, blocking collectives: none -> 26.1 us  [everyone(): return [lax.all_to_all(v, axis, 0, 0, tiled=True)]]
    ppermute x33 -> x19, waiting for transfers between devices: 26.8 us -> 16.8 us  [the longest x15 16.7 us: turn(): return lax.ppermute(v, axis, [(i, (i + d) % size) for i in range(size)])]
    ppermute x33 -> x19, starting transfers between devices: 30.4 us -> 25.1 us  [the longest x15 19.4 us: turn(): return lax.ppermute(v, axis, [(i, (i + d) % size) for i in range(size)])]
    unnamed x12 -> x6, local copies, waits for them, and re-layouts: 4.78 us -> 2.08 us
    pallas_call x8 -> x9, Pallas kernels: 25.4 us -> 26.8 us  [call(): pl.pallas_call(kernel, out_shape=[jax.ShapeDtypeStruct(o, F32) for o in o...]
  transfers between devices with their start and end apart: 33 -> 19, of which waited for: 22 -> 14; matrix products, arithmetic and copies ran while one was open for 0% -> 1% of each run, Pallas kernels for 0% -> 1%
where the time goes in v4:
time: 97.6 us; the launch traced here: 98.6 us
  Pallas kernels  26.8 us (27%)
  blocking collectives  26.1 us (27%)
  starting transfers between devices  25.1 us (26%)
  waiting for transfers between devices  16.8 us (17%)
  local copies, waits for them, and re-layouts  2.08 us (2%)
    pallas_call x9, Pallas kernels, call(): pl.pallas_call(kernel, out_shape=[jax.ShapeDtypeStruct(o, F32) for o in o...  26.8 us
    all_to_all x3, blocking collectives, everyone(): return [lax.all_to_all(v, axis, 0, 0, tiled=True)]  26.1 us
    ppermute x15, starting transfers between devices, turn(): return lax.ppermute(v, axis, [(i, (i + d) % size) for i in range(size)])  19.4 us
    ppermute x15, waiting for transfers between devices, turn(): return lax.ppermute(v, axis, [(i, (i + d) % size) for i in range(size)])  16.7 us
    ppermute x4, starting transfers between devices, flip(): return lax.ppermute(v, axis, [(i, i ^ bit) for i in range(size)])  5.75 us
    unnamed x6, local copies, waits for them, and re-layouts  2.08 us
  transfers between devices with their start and end apart: 19, of which 14 were waited for; matrix products, arithmetic and copies ran while one was open for 1% of the time, Pallas kernels for 1%

profile of v4, /device:TPU:0, one launch (start us, length us, event | category | flops | bytes accessed | tf_op | source)
XLA Modules:
  0.0 98.6 jit_solution(3195950566535403232)
XLA Ops:
  0.6 4.1 %collective-permute-start.1 = (f32[8,2048]{1,0:T(8,128)}, f32[8,2048]{1,0:T(8,128)S(1)}, u32[]{:S(2)}, u32[]{:S(2)}) collective-permute-start(f32[8,2048]{1,0:T(8,128)} %param.6), channel_id=1, source_target_pairs={{0,16},{4,20},{8,24},{12,28},{16,0},{20,4},{24,8},{28,12},{1,17},{... | collective-permute-start | bytes 196616 | tf_op jit(solution)/shard_map/ppermute | solution.py:364
  4.7 1.6 %collective-permute-start = (f32[8,2048]{1,0:T(8,128)}, f32[8,2048]{1,0:T(8,128)S(1)}, u32[]{:S(2)}, u32[]{:S(2)}) collective-permute-start(f32[8,2048]{1,0:T(8,128)} %param.6), channel_id=1, source_target_pairs={{0,8},{4,12},{8,0},{12,4},{16,24},{20,28},{24,16},{28,20},{1,9},{5... | collective-permute-start | bytes 196616 | tf_op jit(solution)/shard_map/ppermute | solution.py:364
  6.3 1.7 %collective-permute-start.3 = (f32[16,1024]{1,0:T(8,128)}, f32[16,1024]{1,0:T(8,128)S(1)}, u32[]{:S(2)}, u32[]{:S(2)}) collective-permute-start(f32[16,1024]{1,0:T(8,128)} %x_ref.1), channel_id=1, source_target_pairs={{0,1},{1,2},{2,3},{3,0},{4,5},{5,6},{6,7},{7,4},{8,9},{9,10},{10,1... | collective-permute-start | bytes 196616 | tf_op jit(solution)/shard_map/ppermute | solution.py:360
  8.0 1.5 %collective-permute-start.4 = (f32[16,1024]{1,0:T(8,128)}, f32[16,1024]{1,0:T(8,128)S(1)}, u32[]{:S(2)}, u32[]{:S(2)}) collective-permute-start(f32[16,1024]{1,0:T(8,128)} %x_ref.1), channel_id=1, source_target_pairs={{0,2},{1,3},{2,0},{3,1},{4,6},{5,7},{6,4},{7,5},{8,10},{9,11},{10,... | collective-permute-start | bytes 196616 | tf_op jit(solution)/shard_map/ppermute | solution.py:360
  13.5 2.5 %collective-permute-start.5 = (f32[16,1024]{1,0:T(8,128)}, f32[16,1024]{1,0:T(8,128)S(1)}, u32[]{:S(2)}, u32[]{:S(2)}) collective-permute-start(f32[16,1024]{1,0:T(8,128)} %x_ref.1), channel_id=1, source_target_pairs={{0,3},{1,0},{2,1},{3,2},{4,7},{5,4},{6,5},{7,6},{8,11},{9,8},{10,9... | collective-permute-start | bytes 196616 | tf_op jit(solution)/shard_map/ppermute | solution.py:360
  16.0 2.3 %collective-permute-done.5.refs_3_ = f32[16,1024]{1,0:T(8,128)S(1)} collective-permute-done((f32[16,1024]{1,0:T(8,128)}, f32[16,1024]{1,0:T(8,128)S(1)}, u32[]{:S(2)}, u32[]{:S(2)}) %collective-permute-start.5) | collective-permute-done | bytes 65568 | tf_op jit(solution)/shard_map/ppermute | solution.py:360
  18.3 4.5 %shard_map.77 = (f32[1024,2048]{1,0:T(8,128)S(1)}, f32[1,1,1024]{2,1,0:T(1,128)S(1)}, f32[1,1024]{1,0:T(1,128)S(1)}, f32[1,2048]{1,0:T(1,128)S(1)}, f32[64,2048]{1,0:T(8,128)S(1)}) custom-call(s32[1]{0:T(128)} %bitcast.me_ref, f32[1,2048]{1,0:T(1,128)S(1)} %get-tuple-element.38.pot_ref, f32[16,1024]{1,0:T(8,128)S(1)} %get-tuple-element.39.refs_0_, ...), custom_call_target="tpu_custom_call" | custom-call | tf_op jit(solution)/shard_map/pallas_call | solution.py:345
  22.8 3.3 %collective-permute-start.9 = (f32[1,1,1024]{2,1,0:T(1,128)S(1)}, f32[1,1,1024]{2,1,0:T(1,128)S(1)}, u32[]{:S(2)}, u32[]{:S(2)}) collective-permute-start(f32[1,1,1024]{2,1,0:T(1,128)S(1)} %get-tuple-element.46.refs_0_), channel_id=1, source_target_pairs={{0,3},{1,0},{2,1},{3,2},{4,7},{5,4},{6,5},{7,6},{8,11},{9,8},{10,9... | collective-permute-start | bytes 12296 | tf_op jit(solution)/shard_map/ppermute | solution.py:360
  27.5 2.3 %collective-permute-done.8.refs_2_ = f32[1,1,1024]{2,1,0:T(1,128)S(1)} collective-permute-done((f32[1,1,1024]{2,1,0:T(1,128)S(1)}, f32[1,1,1024]{2,1,0:T(1,128)S(1)}, u32[]{:S(2)}, u32[]{:S(2)}) %collective-permute-start.8) | collective-permute-done | bytes 4128 | tf_op jit(solution)/shard_map/ppermute | solution.py:360
  31.1 2.7 %shard_map.78 = (f32[1,1024]{1,0:T(1,128)S(1)}, f32[1024,128]{1,0:T(8,128)S(1)}, f32[8,1,2048]{2,1,0:T(1,128)S(1)}) custom-call(f32[1024,2048]{1,0:T(8,128)S(1)} %get-tuple-element.43.s_ref, f32[1,1024]{1,0:T(1,128)S(1)} %get-tuple-element.45.mass_ref, f32[1,1,1024]{2,1,0:T(1,128)S(1)} %get-tuple-element.46.refs_0_, ...), custom_call_target="tpu_custom_call" | custom-call | tf_op jit(solution)/shard_map/pallas_call | solution.py:345
  33.8 9.6 %all_to_all.15.refs_0_ = f32[8,1,2048]{2,1,0:T(1,128)S(1)} all-to-all(f32[8,1,2048]{2,1,0:T(1,128)S(1)} %get-tuple-element.49), channel_id=1, replica_groups=mesh['src'=8,'tgt'=4] {'src'}, dimensions={0} | all-to-all | bytes 131072 | tf_op jit(solution)/shard_map/all_to_all | solution.py:374
  43.4 2.3 %shard_map.79 = (f32[1,2048]{1,0:T(1,128)S(1)}, f32[1024,2048]{1,0:T(8,128)S(1)}, f32[1,1,1024]{2,1,0:T(1,128)S(1)}) custom-call(f32[1024,2048]{1,0:T(8,128)S(1)} %get-tuple-element.43.s_ref, f32[1,2048]{1,0:T(1,128)S(1)} %get-tuple-element.44.mass_ref, f32[1,1024]{1,0:T(1,128)S(1)} %get-tuple-element.47.f_ref, f32[1024,128]{1,0:T(8,128)S(1)} %get-tuple-element.48.wide_ref, ...), custom_call_target="tpu_custom_call" | custom-call | tf_op jit(solution)/shard_map/pallas_call | solution.py:345
  45.8 1.5 %collective-permute-start.11 = (f32[1,1,1024]{2,1,0:T(1,128)S(1)}, f32[1,1,1024]{2,1,0:T(1,128)S(1)}, u32[]{:S(2)}, u32[]{:S(2)}) collective-permute-start(f32[1,1,1024]{2,1,0:T(1,128)S(1)} %get-tuple-element.52.refs_0_), channel_id=1, source_target_pairs={{0,2},{1,3},{2,0},{3,1},{4,6},{5,7},{6,4},{7,5},{8,10},{9,11},{10,... | collective-permute-start | bytes 12296 | tf_op jit(solution)/shard_map/ppermute | solution.py:360
  47.3 1.9 %collective-permute-start.10 = (f32[1,1,1024]{2,1,0:T(1,128)S(1)}, f32[1,1,1024]{2,1,0:T(1,128)S(1)}, u32[]{:S(2)}, u32[]{:S(2)}) collective-permute-start(f32[1,1,1024]{2,1,0:T(1,128)S(1)} %get-tuple-element.52.refs_0_), channel_id=1, source_target_pairs={{0,1},{1,2},{2,3},{3,0},{4,5},{5,6},{6,7},{7,4},{8,9},{9,10},{10,1... | collective-permute-start | bytes 12296 | tf_op jit(solution)/shard_map/ppermute | solution.py:360
  49.5 2.4 %collective-permute-done.10.refs_1_ = f32[1,1,1024]{2,1,0:T(1,128)S(1)} collective-permute-done((f32[1,1,1024]{2,1,0:T(1,128)S(1)}, f32[1,1,1024]{2,1,0:T(1,128)S(1)}, u32[]{:S(2)}, u32[]{:S(2)}) %collective-permute-start.10) | collective-permute-done | bytes 4128 | tf_op jit(solution)/shard_map/ppermute | solution.py:360
  51.8 4.5 %shard_map.80 = (f32[1,1024]{1,0:T(1,128)}, f32[8,1,2048]{2,1,0:T(1,128)S(1)}) custom-call(f32[1024,2048]{1,0:T(8,128)S(1)} %get-tuple-element.43.s_ref, f32[1024,2048]{1,0:T(8,128)S(1)} %get-tuple-element.50.p_ref, f32[1,1024]{1,0:T(1,128)S(1)} %get-tuple-element.45.mass_ref, f32[1,1024]{1,0:T(1,128)S(1)} %get-tuple-element.47.f_ref, ...), custom_call_target="tpu_custom_call" | custom-call | tf_op jit(solution)/shard_map/pallas_call | solution.py:345
  56.3 8.3 %all_to_all.16.refs_0_ = f32[8,1,2048]{2,1,0:T(1,128)S(1)} all-to-all(f32[8,1,2048]{2,1,0:T(1,128)S(1)} %get-tuple-element.53), channel_id=1, replica_groups=mesh['src'=8,'tgt'=4] {'src'}, dimensions={0} | all-to-all | bytes 131072 | tf_op jit(solution)/shard_map/all_to_all | solution.py:374
  67.0 1.5 %collective-permute-start.14 = (f32[1,1,1024]{2,1,0:T(1,128)S(1)}, f32[1,1,1024]{2,1,0:T(1,128)S(1)}, u32[]{:S(2)}, u32[]{:S(2)}) collective-permute-start(f32[1,1,1024]{2,1,0:T(1,128)S(1)} %shard_map.81.refs_0_), channel_id=1, source_target_pairs={{0,2},{1,3},{2,0},{3,1},{4,6},{5,7},{6,4},{7,5},{8,10},{9,11},{10,... | collective-permute-start | bytes 12296 | tf_op jit(solution)/shard_map/ppermute | solution.py:360
  70.6 2.4 %collective-permute-done.13.refs_1_ = f32[1,1,1024]{2,1,0:T(1,128)S(1)} collective-permute-done((f32[1,1,1024]{2,1,0:T(1,128)S(1)}, f32[1,1,1024]{2,1,0:T(1,128)S(1)}, u32[]{:S(2)}, u32[]{:S(2)}) %collective-permute-start.13) | collective-permute-done | bytes 4128 | tf_op jit(solution)/shard_map/ppermute | solution.py:360
  72.9 3.9 %shard_map.82 = (f32[1,1024]{1,0:T(1,128)S(1)}, f32[8,1,2048]{2,1,0:T(1,128)S(1)}) custom-call(f32[1024,2048]{1,0:T(8,128)S(1)} %get-tuple-element.43.s_ref, f32[1024,2048]{1,0:T(8,128)S(1)} %get-tuple-element.50.p_ref, f32[1,1024]{1,0:T(1,128)S(1)} %get-tuple-element.45.mass_ref, f32[1,1024]{1,0:T(1,128)S(1)} %get-tuple-element.47.f_ref, ...), custom_call_target="tpu_custom_call" | custom-call | tf_op jit(solution)/shard_map/pallas_call | solution.py:345
  76.8 8.3 %all_to_all.17.refs_0_ = f32[8,1,2048]{2,1,0:T(1,128)S(1)} all-to-all(f32[8,1,2048]{2,1,0:T(1,128)S(1)} %get-tuple-element.58), channel_id=1, replica_groups=mesh['src'=8,'tgt'=4] {'src'}, dimensions={0} | all-to-all | bytes 131072 | tf_op jit(solution)/shard_map/all_to_all | solution.py:374
  85.1 6.1 %shard_map.83 = (f32[1,1024]{1,0:T(1,128)}, f32[1,2048]{1,0:T(1,128)}, f32[17,1024]{1,0:T(8,128)S(1)}, f32[17,1024]{1,0:T(8,128)S(1)}, f32[17,1024]{1,0:T(8,128)S(1)}, /*index=5*/f32[17,1024]{1,0:T(8,128)S(1)}) custom-call(s32[1]{0:T(128)} %bitcast.me_ref, f32[1024,2048]{1,0:T(8,128)S(1)} %get-tuple-element.43.s_ref, ...), custom_call_target="tpu_custom_call" | custom-call | tf_op jit(solution)/shard_map/pallas_call | solution.py:345
  92.0 2.8 %collective-permute-start.18 = (f32[17,1024]{1,0:T(8,128)S(1)}, f32[17,1024]{1,0:T(8,128)S(1)}, u32[]{:S(2)}, u32[]{:S(2)}) collective-permute-start(f32[17,1024]{1,0:T(8,128)S(1)} %get-tuple-element.64), channel_id=1, source_target_pairs={{0,3},{1,0},{2,1},{3,2},{4,7},{5,4},{6,5},{7,6},{8,11},{9,8},{10,9... | collective-permute-start | bytes 208904 | tf_op jit(solution)/shard_map/ppermute | solution.py:360
  94.8 2.9 %collective-permute-done.16.refs_1_ = f32[17,1024]{1,0:T(8,128)S(1)} collective-permute-done((f32[17,1024]{1,0:T(8,128)S(1)}, f32[17,1024]{1,0:T(8,128)S(1)}, u32[]{:S(2)}, u32[]{:S(2)}) %collective-permute-start.16) | collective-permute-done | bytes 69664 | tf_op jit(solution)/shard_map/ppermute | solution.py:360
  (33 shorter events, 13.1 us)
Async XLA Ops:
  0.6 11.8 %collective-permute-start.1 = (f32[8,2048]{1,0:T(8,128)}, f32[8,2048]{1,0:T(8,128)S(1)}, u32[]{:S(2)}, u32[]{:S(2)}) collective-permute-start(f32[8,2048]{1,0:T(8,128)} %param.6), channel_id=1, source_target_pairs={{0,16},{4,20},{8,24},{12,28},{16,0},{20,4},{24,8},{28,12},{1,17},{... | collective-permute-start | bytes 196616 | tf_op jit(solution)/shard_map/ppermute | solution.py:364
  4.7 7.7 %collective-permute-start = (f32[8,2048]{1,0:T(8,128)}, f32[8,2048]{1,0:T(8,128)S(1)}, u32[]{:S(2)}, u32[]{:S(2)}) collective-permute-start(f32[8,2048]{1,0:T(8,128)} %param.6), channel_id=1, source_target_pairs={{0,8},{4,12},{8,0},{12,4},{16,24},{20,28},{24,16},{28,20},{1,9},{5... | collective-permute-start | bytes 196616 | tf_op jit(solution)/shard_map/ppermute | solution.py:364
  6.3 6.3 %collective-permute-start.2 = (f32[8,2048]{1,0:T(8,128)}, f32[8,2048]{1,0:T(8,128)S(1)}, u32[]{:S(2)}, u32[]{:S(2)}) collective-permute-start(f32[8,2048]{1,0:T(8,128)} %param.6), channel_id=1, source_target_pairs={{0,24},{4,28},{8,16},{12,20},{16,8},{20,12},{24,0},{28,4},{1,25},{... | collective-permute-start | bytes 196616 | tf_op jit(solution)/shard_map/ppermute | solution.py:364
  6.3 7.1 %collective-permute-start.3 = (f32[16,1024]{1,0:T(8,128)}, f32[16,1024]{1,0:T(8,128)S(1)}, u32[]{:S(2)}, u32[]{:S(2)}) collective-permute-start(f32[16,1024]{1,0:T(8,128)} %x_ref.1), channel_id=1, source_target_pairs={{0,1},{1,2},{2,3},{3,0},{4,5},{5,6},{6,7},{7,4},{8,9},{9,10},{10,1... | collective-permute-start | bytes 196616 | tf_op jit(solution)/shard_map/ppermute | solution.py:360
  8.0 5.4 %collective-permute-start.4 = (f32[16,1024]{1,0:T(8,128)}, f32[16,1024]{1,0:T(8,128)S(1)}, u32[]{:S(2)}, u32[]{:S(2)}) collective-permute-start(f32[16,1024]{1,0:T(8,128)} %x_ref.1), channel_id=1, source_target_pairs={{0,2},{1,3},{2,0},{3,1},{4,6},{5,7},{6,4},{7,5},{8,10},{9,11},{10,... | collective-permute-start | bytes 196616 | tf_op jit(solution)/shard_map/ppermute | solution.py:360
  9.5 0.7 copy-start
  10.2 0.7 copy-start.1
  10.9 0.7 copy-start.2
  13.5 4.9 %collective-permute-start.6 = (f32[32,2048]{1,0:T(8,128)S(1)}, f32[32,2048]{1,0:T(8,128)S(1)}, u32[]{:S(2)}, u32[]{:S(2)}) collective-permute-start(f32[32,2048]{1,0:T(8,128)S(1)} %pad_maximum_fusion.refs_4_), channel_id=1, source_target_pairs={{0,4},{4,0},{8,12},{12,8},{16,20},{20,16},{24,28},{28,24},{1,5},{5... | collective-permute-start | bytes 786440 | tf_op jit(solution)/shard_map/ppermute | solution.py:364
  13.5 4.8 %collective-permute-start.5 = (f32[16,1024]{1,0:T(8,128)}, f32[16,1024]{1,0:T(8,128)S(1)}, u32[]{:S(2)}, u32[]{:S(2)}) collective-permute-start(f32[16,1024]{1,0:T(8,128)} %x_ref.1), channel_id=1, source_target_pairs={{0,3},{1,0},{2,1},{3,2},{4,7},{5,4},{6,5},{7,6},{8,11},{9,8},{10,9... | collective-permute-start | bytes 196616 | tf_op jit(solution)/shard_map/ppermute | solution.py:360
  22.8 4.6 %collective-permute-start.9 = (f32[1,1,1024]{2,1,0:T(1,128)S(1)}, f32[1,1,1024]{2,1,0:T(1,128)S(1)}, u32[]{:S(2)}, u32[]{:S(2)}) collective-permute-start(f32[1,1,1024]{2,1,0:T(1,128)S(1)} %get-tuple-element.46.refs_0_), channel_id=1, source_target_pairs={{0,3},{1,0},{2,1},{3,2},{4,7},{5,4},{6,5},{7,6},{8,11},{9,8},{10,9... | collective-permute-start | bytes 12296 | tf_op jit(solution)/shard_map/ppermute | solution.py:360
  26.1 3.6 %collective-permute-start.8 = (f32[1,1,1024]{2,1,0:T(1,128)S(1)}, f32[1,1,1024]{2,1,0:T(1,128)S(1)}, u32[]{:S(2)}, u32[]{:S(2)}) collective-permute-start(f32[1,1,1024]{2,1,0:T(1,128)S(1)} %get-tuple-element.46.refs_0_), channel_id=1, source_target_pairs={{0,2},{1,3},{2,0},{3,1},{4,6},{5,7},{6,4},{7,5},{8,10},{9,11},{10,... | collective-permute-start | bytes 12296 | tf_op jit(solution)/shard_map/ppermute | solution.py:360
  26.6 4.5 %collective-permute-start.7 = (f32[1,1,1024]{2,1,0:T(1,128)S(1)}, f32[1,1,1024]{2,1,0:T(1,128)S(1)}, u32[]{:S(2)}, u32[]{:S(2)}) collective-permute-start(f32[1,1,1024]{2,1,0:T(1,128)S(1)} %get-tuple-element.46.refs_0_), channel_id=1, source_target_pairs={{0,1},{1,2},{2,3},{3,0},{4,5},{5,6},{6,7},{7,4},{8,9},{9,10},{10,1... | collective-permute-start | bytes 12296 | tf_op jit(solution)/shard_map/ppermute | solution.py:360
  45.7 3.7 %collective-permute-start.12 = (f32[1,1,1024]{2,1,0:T(1,128)S(1)}, f32[1,1,1024]{2,1,0:T(1,128)S(1)}, u32[]{:S(2)}, u32[]{:S(2)}) collective-permute-start(f32[1,1,1024]{2,1,0:T(1,128)S(1)} %get-tuple-element.52.refs_0_), channel_id=1, source_target_pairs={{0,3},{1,0},{2,1},{3,2},{4,7},{5,4},{6,5},{7,6},{8,11},{9,8},{10,9... | collective-permute-start | bytes 12296 | tf_op jit(solution)/shard_map/ppermute | solution.py:360
  45.8 3.7 %collective-permute-start.11 = (f32[1,1,1024]{2,1,0:T(1,128)S(1)}, f32[1,1,1024]{2,1,0:T(1,128)S(1)}, u32[]{:S(2)}, u32[]{:S(2)}) collective-permute-start(f32[1,1,1024]{2,1,0:T(1,128)S(1)} %get-tuple-element.52.refs_0_), channel_id=1, source_target_pairs={{0,2},{1,3},{2,0},{3,1},{4,6},{5,7},{6,4},{7,5},{8,10},{9,11},{10,... | collective-permute-start | bytes 12296 | tf_op jit(solution)/shard_map/ppermute | solution.py:360
  47.3 4.5 %collective-permute-start.10 = (f32[1,1,1024]{2,1,0:T(1,128)S(1)}, f32[1,1,1024]{2,1,0:T(1,128)S(1)}, u32[]{:S(2)}, u32[]{:S(2)}) collective-permute-start(f32[1,1,1024]{2,1,0:T(1,128)S(1)} %get-tuple-element.52.refs_0_), channel_id=1, source_target_pairs={{0,1},{1,2},{2,3},{3,0},{4,5},{5,6},{6,7},{7,4},{8,9},{9,10},{10,1... | collective-permute-start | bytes 12296 | tf_op jit(solution)/shard_map/ppermute | solution.py:360
  65.9 3.7 %collective-permute-start.15 = (f32[1,1,1024]{2,1,0:T(1,128)S(1)}, f32[1,1,1024]{2,1,0:T(1,128)S(1)}, u32[]{:S(2)}, u32[]{:S(2)}) collective-permute-start(f32[1,1,1024]{2,1,0:T(1,128)S(1)} %shard_map.81.refs_0_), channel_id=1, source_target_pairs={{0,3},{1,0},{2,1},{3,2},{4,7},{5,4},{6,5},{7,6},{8,11},{9,8},{10,9... | collective-permute-start | bytes 12296 | tf_op jit(solution)/shard_map/ppermute | solution.py:360
  67.0 3.6 %collective-permute-start.14 = (f32[1,1,1024]{2,1,0:T(1,128)S(1)}, f32[1,1,1024]{2,1,0:T(1,128)S(1)}, u32[]{:S(2)}, u32[]{:S(2)}) collective-permute-start(f32[1,1,1024]{2,1,0:T(1,128)S(1)} %shard_map.81.refs_0_), channel_id=1, source_target_pairs={{0,2},{1,3},{2,0},{3,1},{4,6},{5,7},{6,4},{7,5},{8,10},{9,11},{10,... | collective-permute-start | bytes 12296 | tf_op jit(solution)/shard_map/ppermute | solution.py:360
  68.4 4.5 %collective-permute-start.13 = (f32[1,1,1024]{2,1,0:T(1,128)S(1)}, f32[1,1,1024]{2,1,0:T(1,128)S(1)}, u32[]{:S(2)}, u32[]{:S(2)}) collective-permute-start(f32[1,1,1024]{2,1,0:T(1,128)S(1)} %shard_map.81.refs_0_), channel_id=1, source_target_pairs={{0,1},{1,2},{2,3},{3,0},{4,5},{5,6},{6,7},{7,4},{8,9},{9,10},{10,1... | collective-permute-start | bytes 12296 | tf_op jit(solution)/shard_map/ppermute | solution.py:360
  91.3 6.4 %collective-permute-start.16 = (f32[17,1024]{1,0:T(8,128)S(1)}, f32[17,1024]{1,0:T(8,128)S(1)}, u32[]{:S(2)}, u32[]{:S(2)}) collective-permute-start(f32[17,1024]{1,0:T(8,128)S(1)} %get-tuple-element.62), channel_id=1, source_target_pairs={{0,1},{1,2},{2,3},{3,0},{4,5},{5,6},{6,7},{7,4},{8,9},{9,10},{10,1... | collective-permute-start | bytes 208904 | tf_op jit(solution)/shard_map/ppermute | solution.py:360
  91.3 6.5 %collective-permute-start.17 = (f32[17,1024]{1,0:T(8,128)S(1)}, f32[17,1024]{1,0:T(8,128)S(1)}, u32[]{:S(2)}, u32[]{:S(2)}) collective-permute-start(f32[17,1024]{1,0:T(8,128)S(1)} %get-tuple-element.63), channel_id=1, source_target_pairs={{0,2},{1,3},{2,0},{3,1},{4,6},{5,7},{6,4},{7,5},{8,10},{9,11},{10,... | collective-permute-start | bytes 208904 | tf_op jit(solution)/shard_map/ppermute | solution.py:360
  92.0 5.9 %collective-permute-start.18 = (f32[17,1024]{1,0:T(8,128)S(1)}, f32[17,1024]{1,0:T(8,128)S(1)}, u32[]{:S(2)}, u32[]{:S(2)}) collective-permute-start(f32[17,1024]{1,0:T(8,128)S(1)} %get-tuple-element.64), channel_id=1, source_target_pairs={{0,3},{1,0},{2,1},{3,2},{4,7},{5,4},{6,5},{7,6},{8,11},{9,8},{10,9... | collective-permute-start | bytes 208904 | tf_op jit(solution)/shard_map/ppermute | solution.py:360

commit v5 on v4

--- a/solution.py
+++ b/solution.py
@@ -135,49 +135,51 @@
         out_ref[t] = row
 
 
-def early_kernel(sm_ref, tm_ref, pot_ref, x_ref, ls_ref, lt_ref, to_ref, xo_ref):
-    ls_ref[...] = jnp.log2(sm_ref[...])
-    lt_ref[...] = jnp.log2(tm_ref[...])
+def early_kernel(peers, xplan, me_ref, mass_ref, pot_ref, *refs):
+    parts, (ls_ref, to_ref, xn_ref, xt_ref, xs, xw) = refs[: len(xplan)], refs[len(xplan) :]
+    k = xs.shape[0]
+    ls_ref[...] = jnp.log2(mass_ref[...])
     to_ref[...] = pot_ref[...]
-    xo_ref[...] = x_ref[...]
-
-
-def first_kernel(peers, xplan, yplan, me_ref, pot_ref, *refs):
-    xcount, ycount = len(xplan), len(yplan)
-    xparts, yparts, refs = refs[:xcount], refs[xcount : xcount + ycount], refs[xcount + ycount :]
-    s_ref, l_ref, xn_ref, yn_ref, yo_ref, xs, xw, yw, top_ref, sum_ref = refs
-    k = xs.shape[0]
-    me_src, me_tgt = me_ref[0] // peers, lax.rem(me_ref[0], peers)
+    me = lax.rem(me_ref[0], peers)
+    for part, d in zip(parts, xplan):
+        if d is None:
+            xs[...] = part[...]
+            continue
+        own = part.shape[0]
+        xs[pl.ds(pl.multiple_of(lax.rem(me - d + peers, peers) * own, 8), own), :] = part[...]
+    x = xs[...]
+    xn_ref[...] = jnp.sum(x * x, axis=0, keepdims=True) / k
+    x1, x2, x3 = pieces(x)
+    for p, piece in enumerate((x1, x1, x2, x2, x1, x3)):
+        xw[pl.ds(p * k, k), :] = piece
+    xt_ref[...] = xw[...].T
+
+
+def first_kernel(peers, yplan, me_ref, pot_ref, xt_ref, *refs):
+    ycount = len(yplan)
+    yparts, (s_ref, l_ref, yn_ref, yo_ref, yw, top_ref, sum_ref) = refs[:ycount], refs[ycount:]
+    me = me_ref[0] // peers
     for part, owners in zip(yparts, yplan):
         if owners is None:
             yo_ref[...] = part[...]
             continue
         own = part.shape[0] // len(owners)
         for b, d in enumerate(owners):
-            yo_ref[pl.ds(pl.multiple_of((me_src ^ d) * own, 8), own), :] = part[pl.ds(b * own, own), :]
-    for part, d in zip(xparts, xplan):
-        if d is None:
-            xs[...] = part[...]
-            continue
-        own = part.shape[0]
-        xs[pl.ds(pl.multiple_of(lax.rem(me_tgt - d + peers, peers) * own, 8), own), :] = part[...]
+            yo_ref[pl.ds(pl.multiple_of((me ^ d) * own, 8), own), :] = part[pl.ds(b * own, own), :]
     y = yo_ref[...]
-    yn = jnp.sum(y * y, axis=0, keepdims=True) / k
+    yn = jnp.sum(y * y, axis=0, keepdims=True) / y.shape[0]
     yn_ref[...] = yn
+    k = y.shape[0]
     y1, y2, y3 = pieces(y * (2.0 / (k * UNIT)))
-    x = xs[...]
-    xn_ref[...] = jnp.sum(x * x, axis=0, keepdims=True) / k
-    x1, x2, x3 = pieces(x)
-    for p, (xp, yp) in enumerate(((x1, y1), (x1, y2), (x2, y1), (x2, y2), (x1, y3), (x3, y1))):
-        xw[pl.ds(p * k, k), :] = xp
-        yw[pl.ds(p * k, k), :] = yp
+    for p, piece in enumerate((y1, y2, y1, y2, y3, y1)):
+        yw[pl.ds(p * k, k), :] = piece
     n, width = s_ref.shape
     pot8 = jnp.broadcast_to((pot_ref[...] - yn) * (1.0 / UNIT), (8, width))
     step = 256
     for b in range(n // step + 1):
         if b < n // step:
-            s_ref[pl.ds(b * step, step), :] = lax.dot_general(
-                xw[:, pl.ds(b * step, step)], yw[...], (((0,), (0,)), ((), ())), preferred_element_type=F32
+            s_ref[pl.ds(b * step, step), :] = jnp.dot(
+                xt_ref[pl.ds(b * step, step), :], yw[...], preferred_element_type=F32
             )
         if b > 0:
             for r in range((b - 1) * step, b * step, 8):
@@ -196,7 +198,7 @@
 def tgt_first_kernel(count, s_ref, mass_ref, f_ref, wide_ref, *refs):
     parts, (g_ref, p_ref, l_ref, top_ref, sum_ref) = refs[:count], refs[count:]
     n, width = s_ref.shape
-    g = mass_ref[...] - whole_log_sum(parts)
+    g = jnp.log2(mass_ref[...]) - whole_log_sum(parts)
     g_ref[...] = g
     g8 = jnp.broadcast_to(g, (8, width))
 
@@ -249,7 +251,7 @@
 def tgt_kernel(count, s_ref, p_ref, mass_ref, f_ref, g_ref, *refs):
     parts, (l_ref, top_ref, sum_ref) = refs[:count], refs[count:]
     n, width = p_ref.shape
-    change = mass_ref[...] - whole_log_sum(parts)
+    change = jnp.log2(mass_ref[...]) - whole_log_sum(parts)
     v = jnp.exp2(change)
     v8 = jnp.broadcast_to(v, (8, width))
 
@@ -278,7 +280,8 @@
     n, width = s_ref.shape
     peers = len(outs)
     own = k // peers
-    change = mass_ref[...] - whole_log_sum(parts)
+    block = own + 1
+    change = jnp.log2(mass_ref[...]) - whole_log_sum(parts)
     g = g_ref[...] + change
     f = f_ref[...] + u_ref[...]
     sp[...] = f * UNIT + xn_ref[...]
@@ -310,10 +313,12 @@
         total = acc[...].T * rescale
         den = total[k : k + 1, :] + total[k + 1 : k + 2, :]
         for t in range(peers):
-            flat[t] = total[t * own : (t + 1) * own, :]
+            for c in range(n // LANES):
+                at = slice(c * LANES, (c + 1) * LANES)
+                flat[t, pl.ds(c * block, own), :] = total[t * own : (t + 1) * own, at]
+                flat[t, pl.ds(c * block + own, 1), :] = den[:, at]
         for d, out in enumerate(outs):
-            out[pl.ds(0, own), :] = flat[lax.rem(me_ref[0] + d, peers)]
-            out[pl.ds(own, 1), :] = den
+            out[...] = flat[lax.rem(me_ref[0] + d, peers)]
         return den
 
     den = project(lambda rows: p_ref[rows, :], v, u)
@@ -335,16 +340,18 @@
 
 def join_kernel(*refs):
     parts, out_ref = refs[:-1], refs[-1]
-    own = out_ref.shape[0]
-    num = tree(jnp.add, [p[pl.ds(0, own), :] for p in parts])
-    den = tree(jnp.add, [p[pl.ds(own, 1), :] for p in parts])
-    out_ref[...] = num / den
+    own, n = out_ref.shape
+    for c in range(n // LANES):
+        at = c * (own + 1)
+        num = tree(jnp.add, [p[pl.ds(at, own), :] for p in parts])
+        den = tree(jnp.add, [p[pl.ds(at + own, 1), :] for p in parts])
+        out_ref[:, chunk(c)] = num / den
 
 
 def call(kernel, outs, scratch, ins, out_specs=None):
     return pl.pallas_call(
         kernel,
-        out_shape=[jax.ShapeDtypeStruct(o, F32) for o in outs],
+        out_shape=[o if isinstance(o, jax.ShapeDtypeStruct) else jax.ShapeDtypeStruct(o, F32) for o in outs],
         in_specs=[spec for spec, _ in ins],
         out_specs=out_specs or [VMEM] * len(outs),
         scratch_shapes=scratch,
@@ -389,8 +396,7 @@
         return [lax.all_gather(v, "src", axis=0, tiled=True)], [None], other
     order = list(range(0, size, 2))
     mine = jnp.concatenate([v] + [flip(v, "src", size, d) for d in order[1:]], axis=0)
-    mine, *early = lax.optimization_barrier([mine] + other[:-1])
-    other = early + other[-1:]
+    mine, *other = lax.optimization_barrier([mine] + other)
     return [mine, flip(mine, "src", size, 1)], [order, [d + 1 for d in order]], other
 
 
@@ -398,32 +404,25 @@
     own = src_pts.shape[0]
     n, width = src_pts.shape[1], tgt_pts.shape[1]
     k = own * peers_tgt
-    xs, xplan = gather_src(src_pts, peers_tgt)
+    pack = (own + 1) * (n // LANES)
     row, col = (1, n), (1, width)
-    early = call(
-        early_kernel,
-        [row, col, col, src_pts.shape],
-        [],
-        put(src_mass.reshape(row), tgt_mass.reshape(col), init_pot.reshape(col), src_pts),
-    )
-    sm, tm, pot, x = early
-    if xplan[0] is not None:
-        xs[0] = x
-    ys, yplan, (sm, tm, pot, *xs) = gather_tgt(tgt_pts, peers_src, [sm, tm, pot] + xs)
-    me = lax.axis_index(("src", "tgt")).astype(jnp.int32).reshape(1)
     rows, cols = (copies_of(peers_tgt), 1, n), (copies_of(peers_src), 1, width)
     lane = pltpu.VMEM((n, LANES), F32)
-    s, l, xn, yn, yo = call(
-        functools.partial(first_kernel, peers_tgt, xplan, yplan),
-        [(n, width), rows, row, col, (k, width)],
-        [
-            pltpu.VMEM((k, n), F32),
-            pltpu.VMEM((6 * k, n), BF16),
-            pltpu.VMEM((6 * k, width), BF16),
-            lane,
-            lane,
-        ],
-        [(SMEM, me)] + put(pot, *xs, *ys),
+    me = lax.axis_index(("src", "tgt")).astype(jnp.int32).reshape(1)
+    xs, xplan = gather_src(src_pts, peers_tgt)
+    ys, yplan, xs = gather_tgt(tgt_pts, peers_src, xs)
+    tm = tgt_mass.reshape(col)
+    sm, pot, xn, xt = call(
+        functools.partial(early_kernel, peers_tgt, xplan),
+        [row, col, row, jax.ShapeDtypeStruct((n, 6 * k), BF16)],
+        [pltpu.VMEM((k, n), F32), pltpu.VMEM((6 * k, n), BF16)],
+        [(SMEM, me)] + put(src_mass.reshape(row), init_pot.reshape(col), *xs),
+    )
+    s, l, yn, yo = call(
+        functools.partial(first_kernel, peers_tgt, yplan),
+        [(n, width), rows, col, (k, width)],
+        [pltpu.VMEM((6 * k, width), BF16), lane, lane],
+        [(SMEM, me)] + put(pot, xt, *ys),
     )
     parts = everyone(l, "tgt", peers_tgt)
     f, wide, l = call(
@@ -444,13 +443,13 @@
             (l,) = call(functools.partial(tgt_kernel, len(parts)), [rows], [lane, lane], put(s, p, tm, f, g, *parts))
     src_pot, tgt_pot, *blocks = call(
         functools.partial(last_kernel, len(parts)),
-        [row, col] + [(own + 1, n)] * peers_tgt,
+        [row, col] + [(pack, LANES)] * peers_tgt,
         [
             pltpu.VMEM(row, F32),
             pltpu.VMEM(col, F32),
             pltpu.VMEM((2 * LANES, width), BF16),
             lane,
-            pltpu.VMEM((peers_tgt, own, n), F32),
+            pltpu.VMEM((peers_tgt, pack, LANES), F32),
             lane,
             pltpu.SemaphoreType.DMA((2,)),
         ],

time: 97.6 us -> 98.9 us (1.013); the launches traced: 98.6 us -> 97.8 us
  blocking collectives: 26.1 us -> 29 us
  starting transfers between devices: 25.1 us -> 23.2 us
  waiting for transfers between devices: 16.8 us -> 15.6 us
    all_to_all x3, blocking collectives: 26.1 us -> 29 us  [everyone(): return [lax.all_to_all(v, axis, 0, 0, tiled=True)]]
    ppermute x15, waiting for transfers between devices: 16.7 us -> 14 us  [turn(): return lax.ppermute(v, axis, [(i, (i + d) % size) for i in range(size)])]
    ppermute x15, starting transfers between devices: 19.4 us -> 17.5 us  [turn(): return lax.ppermute(v, axis, [(i, (i + d) % size) for i in range(size)])]
    ppermute x4, waiting for transfers between devices: 0.1 us -> 1.61 us  [flip(): return lax.ppermute(v, axis, [(i, i ^ bit) for i in range(size)])]
    unnamed x6 -> x8, local copies, waits for them, and re-layouts: 2.08 us -> 2.23 us
  transfers between devices with their start and end apart: 19 -> 19, of which waited for: 14 -> 13; matrix products, arithmetic and copies ran while one was open for 1% -> 1% of each run, Pallas kernels for 1% -> 0%
where the time goes in v5:
time: 98.9 us; the launch traced here: 97.8 us
  blocking collectives  29 us (29%)
  Pallas kernels  26.2 us (26%)
  starting transfers between devices  23.2 us (23%)
  waiting for transfers between devices  15.6 us (16%)
  local copies, waits for them, and re-layouts  2.23 us (2%)
    all_to_all x3, blocking collectives, everyone(): return [lax.all_to_all(v, axis, 0, 0, tiled=True)]  29 us
    pallas_call x9, Pallas kernels, call(): pl.pallas_call(kernel, out_shape=[o if isinstance(o, jax.ShapeDtypeStruct...  26.2 us
    ppermute x15, starting transfers between devices, turn(): return lax.ppermute(v, axis, [(i, (i + d) % size) for i in range(size)])  17.5 us
    ppermute x15, waiting for transfers between devices, turn(): return lax.ppermute(v, axis, [(i, (i + d) % size) for i in range(size)])  14 us
    ppermute x4, starting transfers between devices, flip(): return lax.ppermute(v, axis, [(i, i ^ bit) for i in range(size)])  5.68 us
    unnamed x8, local copies, waits for them, and re-layouts  2.23 us
  transfers between devices with their start and end apart: 19, of which 13 were waited for; matrix products, arithmetic and copies ran while one was open for 1% of the time, Pallas kernels for 0%

profile of v5, /device:TPU:0, one launch (start us, length us, event | category | flops | bytes accessed | tf_op | source)
XLA Modules:
  0.0 97.8 jit_solution(771698118485224725)
XLA Ops:
  0.6 4.1 %collective-permute-start.1 = (f32[8,2048]{1,0:T(8,128)}, f32[8,2048]{1,0:T(8,128)S(1)}, u32[]{:S(2)}, u32[]{:S(2)}) collective-permute-start(f32[8,2048]{1,0:T(8,128)} %param.6), channel_id=1, source_target_pairs={{0,16},{4,20},{8,24},{12,28},{16,0},{20,4},{24,8},{28,12},{1,17},{... | collective-permute-start | bytes 196616 | tf_op jit(solution)/shard_map/ppermute | solution.py:371
  4.7 1.6 %collective-permute-start = (f32[8,2048]{1,0:T(8,128)}, f32[8,2048]{1,0:T(8,128)S(1)}, u32[]{:S(2)}, u32[]{:S(2)}) collective-permute-start(f32[8,2048]{1,0:T(8,128)} %param.6), channel_id=1, source_target_pairs={{0,8},{4,12},{8,0},{12,4},{16,24},{20,28},{24,16},{28,20},{1,9},{5... | collective-permute-start | bytes 196616 | tf_op jit(solution)/shard_map/ppermute | solution.py:371
  6.3 1.7 %collective-permute-start.4 = (f32[16,1024]{1,0:T(8,128)}, f32[16,1024]{1,0:T(8,128)S(1)}, u32[]{:S(2)}, u32[]{:S(2)}) collective-permute-start(f32[16,1024]{1,0:T(8,128)} %refs_0_), channel_id=1, source_target_pairs={{0,2},{1,3},{2,0},{3,1},{4,6},{5,7},{6,4},{7,5},{8,10},{9,11},{10,... | collective-permute-start | bytes 196616 | tf_op jit(solution)/shard_map/ppermute | solution.py:367
  8.1 1.5 %collective-permute-start.3 = (f32[16,1024]{1,0:T(8,128)}, f32[16,1024]{1,0:T(8,128)S(1)}, u32[]{:S(2)}, u32[]{:S(2)}) collective-permute-start(f32[16,1024]{1,0:T(8,128)} %refs_0_), channel_id=1, source_target_pairs={{0,1},{1,2},{2,3},{3,0},{4,5},{5,6},{6,7},{7,4},{8,9},{9,10},{10,1... | collective-permute-start | bytes 196616 | tf_op jit(solution)/shard_map/ppermute | solution.py:367
  9.6 1.4 %collective-permute-start.5 = (f32[16,1024]{1,0:T(8,128)}, f32[16,1024]{1,0:T(8,128)S(1)}, u32[]{:S(2)}, u32[]{:S(2)}) collective-permute-start(f32[16,1024]{1,0:T(8,128)} %refs_0_), channel_id=1, source_target_pairs={{0,3},{1,0},{2,1},{3,2},{4,7},{5,4},{6,5},{7,6},{8,11},{9,8},{10,9... | collective-permute-start | bytes 196616 | tf_op jit(solution)/shard_map/ppermute | solution.py:367
  11.0 1.6 %collective-permute-done.2 = f32[8,2048]{1,0:T(8,128)S(1)} collective-permute-done((f32[8,2048]{1,0:T(8,128)}, f32[8,2048]{1,0:T(8,128)S(1)}, u32[]{:S(2)}, u32[]{:S(2)}) %collective-permute-start.2) | collective-permute-done | bytes 65568 | tf_op jit(solution)/shard_map/ppermute | solution.py:371
  16.6 4.4 %shard_map.77 = (f32[1024,2048]{1,0:T(8,128)S(1)}, f32[1,1,1024]{2,1,0:T(1,128)S(1)}, f32[1,2048]{1,0:T(1,128)S(1)}, f32[64,2048]{1,0:T(8,128)S(1)}) custom-call(s32[1]{0:T(128)} %bitcast.me_ref, f32[1,2048]{1,0:T(1,128)S(1)} %get-tuple-element.35.pot_ref, bf16[1024,384]{1,0:T(8,128)(2,1)S(1)} %get-tuple-element.36.xt_ref, ...), custom_call_target="tpu_custom_call" | custom-call | tf_op jit(solution)/shard_map/pallas_call | solution.py:352
  21.0 2.4 %collective-permute-start.9 = (f32[1,1,1024]{2,1,0:T(1,128)S(1)}, f32[1,1,1024]{2,1,0:T(1,128)S(1)}, u32[]{:S(2)}, u32[]{:S(2)}) collective-permute-start(f32[1,1,1024]{2,1,0:T(1,128)S(1)} %get-tuple-element.40.refs_0_), channel_id=1, source_target_pairs={{0,3},{1,0},{2,1},{3,2},{4,7},{5,4},{6,5},{7,6},{8,11},{9,8},{10,9... | collective-permute-start | bytes 12296 | tf_op jit(solution)/shard_map/ppermute | solution.py:367
  24.7 2.3 %collective-permute-done.8.refs_2_ = f32[1,1,1024]{2,1,0:T(1,128)S(1)} collective-permute-done((f32[1,1,1024]{2,1,0:T(1,128)S(1)}, f32[1,1,1024]{2,1,0:T(1,128)S(1)}, u32[]{:S(2)}, u32[]{:S(2)}) %collective-permute-start.8) | collective-permute-done | bytes 4128 | tf_op jit(solution)/shard_map/ppermute | solution.py:367
  28.2 2.7 %shard_map.78 = (f32[1,1024]{1,0:T(1,128)S(1)}, f32[1024,128]{1,0:T(8,128)S(1)}, f32[8,1,2048]{2,1,0:T(1,128)S(1)}) custom-call(f32[1024,2048]{1,0:T(8,128)S(1)} %get-tuple-element.38.s_ref, f32[1,1024]{1,0:T(1,128)S(1)} %get-tuple-element.39.mass_ref, f32[1,1,1024]{2,1,0:T(1,128)S(1)} %get-tuple-element.40.refs_0_, ...), custom_call_target="tpu_custom_call" | custom-call | tf_op jit(solution)/shard_map/pallas_call | solution.py:352
  30.9 12.5 %all_to_all.15.refs_0_ = f32[8,1,2048]{2,1,0:T(1,128)S(1)} all-to-all(f32[8,1,2048]{2,1,0:T(1,128)S(1)} %get-tuple-element.43), channel_id=1, replica_groups=mesh['src'=8,'tgt'=4] {'src'}, dimensions={0} | all-to-all | bytes 131072 | tf_op jit(solution)/shard_map/all_to_all | solution.py:381
  43.3 2.3 %shard_map.79 = (f32[1,2048]{1,0:T(1,128)S(1)}, f32[1024,2048]{1,0:T(8,128)S(1)}, f32[1,1,1024]{2,1,0:T(1,128)S(1)}) custom-call(f32[1024,2048]{1,0:T(8,128)S(1)} %get-tuple-element.38.s_ref, f32[1,2048]{1,0:T(1,128)S(1)} %bitcast.6, f32[1,1024]{1,0:T(1,128)S(1)} %get-tuple-element.41.f_ref, f32[1024,128]{1,0:T(8,128)S(1)} %get-tuple-element.42.wide_ref, ...), custom_call_target="tpu_custom_call" | custom-call | tf_op jit(solution)/shard_map/pallas_call | solution.py:352
  45.8 1.5 %collective-permute-start.11 = (f32[1,1,1024]{2,1,0:T(1,128)S(1)}, f32[1,1,1024]{2,1,0:T(1,128)S(1)}, u32[]{:S(2)}, u32[]{:S(2)}) collective-permute-start(f32[1,1,1024]{2,1,0:T(1,128)S(1)} %get-tuple-element.46.refs_0_), channel_id=1, source_target_pairs={{0,2},{1,3},{2,0},{3,1},{4,6},{5,7},{6,4},{7,5},{8,10},{9,11},{10,... | collective-permute-start | bytes 12296 | tf_op jit(solution)/shard_map/ppermute | solution.py:367
  47.4 1.9 %collective-permute-start.10 = (f32[1,1,1024]{2,1,0:T(1,128)S(1)}, f32[1,1,1024]{2,1,0:T(1,128)S(1)}, u32[]{:S(2)}, u32[]{:S(2)}) collective-permute-start(f32[1,1,1024]{2,1,0:T(1,128)S(1)} %get-tuple-element.46.refs_0_), channel_id=1, source_target_pairs={{0,1},{1,2},{2,3},{3,0},{4,5},{5,6},{6,7},{7,4},{8,9},{9,10},{10,1... | collective-permute-start | bytes 12296 | tf_op jit(solution)/shard_map/ppermute | solution.py:367
  49.4 2.4 %collective-permute-done.10.refs_1_ = f32[1,1,1024]{2,1,0:T(1,128)S(1)} collective-permute-done((f32[1,1,1024]{2,1,0:T(1,128)S(1)}, f32[1,1,1024]{2,1,0:T(1,128)S(1)}, u32[]{:S(2)}, u32[]{:S(2)}) %collective-permute-start.10) | collective-permute-done | bytes 4128 | tf_op jit(solution)/shard_map/ppermute | solution.py:367
  51.9 4.5 %shard_map.80 = (f32[1,1024]{1,0:T(1,128)}, f32[8,1,2048]{2,1,0:T(1,128)S(1)}) custom-call(f32[1024,2048]{1,0:T(8,128)S(1)} %get-tuple-element.38.s_ref, f32[1024,2048]{1,0:T(8,128)S(1)} %get-tuple-element.44.p_ref, f32[1,1024]{1,0:T(1,128)S(1)} %get-tuple-element.39.mass_ref, f32[1,1024]{1,0:T(1,128)S(1)} %get-tuple-element.41.f_ref, ...), custom_call_target="tpu_custom_call" | custom-call | tf_op jit(solution)/shard_map/pallas_call | solution.py:352
  56.3 8.3 %all_to_all.16.refs_0_ = f32[8,1,2048]{2,1,0:T(1,128)S(1)} all-to-all(f32[8,1,2048]{2,1,0:T(1,128)S(1)} %get-tuple-element.47), channel_id=1, replica_groups=mesh['src'=8,'tgt'=4] {'src'}, dimensions={0} | all-to-all | bytes 131072 | tf_op jit(solution)/shard_map/all_to_all | solution.py:381
  67.0 1.5 %collective-permute-start.14 = (f32[1,1,1024]{2,1,0:T(1,128)S(1)}, f32[1,1,1024]{2,1,0:T(1,128)S(1)}, u32[]{:S(2)}, u32[]{:S(2)}) collective-permute-start(f32[1,1,1024]{2,1,0:T(1,128)S(1)} %shard_map.81.refs_0_), channel_id=1, source_target_pairs={{0,2},{1,3},{2,0},{3,1},{4,6},{5,7},{6,4},{7,5},{8,10},{9,11},{10,... | collective-permute-start | bytes 12296 | tf_op jit(solution)/shard_map/ppermute | solution.py:367
  70.6 2.4 %collective-permute-done.13.refs_1_ = f32[1,1,1024]{2,1,0:T(1,128)S(1)} collective-permute-done((f32[1,1,1024]{2,1,0:T(1,128)S(1)}, f32[1,1,1024]{2,1,0:T(1,128)S(1)}, u32[]{:S(2)}, u32[]{:S(2)}) %collective-permute-start.13) | collective-permute-done | bytes 4128 | tf_op jit(solution)/shard_map/ppermute | solution.py:367
  73.0 3.9 %shard_map.82 = (f32[1,1024]{1,0:T(1,128)S(1)}, f32[8,1,2048]{2,1,0:T(1,128)S(1)}) custom-call(f32[1024,2048]{1,0:T(8,128)S(1)} %get-tuple-element.38.s_ref, f32[1024,2048]{1,0:T(8,128)S(1)} %get-tuple-element.44.p_ref, f32[1,1024]{1,0:T(1,128)S(1)} %get-tuple-element.39.mass_ref, f32[1,1024]{1,0:T(1,128)S(1)} %get-tuple-element.41.f_ref, ...), custom_call_target="tpu_custom_call" | custom-call | tf_op jit(solution)/shard_map/pallas_call | solution.py:352
  76.9 8.3 %all_to_all.17.refs_0_ = f32[8,1,2048]{2,1,0:T(1,128)S(1)} all-to-all(f32[8,1,2048]{2,1,0:T(1,128)S(1)} %get-tuple-element.52), channel_id=1, replica_groups=mesh['src'=8,'tgt'=4] {'src'}, dimensions={0} | all-to-all | bytes 131072 | tf_op jit(solution)/shard_map/all_to_all | solution.py:381
  85.2 6.1 %shard_map.83 = (f32[1,1024]{1,0:T(1,128)}, f32[1,2048]{1,0:T(1,128)}, f32[136,128]{1,0:T(8,128)S(1)}, f32[136,128]{1,0:T(8,128)S(1)}, f32[136,128]{1,0:T(8,128)S(1)}, /*index=5*/f32[136,128]{1,0:T(8,128)S(1)}) custom-call(s32[1]{0:T(128)} %bitcast.me_ref, f32[1024,2048]{1,0:T(8,128)S(1)} %get-tuple-element.38.s_ref, ...), custom_call_target="tpu_custom_call" | custom-call | tf_op jit(solution)/shard_map/pallas_call | solution.py:352
  92.0 2.8 %collective-permute-start.18 = (f32[136,128]{1,0:T(8,128)S(1)}, f32[136,128]{1,0:T(8,128)S(1)}, u32[]{:S(2)}, u32[]{:S(2)}) collective-permute-start(f32[136,128]{1,0:T(8,128)S(1)} %get-tuple-element.58), channel_id=1, source_target_pairs={{0,3},{1,0},{2,1},{3,2},{4,7},{5,4},{6,5},{7,6},{8,11},{9,8},{10,9... | collective-permute-start | bytes 208904 | tf_op jit(solution)/shard_map/ppermute | solution.py:367
  94.8 1.9 %collective-permute-done.16.refs_1_ = f32[136,128]{1,0:T(8,128)S(1)} collective-permute-done((f32[136,128]{1,0:T(8,128)S(1)}, f32[136,128]{1,0:T(8,128)S(1)}, u32[]{:S(2)}, u32[]{:S(2)}) %collective-permute-start.16) | collective-permute-done | bytes 69664 | tf_op jit(solution)/shard_map/ppermute | solution.py:367
  (35 shorter events, 12.9 us)
Async XLA Ops:
  0.6 42.7 %copy-start = (f32[2048]{0:T(1024)S(1)}, f32[2048]{0:T(1024)}, u32[]{:S(2)}) copy-start(f32[2048]{0:T(1024)} %param.8) | copy-start | bytes 24580
  0.6 8.9 %collective-permute-start.1 = (f32[8,2048]{1,0:T(8,128)}, f32[8,2048]{1,0:T(8,128)S(1)}, u32[]{:S(2)}, u32[]{:S(2)}) collective-permute-start(f32[8,2048]{1,0:T(8,128)} %param.6), channel_id=1, source_target_pairs={{0,16},{4,20},{8,24},{12,28},{16,0},{20,4},{24,8},{28,12},{1,17},{... | collective-permute-start | bytes 196616 | tf_op jit(solution)/shard_map/ppermute | solution.py:371
  4.7 6.3 %collective-permute-start = (f32[8,2048]{1,0:T(8,128)}, f32[8,2048]{1,0:T(8,128)S(1)}, u32[]{:S(2)}, u32[]{:S(2)}) collective-permute-start(f32[8,2048]{1,0:T(8,128)} %param.6), channel_id=1, source_target_pairs={{0,8},{4,12},{8,0},{12,4},{16,24},{20,28},{24,16},{28,20},{1,9},{5... | collective-permute-start | bytes 196616 | tf_op jit(solution)/shard_map/ppermute | solution.py:371
  6.3 6.3 %collective-permute-start.2 = (f32[8,2048]{1,0:T(8,128)}, f32[8,2048]{1,0:T(8,128)S(1)}, u32[]{:S(2)}, u32[]{:S(2)}) collective-permute-start(f32[8,2048]{1,0:T(8,128)} %param.6), channel_id=1, source_target_pairs={{0,24},{4,28},{8,16},{12,20},{16,8},{20,12},{24,0},{28,4},{1,25},{... | collective-permute-start | bytes 196616 | tf_op jit(solution)/shard_map/ppermute | solution.py:371
  6.3 7.1 %collective-permute-start.4 = (f32[16,1024]{1,0:T(8,128)}, f32[16,1024]{1,0:T(8,128)S(1)}, u32[]{:S(2)}, u32[]{:S(2)}) collective-permute-start(f32[16,1024]{1,0:T(8,128)} %refs_0_), channel_id=1, source_target_pairs={{0,2},{1,3},{2,0},{3,1},{4,6},{5,7},{6,4},{7,5},{8,10},{9,11},{10,... | collective-permute-start | bytes 196616 | tf_op jit(solution)/shard_map/ppermute | solution.py:367
  8.1 5.4 %collective-permute-start.3 = (f32[16,1024]{1,0:T(8,128)}, f32[16,1024]{1,0:T(8,128)S(1)}, u32[]{:S(2)}, u32[]{:S(2)}) collective-permute-start(f32[16,1024]{1,0:T(8,128)} %refs_0_), channel_id=1, source_target_pairs={{0,1},{1,2},{2,3},{3,0},{4,5},{5,6},{6,7},{7,4},{8,9},{9,10},{10,1... | collective-permute-start | bytes 196616 | tf_op jit(solution)/shard_map/ppermute | solution.py:367
  9.6 4.5 %collective-permute-start.5 = (f32[16,1024]{1,0:T(8,128)}, f32[16,1024]{1,0:T(8,128)S(1)}, u32[]{:S(2)}, u32[]{:S(2)}) collective-permute-start(f32[16,1024]{1,0:T(8,128)} %refs_0_), channel_id=1, source_target_pairs={{0,3},{1,0},{2,1},{3,2},{4,7},{5,4},{6,5},{7,6},{8,11},{9,8},{10,9... | collective-permute-start | bytes 196616 | tf_op jit(solution)/shard_map/ppermute | solution.py:367
  14.0 2.5 %collective-permute-start.6 = (f32[32,2048]{1,0:T(8,128)S(1)}, f32[32,2048]{1,0:T(8,128)S(1)}, u32[]{:S(2)}, u32[]{:S(2)}) collective-permute-start(f32[32,2048]{1,0:T(8,128)S(1)} %pad_maximum_fusion.refs_0_), channel_id=1, source_target_pairs={{0,4},{4,0},{8,12},{12,8},{16,20},{20,16},{24,28},{28,24},{1,5},{5... | collective-permute-start | bytes 786440 | tf_op jit(solution)/shard_map/ppermute | solution.py:371
  14.0 0.8 copy-start.1
  14.9 0.7 copy-start.2
  15.6 0.7 copy-start.3
  21.0 3.7 %collective-permute-start.9 = (f32[1,1,1024]{2,1,0:T(1,128)S(1)}, f32[1,1,1024]{2,1,0:T(1,128)S(1)}, u32[]{:S(2)}, u32[]{:S(2)}) collective-permute-start(f32[1,1,1024]{2,1,0:T(1,128)S(1)} %get-tuple-element.40.refs_0_), channel_id=1, source_target_pairs={{0,3},{1,0},{2,1},{3,2},{4,7},{5,4},{6,5},{7,6},{8,11},{9,8},{10,9... | collective-permute-start | bytes 12296 | tf_op jit(solution)/shard_map/ppermute | solution.py:367
  23.4 3.6 %collective-permute-start.8 = (f32[1,1,1024]{2,1,0:T(1,128)S(1)}, f32[1,1,1024]{2,1,0:T(1,128)S(1)}, u32[]{:S(2)}, u32[]{:S(2)}) collective-permute-start(f32[1,1,1024]{2,1,0:T(1,128)S(1)} %get-tuple-element.40.refs_0_), channel_id=1, source_target_pairs={{0,2},{1,3},{2,0},{3,1},{4,6},{5,7},{6,4},{7,5},{8,10},{9,11},{10,... | collective-permute-start | bytes 12296 | tf_op jit(solution)/shard_map/ppermute | solution.py:367
  23.7 4.5 %collective-permute-start.7 = (f32[1,1,1024]{2,1,0:T(1,128)S(1)}, f32[1,1,1024]{2,1,0:T(1,128)S(1)}, u32[]{:S(2)}, u32[]{:S(2)}) collective-permute-start(f32[1,1,1024]{2,1,0:T(1,128)S(1)} %get-tuple-element.40.refs_0_), channel_id=1, source_target_pairs={{0,1},{1,2},{2,3},{3,0},{4,5},{5,6},{6,7},{7,4},{8,9},{9,10},{10,1... | collective-permute-start | bytes 12296 | tf_op jit(solution)/shard_map/ppermute | solution.py:367
  45.7 3.7 %collective-permute-start.12 = (f32[1,1,1024]{2,1,0:T(1,128)S(1)}, f32[1,1,1024]{2,1,0:T(1,128)S(1)}, u32[]{:S(2)}, u32[]{:S(2)}) collective-permute-start(f32[1,1,1024]{2,1,0:T(1,128)S(1)} %get-tuple-element.46.refs_0_), channel_id=1, source_target_pairs={{0,3},{1,0},{2,1},{3,2},{4,7},{5,4},{6,5},{7,6},{8,11},{9,8},{10,9... | collective-permute-start | bytes 12296 | tf_op jit(solution)/shard_map/ppermute | solution.py:367
  45.8 3.6 %collective-permute-start.11 = (f32[1,1,1024]{2,1,0:T(1,128)S(1)}, f32[1,1,1024]{2,1,0:T(1,128)S(1)}, u32[]{:S(2)}, u32[]{:S(2)}) collective-permute-start(f32[1,1,1024]{2,1,0:T(1,128)S(1)} %get-tuple-element.46.refs_0_), channel_id=1, source_target_pairs={{0,2},{1,3},{2,0},{3,1},{4,6},{5,7},{6,4},{7,5},{8,10},{9,11},{10,... | collective-permute-start | bytes 12296 | tf_op jit(solution)/shard_map/ppermute | solution.py:367
  47.4 4.5 %collective-permute-start.10 = (f32[1,1,1024]{2,1,0:T(1,128)S(1)}, f32[1,1,1024]{2,1,0:T(1,128)S(1)}, u32[]{:S(2)}, u32[]{:S(2)}) collective-permute-start(f32[1,1,1024]{2,1,0:T(1,128)S(1)} %get-tuple-element.46.refs_0_), channel_id=1, source_target_pairs={{0,1},{1,2},{2,3},{3,0},{4,5},{5,6},{6,7},{7,4},{8,9},{9,10},{10,1... | collective-permute-start | bytes 12296 | tf_op jit(solution)/shard_map/ppermute | solution.py:367
  65.9 3.7 %collective-permute-start.15 = (f32[1,1,1024]{2,1,0:T(1,128)S(1)}, f32[1,1,1024]{2,1,0:T(1,128)S(1)}, u32[]{:S(2)}, u32[]{:S(2)}) collective-permute-start(f32[1,1,1024]{2,1,0:T(1,128)S(1)} %shard_map.81.refs_0_), channel_id=1, source_target_pairs={{0,3},{1,0},{2,1},{3,2},{4,7},{5,4},{6,5},{7,6},{8,11},{9,8},{10,9... | collective-permute-start | bytes 12296 | tf_op jit(solution)/shard_map/ppermute | solution.py:367
  67.0 3.6 %collective-permute-start.14 = (f32[1,1,1024]{2,1,0:T(1,128)S(1)}, f32[1,1,1024]{2,1,0:T(1,128)S(1)}, u32[]{:S(2)}, u32[]{:S(2)}) collective-permute-start(f32[1,1,1024]{2,1,0:T(1,128)S(1)} %shard_map.81.refs_0_), channel_id=1, source_target_pairs={{0,2},{1,3},{2,0},{3,1},{4,6},{5,7},{6,4},{7,5},{8,10},{9,11},{10,... | collective-permute-start | bytes 12296 | tf_op jit(solution)/shard_map/ppermute | solution.py:367
  68.5 4.5 %collective-permute-start.13 = (f32[1,1,1024]{2,1,0:T(1,128)S(1)}, f32[1,1,1024]{2,1,0:T(1,128)S(1)}, u32[]{:S(2)}, u32[]{:S(2)}) collective-permute-start(f32[1,1,1024]{2,1,0:T(1,128)S(1)} %shard_map.81.refs_0_), channel_id=1, source_target_pairs={{0,1},{1,2},{2,3},{3,0},{4,5},{5,6},{6,7},{7,4},{8,9},{9,10},{10,1... | collective-permute-start | bytes 12296 | tf_op jit(solution)/shard_map/ppermute | solution.py:367
  91.3 5.4 %collective-permute-start.16 = (f32[136,128]{1,0:T(8,128)S(1)}, f32[136,128]{1,0:T(8,128)S(1)}, u32[]{:S(2)}, u32[]{:S(2)}) collective-permute-start(f32[136,128]{1,0:T(8,128)S(1)} %get-tuple-element.56), channel_id=1, source_target_pairs={{0,1},{1,2},{2,3},{3,0},{4,5},{5,6},{6,7},{7,4},{8,9},{9,10},{10,1... | collective-permute-start | bytes 208904 | tf_op jit(solution)/shard_map/ppermute | solution.py:367
  91.3 5.4 %collective-permute-start.17 = (f32[136,128]{1,0:T(8,128)S(1)}, f32[136,128]{1,0:T(8,128)S(1)}, u32[]{:S(2)}, u32[]{:S(2)}) collective-permute-start(f32[136,128]{1,0:T(8,128)S(1)} %get-tuple-element.57), channel_id=1, source_target_pairs={{0,2},{1,3},{2,0},{3,1},{4,6},{5,7},{6,4},{7,5},{8,10},{9,11},{10,... | collective-permute-start | bytes 208904 | tf_op jit(solution)/shard_map/ppermute | solution.py:367
  92.0 5.1 %collective-permute-start.18 = (f32[136,128]{1,0:T(8,128)S(1)}, f32[136,128]{1,0:T(8,128)S(1)}, u32[]{:S(2)}, u32[]{:S(2)}) collective-permute-start(f32[136,128]{1,0:T(8,128)S(1)} %get-tuple-element.58), channel_id=1, source_target_pairs={{0,3},{1,0},{2,1},{3,2},{4,7},{5,4},{6,5},{7,6},{8,11},{9,8},{10,9... | collective-permute-start | bytes 208904 | tf_op jit(solution)/shard_map/ppermute | solution.py:367
